TPU v7x, 256 devices: a whole 4x4x8 slice. The times are simulated.
256 devices in a mesh: pool: 2 (over y_lo), inst: 4 (over x), tp: 32 (over z, y_hi, core).
Axes of the slice: x: 4, y: 4 (y_hi: 2, y_lo: 2; y = y_hi * 2 + y_lo), z: 8, core: 2. Of those that a mesh axis runs over, the one named last changes fastest.
Arguments:
- hidden_states: bfloat16 [4, 32, 8192], P('inst', None, ('pool', 'tp')), may hold values from -6 to 6
- norm_gain: bfloat16 [8192], P(('pool', 'tp')), may hold values from 0.25 to 1.75
- query_weight: bfloat16 [8192, 4096], P(None, 'tp'), may hold values from -0.0625 to 0.0625
- key_weight: bfloat16 [8192, 512], P(('pool', 'tp')), may hold values from -0.0625 to 0.0625
- value_weight: bfloat16 [8192, 512], P(('pool', 'tp')), may hold values from -0.0625 to 0.0625
- output_weight: bfloat16 [4096, 8192], P('tp'), may hold values from -0.09375 to 0.09375
- key_cache: bfloat16 [2, 4, 32, 128, 512], P('pool', 'inst')
- value_cache: bfloat16 [2, 4, 32, 128, 512], P('pool', 'inst'), may hold values from -24 to 24
- lengths: int32 [4, 32], replicated, may hold values from 1 to 128, as said below
- offload: int32 [4, 32], replicated, may hold values 0 or 1
- host_instance: int32 [4, 32], replicated, may hold values from 0 to 3, as said below
- cache_slot: int32 [4, 32], replicated, may hold values from 0 to 31, as said below
Outputs:
- attention_out: bfloat16 [4, 32, 8192], P('inst', None, ('pool', 'tp'))
Inputs may be any that keep to these rules, and one draw needn't show every extreme that they name: `lengths`: each request's context; in every draw some request has exactly 128. `host_instance`: together with cache_slot, no two requests name the same pair. `cache_slot`: together with host_instance, no two requests name the same pair.
All inputs are finite; a program needn't handle non-finite values.
Results may differ from a plain program's by a relative error of at most 0.012.
The roundings to bfloat16 on the way count: a program that leaves them out, or rounds other values in their place, can miss the bound.
Values may be sent and summed in bfloat16 or wider, within the bound.
No kernel may reach another device: no remote copies, remote signals or barrier semaphores. Data moves between devices by JAX's collectives and lax.ppermute only.
A program may use at most 64 MiB of HBM per device.

v0:
```python
import jax
import jax.numpy as jnp
from jax import lax
from jax.sharding import PartitionSpec as P

HD = 128
HQ = 32
CH = 4


epsilon = 1e-05
rope_base = 500000.0


def rotate(values, positions):
    half_width = values.shape[-1] // 2
    frequency = jnp.power(
        rope_base, -jnp.arange(half_width, dtype=jnp.float32) * 2.0 / values.shape[-1]
    )
    angles = positions.astype(jnp.float32)[:, None] * frequency[None, :]
    cosine_part = jnp.cos(angles)[:, None, :]
    sine_part = jnp.sin(angles)[:, None, :]
    first_half = values[..., :half_width]
    second_half = values[..., half_width:]
    return jnp.concatenate(
        [
            first_half * cosine_part - second_half * sine_part,
            first_half * sine_part + second_half * cosine_part,
        ],
        axis=-1,
    )


def attend(queries, cached_keys, cached_values, visible_count, own_keys, own_values):
    row_count, group_count, share_count, head_dim = queries.shape
    factor = head_dim ** (-0.5)
    key_blocks = cached_keys.reshape(row_count, cached_keys.shape[1], group_count, head_dim)
    value_blocks = cached_values.reshape(row_count, cached_values.shape[1], group_count, head_dim)
    own_key_rows = own_keys.reshape(row_count, group_count, head_dim)
    own_value_rows = own_values.reshape(row_count, group_count, head_dim)
    scores = (
        jnp.einsum("rcgd,rpcd->rcgp", queries, key_blocks, preferred_element_type=jnp.float32)
        * factor
    )
    own_score = (
        jnp.einsum("rcgd,rcd->rcg", queries, own_key_rows, preferred_element_type=jnp.float32)
        * factor
    )
    visible = (
        jnp.arange(cached_keys.shape[1], dtype=jnp.int32)[None, None, None, :]
        < visible_count[:, None, None, None]
    )
    peak = jnp.maximum(jnp.max(jnp.where(visible, scores, -jnp.inf), axis=-1), own_score)
    exps = jnp.where(visible, jnp.exp(scores - peak[..., None]), 0.0)
    own_exp = jnp.exp(own_score - peak)
    denominator = jnp.sum(exps, axis=-1) + own_exp
    weights_soft = (exps / denominator[..., None]).astype(jnp.bfloat16)
    own_weight = (own_exp / denominator).astype(jnp.bfloat16)
    mixed = jnp.einsum(
        "rcgp,rpcd->rcgd", weights_soft, value_blocks, preferred_element_type=jnp.float32
    )
    mixed = (
        mixed
        + own_weight.astype(jnp.float32)[..., None]
        * own_value_rows.astype(jnp.float32)[:, :, None, :]
    )
    return mixed.astype(jnp.bfloat16).reshape(row_count, -1)


def shards(
    hidden_states,
    norm_gain,
    query_weight,
    key_weight,
    value_weight,
    output_weight,
    key_cache,
    value_cache,
    lengths,
    offload,
    host_instance,
    cache_slot,
):
    pool_id = lax.axis_index("pool")
    inst_id = lax.axis_index("inst")
    tp_id = lax.axis_index("tp")
    instance_count = lax.axis_size("inst")
    batch_rows = hidden_states.shape[1]
    head_dim = HD
    head_count = query_weight.shape[1] // head_dim
    group_size = HQ // CH
    kv_count = max(1, head_count // group_size)
    kv_width = kv_count * head_dim
    kv_start = tp_id * head_count // group_size
    model_width = query_weight.shape[0]
    tokens = hidden_states[0]
    gains = norm_gain.reshape(1, -1)
    local_scaled = (tokens.astype(jnp.float32) * gains.astype(jnp.float32)).astype(jnp.bfloat16)
    key_terms = jnp.dot(local_scaled, key_weight, preferred_element_type=jnp.float32)
    value_terms = jnp.dot(local_scaled, value_weight, preferred_element_type=jnp.float32)
    piece_tokens = lax.all_gather(tokens, ("pool", "tp"), axis=1, tiled=True)
    piece_gain = lax.all_gather(gains, ("pool", "tp"), axis=1, tiled=True)
    widened = piece_tokens.astype(jnp.float32)
    scaled = (widened * piece_gain.astype(jnp.float32)).astype(jnp.bfloat16)
    query_sum = jnp.dot(scaled, query_weight, preferred_element_type=jnp.float32)
    squares = jnp.sum(widened * widened, axis=1)
    key_total, value_total = lax.psum((key_terms, value_terms), ("pool", "tp"))
    key_sum = lax.dynamic_slice_in_dim(key_total, kv_start * head_dim, kv_width, 1)
    value_sum = lax.dynamic_slice_in_dim(value_total, kv_start * head_dim, kv_width, 1)
    root = jnp.sqrt(squares / model_width + epsilon)
    positions = lax.dynamic_index_in_dim(lengths, inst_id, 0, keepdims=False)
    queries = rotate(
        (query_sum / root[:, None]).reshape(batch_rows, head_count, head_dim), positions
    ).astype(jnp.bfloat16)
    own_keys = (
        rotate((key_sum / root[:, None]).reshape(batch_rows, kv_count, head_dim), positions)
        .reshape(batch_rows, kv_width)
        .astype(jnp.bfloat16)
    )
    own_values = (value_sum / root[:, None]).astype(jnp.bfloat16)
    queries_flat = queries.reshape(batch_rows, head_count * head_dim)
    offloaded = lax.dynamic_index_in_dim(offload, inst_id, 0, keepdims=False)
    host_row = lax.dynamic_index_in_dim(host_instance, inst_id, 0, keepdims=False)
    on_prefill = pool_id == 1
    moving = (offloaded == 1) & on_prefill
    routed = (host_row[None, :] == jnp.arange(instance_count, dtype=jnp.int32)[:, None]) & moving[
        None, :
    ]
    routed_rows = routed[:, :, None]
    send_queries = jnp.where(routed_rows, queries_flat[None], jnp.zeros((), jnp.bfloat16))
    send_keys = jnp.where(routed_rows, own_keys[None], jnp.zeros((), jnp.bfloat16))
    send_values = jnp.where(routed_rows, own_values[None], jnp.zeros((), jnp.bfloat16))
    got_queries, got_keys, got_values = (
        lax.all_to_all(send_queries, "inst", split_axis=0, concat_axis=0, tiled=True),
        lax.all_to_all(send_keys, "inst", split_axis=0, concat_axis=0, tiled=True),
        lax.all_to_all(send_values, "inst", split_axis=0, concat_axis=0, tiled=True),
    )
    slot_count = key_cache.shape[2]
    flags_flat = offload.reshape(-1)
    hosts_flat = host_instance.reshape(-1)
    slots_flat = cache_slot.reshape(-1)
    lengths_flat = lengths.reshape(-1)
    ownership = (flags_flat[None, :] == 1) & (hosts_flat[None, :] == inst_id) & on_prefill
    ownership = ownership & (
        slots_flat[None, :] == jnp.arange(slot_count, dtype=jnp.int32)[:, None]
    )
    ownership_matrix = ownership.astype(jnp.bfloat16)
    hosted_queries = jnp.dot(
        ownership_matrix,
        got_queries.reshape(-1, head_count * head_dim),
        preferred_element_type=jnp.float32,
    ).astype(jnp.bfloat16)
    hosted_keys = jnp.dot(
        ownership_matrix, got_keys.reshape(-1, kv_width), preferred_element_type=jnp.float32
    ).astype(jnp.bfloat16)
    hosted_values = jnp.dot(
        ownership_matrix, got_values.reshape(-1, kv_width), preferred_element_type=jnp.float32
    ).astype(jnp.bfloat16)
    hosted_lengths = jnp.sum(jnp.where(ownership, lengths_flat[None, :], 0), axis=1)
    use_queries = jnp.where(on_prefill, hosted_queries, queries_flat)
    use_keys = jnp.where(on_prefill, hosted_keys, own_keys)
    use_values = jnp.where(on_prefill, hosted_values, own_values)
    use_lengths = jnp.where(on_prefill, hosted_lengths, positions)
    local_keys = lax.dynamic_slice_in_dim(key_cache[0, 0], kv_start * head_dim, kv_width, 2)
    local_values = lax.dynamic_slice_in_dim(value_cache[0, 0], kv_start * head_dim, kv_width, 2)
    attended = attend(
        use_queries.reshape(slot_count, kv_count, head_count // kv_count, head_dim),
        local_keys,
        local_values,
        use_lengths,
        use_keys,
        use_values,
    )
    replies = jnp.dot(ownership_matrix.T, attended, preferred_element_type=jnp.float32).astype(
        jnp.bfloat16
    )
    replies = replies.reshape(instance_count, batch_rows, head_count * head_dim)
    returned = lax.all_to_all(replies, "inst", split_axis=0, concat_axis=0, tiled=True)
    returned_rows = jnp.sum(returned.astype(jnp.float32), axis=0).astype(jnp.bfloat16)
    resident = jnp.where((offloaded == 0)[:, None], attended, jnp.zeros((), jnp.bfloat16))
    own_rows = jnp.where(on_prefill, returned_rows, resident)
    partial_value = jnp.dot(own_rows, output_weight, preferred_element_type=jnp.float32)
    result = lax.psum_scatter(partial_value, ("pool", "tp"), scatter_dimension=1, tiled=True)
    return result.astype(jnp.bfloat16).reshape(1, batch_rows, -1)


def solution(mesh):
    in_specs = (
        P("inst", None, ("pool", "tp")),
        P(("pool", "tp")),
        P(None, "tp"),
        P(("pool", "tp"), None),
        P(("pool", "tp"), None),
        P("tp", None),
        P("pool", "inst", None, None, None),
        P("pool", "inst", None, None, None),
        P(),
        P(),
        P(),
        P(),
    )
    out_specs = P("inst", None, ("pool", "tp"))
    return jax.shard_map(shards, mesh=mesh, in_specs=in_specs, out_specs=out_specs, check_vma=False)
```

profile of v0, /device:TPU:2, one launch (start us, length us, event | category | flops | bytes accessed | tf_op | source)
XLA Modules:
  0.0 491.4 jit_solution(5752311513406988257)
XLA Ops:
  6.5 0.0 copy-start
  6.5 0.0 all-reduce.3.cloned.1.call-start
  6.5 0.8 convert_element_type.87
  7.3 1.7 fusion.63
  9.0 1.7 fusion.65
  10.7 0.0 all-reduce.3.cloned.1.call-update
  10.7 0.8 broadcast_in_dim.96
  11.5 0.7 fusion.73
  12.2 0.7 fusion.72
  12.9 0.7 and_and_fusion
  13.6 0.7 compare_bitcast_fusion
  14.3 78.8 %all-gather = bf16[1,32,8192]{2,1,0:T(8,128)(2,1)S(1)} all-gather(bf16[1,32,128]{2,1,0:T(8,128)(2,1)} %param.12), channel_id=2, replica_groups=mesh['pool'=2,'inst'=4,'tp'=32] {'pool','tp'}, dimensions={2}, use_global_device_ids=true | all-gather | bytes 532480 | tf_op jit(solution)/shard_map/all_gather | solution.py:101
  93.1 0.1 and.61
  93.2 0.8 eq.86
  94.0 69.0 %all-gather.2 = bf16[64,1,128]{2,1,0:T(2,128)(2,1)S(1)} all-gather(bf16[1,1,128]{2,1,0:T(2,128)(2,1)} %bitcast.73), channel_id=3, replica_groups=mesh['pool'=2,'inst'=4,'tp'=32] {'pool','tp'}, dimensions={0}, use_global_device_ids=true | all-gather | bytes 16640 | tf_op jit(solution)/shard_map/all_gather | solution.py:102
  163.0 0.2 fusion.12
  163.3 0.1 select_reduce_fusion.1
  163.4 2.0 fusion
  165.5 21.4 %all-reduce.3.cloned.1.call-done = (f32[32,512]{1,0:T(8,128)}, f32[32,512]{1,0:T(8,128)}) async-done(((f32[32,512]{1,0:T(8,128)}, f32[32,512]{1,0:T(8,128)}), (f32[32,512]{1,0:T(8,128)}, f32[32,512]{1,0:T(8,128)})) %all-reduce.3.cloned.1.call-update) | async-done | bytes 131088 | tf_op jit(solution)/shard_map/psum | solution.py:107
  186.8 0.8 divide_convert_fusion
  187.6 0.1 fusion.35
  187.8 0.1 maximum_bitcast_fusion
  187.9 0.1 pad_maximum_fusion
  188.0 0.7 broadcast_select_fusion
  188.7 4.8 all-to-all-start
  193.5 0.7 broadcast_select_fusion.3
  194.2 3.5 all-to-all-done
  197.6 4.7 all-to-all-start.1
  202.3 0.1 fusion.1
  202.4 3.9 all-to-all-done.1
  206.3 4.7 all-to-all-start.2
  211.0 0.0 reduce-scatter.2.cloned.1.call-start
  211.0 0.2 fusion.5
  211.2 1.9 fusion.15
  213.1 0.2 select_reduce_fusion
  213.3 0.2 fusion.46
  213.5 0.1 fusion.57
  213.6 1.6 fusion.13
  215.2 0.0 all-to-all-done.2
  215.2 0.1 fusion.10
  215.3 0.3 convolution_convert_fusion
  215.6 8.6 %all_to_all.20 = bf16[4,32,128]{2,1,0:T(8,128)(2,1)S(1)} all-to-all(bf16[4,32,128]{2,1,0:T(8,128)(2,1)S(1)} %bitcast.70), channel_id=1, replica_groups=mesh['pool'=2,'inst'=4,'tp'=32] {'inst'}, dimensions={0} | all-to-all | bytes 65536 | tf_op jit(solution)/shard_map/all_to_all | solution.py:178
  224.2 0.0 copy-done
  224.2 1.5 fusion.47
  225.7 0.0 reduce-scatter.2.cloned.1.call-update
  225.7 257.5 %reduce-scatter.2.cloned.1.call-done = f32[32,128]{1,0:T(8,128)} async-done(((f32[32,8192]{1,0:T(8,128)}), f32[32,128]{1,0:T(8,128)}) %reduce-scatter.2.cloned.1.call-update) | async-done | bytes 16400 | tf_op jit(solution)/shard_map/reduce_scatter | solution.py:183
  483.2 1.3 convert_bitcast_fusion
  (7 shorter events, 0.1 us)
Async XLA Ops:
  6.5 217.7 %copy-start = (bf16[128,8192]{1,0:T(8,128)(2,1)S(1)}, bf16[128,8192]{1,0:T(8,128)(2,1)}, u32[]{:S(2)}) copy-start(bf16[128,8192]{1,0:T(8,128)(2,1)} %param.17) | copy-start | bytes 6291460
  6.5 180.3 %all-reduce.3.cloned.1.call-start = ((), (), s32[]{:S(2)}) async-start(), calls=%async_computation.6 | async-start | bytes 262144 | tf_op jit(solution)/shard_map/psum | solution.py:107
  188.7 8.9 %all-to-all-start = ((bf16[4,32,128]{2,1,0:T(8,128)(2,1)}), bf16[4,32,128]{2,1,0:T(8,128)(2,1)S(1)}, u32[]{:S(2)}, u32[]{:S(2)}) async-start(bf16[4,32,128]{2,1,0:T(8,128)(2,1)} %get-tuple-element.19), calls=%async_computation | async-start | bytes 65536 | tf_op jit(solution)/shard_map/all_to_all | solution.py:134
  197.6 8.7 %all-to-all-start.1 = ((bf16[4,32,128]{2,1,0:T(8,128)(2,1)}), bf16[4,32,128]{2,1,0:T(8,128)(2,1)S(1)}, u32[]{:S(2)}, u32[]{:S(2)}) async-start(bf16[4,32,128]{2,1,0:T(8,128)(2,1)} %get-tuple-element.18), calls=%async_computation.1 | async-start | bytes 65536 | tf_op jit(solution)/shard_map/all_to_all | solution.py:135
  206.3 8.9 %all-to-all-start.2 = ((bf16[4,32,128]{2,1,0:T(8,128)(2,1)}), bf16[4,32,128]{2,1,0:T(8,128)(2,1)S(1)}, u32[]{:S(2)}, u32[]{:S(2)}) async-start(bf16[4,32,128]{2,1,0:T(8,128)(2,1)} %get-tuple-element.17), calls=%async_computation.2 | async-start | bytes 65536 | tf_op jit(solution)/shard_map/all_to_all | solution.py:136
  211.0 272.2 %reduce-scatter.2.cloned.1.call-start = ((), (), s32[]{:S(2)}) async-start(), calls=%async_computation.5 | async-start | bytes 1064960 | tf_op jit(solution)/shard_map/reduce_scatter | solution.py:183
Sparse Core Ops, SparseCore 0:
  10.9 175.8 all-reduce.2
  225.8 257.3 reduce-scatter.1
where the time goes:
time: 499 us; the launch traced here: 491 us
  waiting for transfers between devices  286 us (57%)
  blocking collectives  156 us (31%)
  starting transfers between devices  14.2 us (3%)
  between operations  13.5 us (3%)
  matrix products  11 us (2%)
  other arithmetic  7.64 us (2%)
    reduce_scatter x1, waiting for transfers between devices, shards(): lax.psum_scatter(partial_value, ('pool', 'tp'), scatter_dimension=1, tile...  258 us
    all_gather x1, blocking collectives, shards(): piece_tokens = lax.all_gather(tokens, ('pool', 'tp'), axis=1, tiled=True)  78.8 us
    all_gather x1, blocking collectives, shards(): piece_gain = lax.all_gather(gains, ('pool', 'tp'), axis=1, tiled=True)  69 us
    psum x1, waiting for transfers between devices, shards(): key_total, value_total = lax.psum((key_terms, value_terms), ('pool', 'tp'))  21.4 us
  transfers between devices with their start and end apart: 5, of which 4 were waited for; matrix products, arithmetic and copies ran while one was open for 2% of the time, Pallas kernels for 0%

commit v1 on v0

v1 whole, which is shorter than its diff:
```python
import jax
import jax.numpy as jnp
import numpy as np
from jax import lax
from jax.sharding import Mesh
from jax.sharding import PartitionSpec as P

HD = 128
G = 8
epsilon = 1e-05
rope_base = 500000.0
AXES = ("pool", "inst", "z", "yh", "core")
SIZES = (2, 4, 8, 2, 2)
TP = ("z", "yh", "core")
RING = ("z", "yh")
BF = jnp.bfloat16
F32 = jnp.float32


def swap_core(x):
    return lax.ppermute(x, "core", [(0, 1), (1, 0)])


def shards(
    hidden_states,
    norm_gain,
    query_weight,
    key_weight,
    value_weight,
    output_weight,
    key_cache,
    value_cache,
    lengths,
    offload,
    host_instance,
    cache_slot,
):
    pool = lax.axis_index("pool")
    inst = lax.axis_index("inst")
    z = lax.axis_index("z")
    core = lax.axis_index("core")
    rows = hidden_states.shape[1]
    width = query_weight.shape[0]
    half = width // 2
    ring = SIZES[2] * SIZES[3]

    x = hidden_states[0].astype(F32)
    scaled = (x * norm_gain.astype(F32)[None, :]).astype(BF)
    squares = jnp.sum(x * x, axis=1)
    high = squares.astype(BF)
    low = (squares - high.astype(F32)).astype(BF)
    extra = jnp.zeros((16, HD), BF).at[0, :rows].set(high).at[1, :rows].set(low)
    k_terms = jnp.dot(scaled, key_weight, preferred_element_type=F32).astype(BF)
    v_terms = jnp.dot(scaled, value_weight, preferred_element_type=F32).astype(BF)

    def by_peer(t):
        t = t.reshape(rows, 4, HD).transpose(1, 0, 2)
        return jnp.repeat(t, ring // 4, axis=0)

    message = jnp.concatenate(
        [
            jnp.broadcast_to(scaled[None], (ring, rows, HD)),
            by_peer(k_terms),
            by_peer(v_terms),
            jnp.broadcast_to(extra[None], (ring, 16, HD)),
        ],
        axis=1,
    )
    got = lax.all_to_all(message, RING, 0, 0, tiled=True)
    other = swap_core(got)
    core0 = jnp.where(core == 0, got, other)
    core1 = jnp.where(core == 0, other, got)
    both = jnp.stack([core0, core1], axis=1).reshape(2 * ring, -1, HD)

    tokens = both[:, :rows].transpose(1, 0, 2).reshape(rows, half)
    weight = lax.dynamic_slice_in_dim(query_weight, pool * half, half, 0)
    q_part = jnp.dot(tokens, weight, preferred_element_type=F32)
    sums = jnp.sum(both[:, rows:].astype(F32), axis=0)
    squares = sums[2 * rows, :rows] + sums[2 * rows + 1, :rows]
    high = squares.astype(BF)
    low = (squares - high.astype(F32)).astype(BF)
    lane = jnp.arange(HD)[None, :]
    extra = jnp.where(lane < HD // 2, high[:, None], low[:, None])
    message = jnp.concatenate([q_part.astype(BF), sums[: 2 * rows].astype(BF), extra], axis=0)
    message = jnp.broadcast_to(message[None], (8, 4 * rows, HD))
    got = lax.all_to_all(message, ("pool", "inst"), 0, 0, tiled=True)

    flags = offload.reshape(-1)
    hosts = host_instance.reshape(-1)
    slots = cache_slot.reshape(-1)
    spans = lengths.reshape(-1)
    request = jnp.arange(flags.shape[0], dtype=jnp.int32)
    slot = jnp.arange(rows, dtype=jnp.int32)[:, None]
    hosted = (flags == 1)[None, :] & (hosts == inst)[None, :] & (slots[None, :] == slot)
    resident = request[None, :] == inst * rows + slot
    chosen = jnp.where(pool == 1, hosted, resident)
    positions = jnp.sum(jnp.where(chosen, spans[None, :], 0), axis=1)
    pick = chosen.astype(BF)
    pick = jnp.concatenate([pick, pick], axis=1)
    parts = got.reshape(8, 4, rows, HD).transpose(0, 2, 1, 3).reshape(8 * rows, 4 * HD)
    mine = jnp.dot(pick, parts, preferred_element_type=F32)
    q, k, v, s = jnp.split(mine, 4, axis=1)
    squares = s[:, 0] + s[:, HD // 2]
    root = jnp.sqrt(squares / width + epsilon)[:, None]
    frequency = jnp.asarray(
        np.power(np.float32(rope_base), -np.arange(HD // 2, dtype=np.float32) * 2.0 / HD).astype(np.float32)
    )
    angles = positions.astype(F32)[:, None] * frequency[None, :]
    cosine, sine = jnp.cos(angles), jnp.sin(angles)

    def rotate(t):
        a, b = t[:, : HD // 2], t[:, HD // 2 :]
        return jnp.concatenate([a * cosine - b * sine, a * sine + b * cosine], axis=1)

    q = rotate(q / root).astype(BF)
    k = rotate(k / root).astype(BF)
    v = (v / root).astype(BF)

    start = (z // 2) * HD
    keys = lax.dynamic_slice_in_dim(key_cache[0, 0], start, HD, 2)
    values = lax.dynamic_slice_in_dim(value_cache[0, 0], start, HD, 2)
    factor = HD ** (-0.5)
    scores = jnp.einsum("rd,rpd->rp", q, keys, preferred_element_type=F32) * factor
    own_score = jnp.sum(q.astype(F32) * k.astype(F32), axis=1, keepdims=True) * factor
    visible = jnp.arange(keys.shape[1])[None, :] < positions[:, None]
    peak = jnp.maximum(jnp.max(jnp.where(visible, scores, -jnp.inf), axis=1, keepdims=True), own_score)
    exps = jnp.where(visible, jnp.exp(scores - peak), 0.0)
    own_exp = jnp.exp(own_score - peak)
    total = jnp.sum(exps, axis=1, keepdims=True) + own_exp
    weights = (exps / total).astype(BF)
    own_weight = (own_exp / total).astype(BF)
    mixed = jnp.einsum("rp,rpd->rd", weights, values, preferred_element_type=F32)
    mixed = (mixed + own_weight.astype(F32) * v.astype(F32)).astype(BF)

    got = lax.all_to_all(jnp.broadcast_to(mixed[None], (8, rows, HD)), ("pool", "inst"), 0, 0, tiled=True)
    flags_own = lax.dynamic_index_in_dim(offload, inst, 0, keepdims=False)
    hosts_own = lax.dynamic_index_in_dim(host_instance, inst, 0, keepdims=False)
    slots_own = lax.dynamic_index_in_dim(cache_slot, inst, 0, keepdims=False)
    place = jnp.where(flags_own == 1, (4 + hosts_own) * rows + slots_own, inst * rows + slot[:, 0])
    back = (place[:, None] == jnp.arange(8 * rows, dtype=jnp.int32)[None, :]).astype(BF)
    attended = jnp.dot(back, got.reshape(8 * rows, HD), preferred_element_type=F32).astype(BF)

    weight = lax.dynamic_slice_in_dim(output_weight, pool * half, half, 1)
    partial = jnp.dot(attended, weight, preferred_element_type=F32).astype(BF)
    partial = partial.reshape(rows, ring, 2, HD).transpose(2, 1, 0, 3)
    keep = lax.dynamic_index_in_dim(partial, core, 0, keepdims=False)
    give = lax.dynamic_index_in_dim(partial, 1 - core, 0, keepdims=False)
    pair = (keep.astype(F32) + swap_core(give).astype(F32)).astype(BF)
    got = lax.all_to_all(pair, RING, 0, 0, tiled=True)
    return jnp.sum(got.astype(F32), axis=0).astype(BF)[None]


def solution(mesh):
    finer = Mesh(mesh.devices.reshape(SIZES), AXES)
    in_specs = (
        P("inst", None, ("pool",) + TP),
        P(("pool",) + TP),
        P(None, TP),
        P(("pool",) + TP, None),
        P(("pool",) + TP, None),
        P(TP, None),
        P("pool", "inst", None, None, None),
        P("pool", "inst", None, None, None),
        P(),
        P(),
        P(),
        P(),
    )
    out_specs = P("inst", None, ("pool",) + TP)
    return jax.shard_map(shards, mesh=finer, in_specs=in_specs, out_specs=out_specs, check_vma=False)
```

time: 499 us -> 81.9 us (0.16); the launches traced: 491 us -> 81.2 us
  waiting for transfers between devices: 286 us -> 14.1 us
  blocking collectives: 156 us -> 43.2 us
  between operations: 13.5 us -> 0.32 us
    reduce_scatter x1 -> x0, waiting for transfers between devices: 258 us -> none  [shards(): lax.psum_scatter(partial_value, ('pool', 'tp'), scatter_dimension=1, tile...]
    all_gather x2 -> x0, blocking collectives: 148 us -> none  [the longest x1 78.8 us: shards(): piece_tokens = lax.all_gather(tokens, ('pool', 'tp'), axis=1, tiled=True)]
    all_to_all x1 -> x2, blocking collectives: 8.59 us -> 43.2 us  [the longest x1 28.4 us: shards(): got = lax.all_to_all(message, RING, 0, 0, tiled=True)]
    psum x1 -> x0, waiting for transfers between devices: 21.4 us -> none  [shards(): key_total, value_total = lax.psum((key_terms, value_terms), ('pool', 'tp'))]
    all_to_all x3 -> x2, starting transfers between devices: 14.2 us -> 9.37 us  [the longest x1 4.95 us: shards(): got = lax.all_to_all(message, ('pool', 'inst'), 0, 0, tiled=True)]
    dot_general x10 -> x7, matrix products: 11 us -> 6.45 us  [the longest x1 1.85 us: shards(): jnp.einsum('rd,rpd->rp', q, keys, preferred_element_type=F32) * factor]
    all_to_all x3 -> x2, waiting for transfers between devices: 7.33 us -> 11 us  [the longest x1 5.94 us: shards(): got = lax.all_to_all(message, ('pool', 'inst'), 0, 0, tiled=True)]
  transfers between devices with their start and end apart: 5 -> 4, of which waited for: 4 -> 4; matrix products, arithmetic and copies ran while one was open for 2% -> 1% of each run, Pallas kernels for 0% -> 0%
where the time goes in v1:
time: 81.9 us; the launch traced here: 81.2 us
  blocking collectives  43.2 us (53%)
  waiting for transfers between devices  14.1 us (17%)
  starting transfers between devices  9.46 us (12%)
  matrix products  6.45 us (8%)
  other arithmetic  4.74 us (6%)
  local copies, waits for them, and re-layouts  2.91 us (4%)
    all_to_all x1, blocking collectives, shards(): got = lax.all_to_all(message, RING, 0, 0, tiled=True)  28.4 us
    all_to_all x1, blocking collectives, shards(): got = lax.all_to_all(pair, RING, 0, 0, tiled=True)  14.8 us
    all_to_all x1, waiting for transfers between devices, shards(): got = lax.all_to_all(message, ('pool', 'inst'), 0, 0, tiled=True)  5.94 us
    all_to_all x1, waiting for transfers between devices, shards(): lax.all_to_all(jnp.broadcast_to(mixed[None], (8, rows, HD)), ('pool', 'in...  5.09 us
    all_to_all x1, starting transfers between devices, shards(): got = lax.all_to_all(message, ('pool', 'inst'), 0, 0, tiled=True)  4.95 us
    all_to_all x1, starting transfers between devices, shards(): lax.all_to_all(jnp.broadcast_to(mixed[None], (8, rows, HD)), ('pool', 'in...  4.42 us
    ppermute x2, waiting for transfers between devices, swap_core(): return lax.ppermute(x, 'core', [(0, 1), (1, 0)])  3.1 us
    dot_general x1, matrix products, shards(): jnp.einsum('rd,rpd->rp', q, keys, preferred_element_type=F32) * factor  1.85 us
  transfers between devices with their start and end apart: 4, of which 4 were waited for; matrix products, arithmetic and copies ran while one was open for 1% of the time, Pallas kernels for 0%

profile of v1, /device:TPU:2, one launch (start us, length us, event | category | flops | bytes accessed | tf_op | source)
XLA Modules:
  0.0 81.2 jit_solution(673918520540644196)
XLA Ops:
  0.0 0.0 copy-start
  0.0 0.0 copy-start.4
  0.0 0.0 copy-start.3
  0.0 1.0 %fusion.28 = f32[32]{0:T(128)S(1)} fusion(bf16[1,32,128]{2,1,0:T(8,128)(2,1)} %param.17), kind=kLoop, calls=%fused_computation.48 | loop fusion | flops 12256 | bytes 8320 | tf_op jit(solution)/shard_map/reduce_sum | solution.py:49
  1.0 0.7 convert_element_type.151
  1.6 0.7 fusion.50
  2.3 1.0 %convolution_convert_fusion.2 = bf16[32,512]{1,0:T(8,128)(2,1)S(1)} fusion(bf16[128,512]{1,0:T(8,128)(2,1)} %param.20, bf16[1,32,128]{2,1,0:T(8,128)(2,1)} %param.17, f32[128]{0:T(128)S(1)} %convert_element_type.151), kind=kOutput, calls=%fused_computation.3 | convolution fusion | flops 4222976 | bytes 172544 | tf_op jit(solution)/shard_map/dot_general | solution.py:53
  3.4 1.1 %convolution_convert_fusion.1 = bf16[32,512]{1,0:T(8,128)(2,1)S(1)} fusion(bf16[128,512]{1,0:T(8,128)(2,1)} %param.21, bf16[1,32,128]{2,1,0:T(8,128)(2,1)} %param.17, f32[128]{0:T(128)S(1)} %convert_element_type.151), kind=kOutput, calls=%fused_computation.2 | convolution fusion | flops 4222976 | bytes 172544 | tf_op jit(solution)/shard_map/dot_general | solution.py:54
  4.6 0.2 scatter.9
  4.9 28.4 %all_to_all.20 = bf16[16,112,128]{2,1,0:T(8,128)(2,1)S(1)} all-to-all(bf16[16,112,128]{2,1,0:T(8,128)(2,1)S(1)} %pad_maximum_fusion.1), channel_id=1, replica_groups=mesh['pool'=2,'inst'=4,'z'=8,'yh'=2,'core'=2] {'z','yh'}, dimensions={0} | all-to-all | bytes 917504 | tf_op jit(solution)/shard_map/all_to_all | solution.py:69
  33.2 0.0 collective-permute-start
  33.2 0.0 copy-done.4
  33.2 0.0 copy-done.3
  33.3 0.0 copy-start.1
  33.3 1.8 %collective-permute-done = bf16[16,112,128]{2,1,0:T(8,128)(2,1)S(1)} collective-permute-done((bf16[16,112,128]{2,1,0:T(8,128)(2,1)S(1)}, bf16[16,112,128]{2,1,0:T(8,128)(2,1)S(1)}, u32[]{:S(2)}, u32[]{:S(2)}) %collective-permute-start) | collective-permute-done | bytes 458784 | tf_op jit(solution)/shard_map/ppermute | solution.py:21
  35.0 0.1 select_bitcast_fusion.1
  35.1 0.0 copy-start.5
  35.1 0.0 copy-start.2
  35.1 0.1 pad_maximum_fusion
  35.2 0.0 copy-start.6
  35.2 0.1 convert_reduce_fusion
  35.4 0.0 copy-done.1
  35.4 0.3 convolution_convert_fusion.4
  35.7 0.1 broadcast_select_fusion
  35.8 0.7 broadcast_in_dim.110
  36.5 4.9 %all-to-all-start.1 = ((bf16[8,128,128]{2,1,0:T(8,128)(2,1)}), bf16[8,128,128]{2,1,0:T(8,128)(2,1)S(1)}, u32[]{:S(2)}, u32[]{:S(2)}) async-start(bf16[8,128,128]{2,1,0:T(8,128)(2,1)} %broadcast_in_dim.110), calls=%async_computation.1 | async-start | bytes 524288 | tf_op jit(solution)/shard_map/all_to_all | solution.py:86
  41.4 0.1 and.35
  41.5 0.0 copy-done.5
  41.5 0.1 broadcast_in_dim.61
  41.6 0.0 copy-done.2
  41.6 0.1 eq.92
  41.7 0.2 select_reduce_fusion.1
  41.9 5.9 %all-to-all-done.1 = bf16[8,128,128]{2,1,0:T(8,128)(2,1)S(1)} async-done(((bf16[8,128,128]{2,1,0:T(8,128)(2,1)}), bf16[8,128,128]{2,1,0:T(8,128)(2,1)S(1)}, u32[]{:S(2)}, u32[]{:S(2)}) %all-to-all-start.1) | async-done | bytes 262176 | tf_op jit(solution)/shard_map/all_to_all | solution.py:86
  47.9 0.1 copy.34
  48.0 0.2 fusion.8
  48.1 0.2 fusion.42
  48.3 0.1 slice_divide_fusion.1
  48.4 0.0 copy-done.6
  48.4 0.1 fusion.35
  48.6 0.1 fusion.58
  48.7 1.8 %fusion.2 = f32[32,1,128]{2,1,0:T(1,128)S(1)} fusion(bf16[1,1,32,128,512]{4,3,2,1,0:T(8,128)(2,1)} %param.23, s32[]{:T(128)S(6)} %select_n.80, bf16[32,128,1]{1,0,2:T(8,128)(2,1)S(1)} %fusion.58), kind=kOutput, calls=%fused_computation.8 | convolution fusion | flops 1048576 | bytes 1073156 | tf_op jit(solution)/shard_map/rd,rpd->rp/dot_general | solution.py:123
  50.5 0.2 multiply_reduce_fusion
  50.7 0.2 fusion.49
  50.9 0.1 fusion.51
  51.0 1.6 %fusion = f32[32,1,128]{2,1,0:T(1,128)S(1)} fusion(bf16[1,1,32,128,512]{4,3,2,1,0:T(8,128)(2,1)} %param.24, s32[]{:T(128)S(6)} %select_n.80, bf16[32,128,1]{1,0,2:T(8,128)(2,1)S(1)} %fusion.51), kind=kOutput, calls=%fused_computation.6 | convolution fusion | flops 1048576 | bytes 1073156 | tf_op jit(solution)/shard_map/rp,rpd->rd/dot_general | solution.py:132
  52.7 0.1 add_convert_fusion
  52.8 0.6 broadcast_in_dim.113
  53.4 4.4 %all-to-all-start.2 = ((bf16[8,32,128]{2,1,0:T(8,128)(2,1)}), bf16[8,32,128]{2,1,0:T(8,128)(2,1)S(1)}, u32[]{:S(2)}, u32[]{:S(2)}) async-start(bf16[8,32,128]{2,1,0:T(8,128)(2,1)} %broadcast_in_dim.113), calls=%async_computation.2 | async-start | bytes 131072 | tf_op jit(solution)/shard_map/all_to_all | solution.py:135
  57.8 5.1 %all-to-all-done.2 = bf16[8,32,128]{2,1,0:T(8,128)(2,1)S(1)} async-done(((bf16[8,32,128]{2,1,0:T(8,128)(2,1)}), bf16[8,32,128]{2,1,0:T(8,128)(2,1)S(1)}, u32[]{:S(2)}, u32[]{:S(2)}) %all-to-all-start.2) | async-done | bytes 65568 | tf_op jit(solution)/shard_map/all_to_all | solution.py:135
  62.9 0.0 copy-done
  62.9 0.4 convolution_convert_fusion
  63.4 0.2 reshape.243
  63.6 0.6 constant_dynamic-slice_fusion
  64.1 0.1 copy.59
  64.2 0.1 collective-permute-start.1
  64.3 1.3 %collective-permute-done.1 = bf16[16,32,128]{2,1,0:T(8,128)(2,1)S(1)} collective-permute-done((bf16[16,32,128]{2,1,0:T(8,128)(2,1)S(1)}, bf16[16,32,128]{2,1,0:T(8,128)(2,1)S(1)}, u32[]{:S(2)}, u32[]{:S(2)}) %collective-permute-start.1) | collective-permute-done | bytes 131104 | tf_op jit(solution)/shard_map/ppermute | solution.py:21
  65.6 0.1 fusion.13
  65.7 14.8 %all_to_all.21 = bf16[16,32,128]{2,1,0:T(8,128)(2,1)S(1)} all-to-all(bf16[16,32,128]{2,1,0:T(8,128)(2,1)S(1)} %fusion.13), channel_id=1, replica_groups=mesh['pool'=2,'inst'=4,'z'=8,'yh'=2,'core'=2] {'z','yh'}, dimensions={0} | all-to-all | bytes 262144 | tf_op jit(solution)/shard_map/all_to_all | solution.py:149
  80.6 0.6 reduce_sum.65
  (23 shorter events, 0.2 us)
Async XLA Ops:
  0.0 62.9 %copy-start = (bf16[128,8192]{1,0:T(8,128)(2,1)S(1)}, bf16[128,8192]{1,0:T(8,128)(2,1)}, u32[]{:S(2)}) copy-start(bf16[128,8192]{1,0:T(8,128)(2,1)} %param.22) | copy-start | bytes 6291460
  0.0 33.2 %copy-start.4 = (s32[4,32]{1,0:T(4,128)S(1)}, s32[4,32]{1,0:T(4,128)}, u32[]{:S(2)}) copy-start(s32[4,32]{1,0:T(4,128)} %param.26) | copy-start | bytes 1540
  0.0 33.2 %copy-start.3 = (s32[4,32]{1,0:T(4,128)S(1)}, s32[4,32]{1,0:T(4,128)}, u32[]{:S(2)}) copy-start(s32[4,32]{1,0:T(4,128)} %param.27) | copy-start | bytes 1540
  33.2 1.8 %collective-permute-start = (bf16[16,112,128]{2,1,0:T(8,128)(2,1)S(1)}, bf16[16,112,128]{2,1,0:T(8,128)(2,1)S(1)}, u32[]{:S(2)}, u32[]{:S(2)}) collective-permute-start(bf16[16,112,128]{2,1,0:T(8,128)(2,1)S(1)} %all_to_all.20), channel_id=1, source_target_pairs={{0,1},{1,0},{2,3},{3,2},{4,5},{5,4},{6,7},{7,6},{8,9},{9,8},{10,11... | collective-permute-start | bytes 1376264 | tf_op jit(solution)/shard_map/ppermute | solution.py:21
  33.3 2.1 %copy-start.1 = (bf16[8192,128]{1,0:T(8,128)(2,1)S(1)}, bf16[8192,128]{1,0:T(8,128)(2,1)}, u32[]{:S(2)}) copy-start(bf16[8192,128]{1,0:T(8,128)(2,1)} %param.19) | copy-start | bytes 6291460
  35.1 6.4 %copy-start.5 = (s32[4,32]{1,0:T(4,128)S(1)}, s32[4,32]{1,0:T(4,128)}, u32[]{:S(2)}) copy-start(s32[4,32]{1,0:T(4,128)} %param.25) | copy-start | bytes 1540
  35.1 6.5 %copy-start.2 = (s32[4,32]{1,0:T(4,128)S(1)}, s32[4,32]{1,0:T(4,128)}, u32[]{:S(2)}) copy-start(s32[4,32]{1,0:T(4,128)} %param.28) | copy-start | bytes 1540
  35.2 13.2 %copy-start.6 = (f32[64]{0:T(128)S(1)}, f32[64]{0:T(128)}, u32[]{:S(2)}) copy-start(f32[64]{0:T(128)} %constant.141.clone) | copy-start | bytes 772
  36.5 11.4 %all-to-all-start.1 = ((bf16[8,128,128]{2,1,0:T(8,128)(2,1)}), bf16[8,128,128]{2,1,0:T(8,128)(2,1)S(1)}, u32[]{:S(2)}, u32[]{:S(2)}) async-start(bf16[8,128,128]{2,1,0:T(8,128)(2,1)} %broadcast_in_dim.110), calls=%async_computation.1 | async-start | bytes 524288 | tf_op jit(solution)/shard_map/all_to_all | solution.py:86
  53.4 9.5 %all-to-all-start.2 = ((bf16[8,32,128]{2,1,0:T(8,128)(2,1)}), bf16[8,32,128]{2,1,0:T(8,128)(2,1)S(1)}, u32[]{:S(2)}, u32[]{:S(2)}) async-start(bf16[8,32,128]{2,1,0:T(8,128)(2,1)} %broadcast_in_dim.113), calls=%async_computation.2 | async-start | bytes 131072 | tf_op jit(solution)/shard_map/all_to_all | solution.py:135
  64.2 1.4 %collective-permute-start.1 = (bf16[16,32,128]{2,1,0:T(8,128)(2,1)S(1)}, bf16[16,32,128]{2,1,0:T(8,128)(2,1)S(1)}, u32[]{:S(2)}, u32[]{:S(2)}) collective-permute-start(bf16[16,32,128]{2,1,0:T(8,128)(2,1)S(1)} %bitcast.98), channel_id=1, source_target_pairs={{0,1},{1,0},{2,3},{3,2},{4,5},{5,4},{6,7},{7,6},{8,9},{9,8},{10,11... | collective-permute-start | bytes 393224 | tf_op jit(solution)/shard_map/ppermute | solution.py:21

commit v2 on v1

v2 whole, which is shorter than its diff:
```python
import functools

import jax
import jax.numpy as jnp
from jax import lax
from jax.experimental import pallas as pl
from jax.experimental.pallas import tpu as pltpu
from jax.sharding import Mesh
from jax.sharding import PartitionSpec as P

HD = 128
HEADS = 4
REQ = 32
POOLS, INSTS, ZS, YS, CORES = 2, 4, 8, 2, 2
RING = ZS * POOLS
epsilon = 1e-05
rope_base = 500000.0
AXES = ("pool", "inst", "z", "yh", "core")
SIZES = (POOLS, INSTS, ZS, YS, CORES)
TP = ("z", "yh", "core")
BF = jnp.bfloat16
F32 = jnp.float32
I32 = jnp.int32
VMEM = pl.BlockSpec(memory_space=pltpu.VMEM)
ANY = pl.BlockSpec(memory_space=pl.ANY)


def device_number(p, i, z, y, c):
    return (((p * INSTS + i) * ZS + z) * YS + y) * CORES + c


RINGS = [
    [device_number(p, i, z, p ^ s, c) for z in range(ZS) for p in range(POOLS)]
    for s in range(2)
    for i in range(INSTS)
    for c in range(CORES)
]


def ring_exchange(x):
    return lax.all_to_all(x, AXES, 0, 0, axis_index_groups=RINGS, tiled=True)


def swap_core(x):
    return lax.ppermute(x, "core", [(0, 1), (1, 0)])


def iota(shape, axis):
    return lax.broadcasted_iota(I32, shape, axis)


def dot(a, b):
    return jnp.dot(a, b, preferred_element_type=F32)


def split(x):
    high = x.astype(BF)
    return high, (x - high.astype(F32)).astype(BF)


def features_kernel(x_ref, gain_ref, wk_ref, wv_ref, out_ref):
    x = x_ref[0].astype(F32)
    scaled = (x * gain_ref[...].astype(F32)).astype(BF)
    squares = jnp.sum(x * x, axis=1, keepdims=True)
    eye = iota((REQ, HD), 0) == iota((REQ, HD), 1)
    row = jnp.sum(jnp.where(eye, squares, 0.0), axis=0, keepdims=True)
    high = row.astype(BF).astype(F32)
    at = iota((16, HD), 0)
    extra = jnp.where(at == 0, high, jnp.where(at == 1, row - high, 0.0)).astype(BF)
    k = dot(scaled, wk_ref[...]).astype(BF)
    v = dot(scaled, wv_ref[...]).astype(BF)
    for m in range(RING):
        head = slice((m // POOLS) // (ZS // HEADS) * HD, ((m // POOLS) // (ZS // HEADS) + 1) * HD)
        out_ref[m, 0:REQ, :] = scaled
        out_ref[m, REQ : 2 * REQ, :] = k[:, head]
        out_ref[m, 2 * REQ : 3 * REQ, :] = v[:, head]
        out_ref[m, 3 * REQ :, :] = extra


def query_kernel(own_ref, other_ref, wq_ref, out_ref):
    pool, yh, core = lax.axis_index("pool"), lax.axis_index("yh"), lax.axis_index("core")
    side = pool ^ yh
    q = jnp.zeros((REQ, HD), F32)
    sums = jnp.zeros((2 * REQ, HD), F32)
    extra = jnp.zeros((16, HD), F32)
    for m in range(RING):
        z, p = m // POOLS, m % POOLS
        y = p ^ side
        features = jnp.concatenate([own_ref[m, 0:REQ, :], other_ref[m, 0:REQ, :]], axis=1)
        weight = jnp.concatenate([wq_ref[p, z, y, core], wq_ref[p, z, y, 1 - core]], axis=0)
        q += dot(features, weight)
        sums += own_ref[m, REQ : 3 * REQ, :].astype(F32) + other_ref[m, REQ : 3 * REQ, :].astype(F32)
        extra += own_ref[m, 3 * REQ :, :].astype(F32) + other_ref[m, 3 * REQ :, :].astype(F32)
    row = extra[0:1] + extra[1:2]
    eye = iota((REQ, HD), 0) == iota((REQ, HD), 1)
    squares = jnp.sum(jnp.where(eye, row, 0.0), axis=1, keepdims=True)
    high = squares.astype(BF).astype(F32)
    tail = jnp.where(iota((REQ, HD), 1) < HD // 2, high, squares - high)
    message = jnp.concatenate([q, sums[:REQ], sums[REQ:], tail], axis=1).astype(BF)
    for m in range(POOLS * INSTS):
        out_ref[m] = message


def tables_kernel(
    lengths_ref, offload_ref, host_ref, slot_ref, keys_ref, values_ref,
    keys_out, values_out, pick_ref, back_ref, cos_ref, sin_ref, span_ref, sems,
):
    pool, inst, z = lax.axis_index("pool"), lax.axis_index("inst"), lax.axis_index("z")
    lane = pl.ds(pl.multiple_of((z // (ZS // HEADS)) * HD, HD), HD)
    copies = [
        pltpu.make_async_copy(keys_ref.at[0, 0, :, :, lane], keys_out, sems.at[0]),
        pltpu.make_async_copy(values_ref.at[0, 0, :, :, lane], values_out, sems.at[1]),
    ]
    for copy in copies:
        copy.start()
    home = iota((INSTS, REQ), 0) * REQ + iota((INSTS, REQ), 1)
    away = INSTS * REQ + host_ref[...] * REQ + slot_ref[...]
    seat = jnp.where(offload_ref[...] == 1, away, home)
    spans = lengths_ref[...].astype(F32)
    here = iota((REQ, REQ), 0) + (pool * INSTS + inst) * REQ
    square = iota((REQ, REQ), 0) == iota((REQ, REQ), 1)
    pick = jnp.zeros((REQ, POOLS * INSTS * REQ), F32)
    span = jnp.zeros((REQ, 1), F32)
    column = jnp.zeros((REQ, 1), F32)
    for i in range(INSTS):
        sits = seat[i : i + 1, :] == here
        wide = iota((REQ, POOLS * INSTS * REQ), 1) % (INSTS * REQ)
        place = (wide == iota(wide.shape, 0) + i * REQ).astype(F32).astype(BF)
        pick += dot(sits.astype(F32).astype(BF), place)
        span += jnp.sum(jnp.where(sits, spans[i : i + 1, :], 0.0), axis=1, keepdims=True)
        turned = jnp.sum(jnp.where(square, seat[i : i + 1, :].astype(F32), 0.0), axis=1, keepdims=True)
        column += jnp.where(inst == i, turned, 0.0)
    pick_ref[...] = pick.astype(BF)
    seats = iota((REQ, POOLS * INSTS * REQ), 1).astype(F32)
    back_ref[...] = (column == seats).astype(F32).astype(BF)
    half = HD // 2
    lanes = iota((REQ, HD), 1)
    frequency = jnp.exp((lanes % half).astype(F32) * (-2.0 / HD * 13.122363377404328))
    angles = span * frequency
    cos_ref[...] = jnp.cos(angles)
    sin_ref[...] = jnp.where(lanes < half, -jnp.sin(angles), jnp.sin(angles))
    span_ref[...] = jnp.broadcast_to(span, (REQ, HD))
    for copy in copies:
        copy.wait()


def attend_kernel(got_ref, keys_ref, values_ref, pick_ref, cos_ref, sin_ref, span_ref, out_ref, *, width):
    got = got_ref[...].reshape(POOLS * INSTS * REQ, 4 * HD)
    mine = dot(pick_ref[...], got)
    q, k, v, s = (mine[:, n * HD : (n + 1) * HD] for n in range(4))
    squares = s[:, 0:1] + s[:, HD // 2 : HD // 2 + 1]
    root = jnp.sqrt(squares / width + epsilon)

    def rotate(t):
        return t * cos_ref[...] + pltpu.roll(t, HD // 2, 1) * sin_ref[...]

    q = rotate(q / root).astype(BF)
    k = rotate(k / root).astype(BF)
    v = (v / root).astype(BF)
    keys = keys_ref[...].reshape(REQ * HD, HD)
    values = values_ref[...].reshape(REQ * HD, HD)
    every = lax.dot_general(q, keys, (((1,), (1,)), ((), ())), preferred_element_type=F32)
    request = iota((8, HD), 0)
    rows = []
    for group in range(REQ // 8):
        block = jnp.zeros((8, HD), F32)
        for n in range(8):
            r = group * 8 + n
            block = jnp.where(request == n, every[group * 8 : group * 8 + 8, r * HD : (r + 1) * HD], block)
        rows.append(block)
    factor = HD ** (-0.5)
    scores = jnp.concatenate(rows, axis=0) * factor
    own_score = jnp.sum(q.astype(F32) * k.astype(F32), axis=1, keepdims=True) * factor
    visible = iota((REQ, HD), 1).astype(F32) < span_ref[...]
    scores = jnp.where(visible, scores, -jnp.inf)
    peak = jnp.maximum(jnp.max(scores, axis=1, keepdims=True), own_score)
    exps = jnp.exp(scores - peak)
    own_exp = jnp.exp(own_score - peak)
    total = jnp.sum(exps, axis=1, keepdims=True) + own_exp
    weights = exps / total
    own_weight = (own_exp / total).astype(BF).astype(F32)
    request = iota((REQ, HD), 0)
    spread = jnp.concatenate([jnp.where(request == r, weights, 0.0).astype(BF) for r in range(REQ)], axis=1)
    mixed = (dot(spread, values) + own_weight * v.astype(F32)).astype(BF)
    for m in range(POOLS * INSTS * CORES):
        out_ref[m] = mixed


def output_kernel(got_ref, back_ref, own_ref, other_ref, out_ref):
    pool, yh, core = lax.axis_index("pool"), lax.axis_index("yh"), lax.axis_index("core")
    side = pool ^ yh
    back = back_ref[...]
    seats = POOLS * INSTS * REQ
    mine = dot(back, got_ref[:, core].reshape(seats, HD)).astype(BF)
    buddy = dot(back, got_ref[:, 1 - core].reshape(seats, HD)).astype(BF)
    rows = jnp.concatenate([mine, buddy], axis=1)
    for m in range(RING):
        z, p = m // POOLS, m % POOLS
        block = ((p * ZS + z) * YS + (p ^ side)) * CORES + core
        lane = pl.ds(pl.multiple_of(block * HD, HD), HD)
        weight = jnp.concatenate([own_ref[:, lane], other_ref[:, lane]], axis=0)
        out_ref[m] = dot(rows, weight).astype(BF)


def sum_kernel(got_ref, out_ref):
    total = got_ref[0].astype(F32)
    for m in range(1, RING):
        total += got_ref[m].astype(F32)
    out_ref[0] = total.astype(BF)


def call(kernel, shapes, specs, flops, moved, scratch=(), limit=24):
    one = not isinstance(shapes, list)
    return pl.pallas_call(
        kernel,
        out_shape=shapes if one else tuple(shapes),
        in_specs=specs,
        out_specs=VMEM if one else tuple(VMEM for _ in shapes),
        scratch_shapes=list(scratch),
        cost_estimate=pl.CostEstimate(flops=flops, bytes_accessed=moved, transcendentals=0),
        compiler_params=pltpu.CompilerParams(vmem_limit_bytes=limit << 20),
    )


def shape(*dims, dtype=BF):
    return jax.ShapeDtypeStruct(dims, dtype)


def shards(
    hidden_states,
    norm_gain,
    query_weight,
    key_weight,
    value_weight,
    output_weight,
    key_cache,
    value_cache,
    lengths,
    offload,
    host_instance,
    cache_slot,
):
    width = query_weight.shape[0]
    seats = POOLS * INSTS * REQ

    message = call(features_kernel, shape(RING, 3 * REQ + 16, HD), [VMEM] * 4, 1 << 23, 1 << 20)(
        hidden_states, norm_gain.reshape(1, HD), key_weight, value_weight
    )
    buddy_weight = swap_core(output_weight)
    got = ring_exchange(message)
    other = swap_core(got)
    message = call(query_kernel, shape(POOLS * INSTS, REQ, 4 * HD), [VMEM] * 3, 1 << 25, 1 << 22)(
        got, other, query_weight.reshape(POOLS, ZS, YS, CORES, HD, HD)
    )
    keys, values, pick, back, cos, sin, span = call(
        tables_kernel,
        [
            shape(REQ, HD, HD),
            shape(REQ, HD, HD),
            shape(REQ, seats),
            shape(REQ, seats),
            shape(REQ, HD, dtype=F32),
            shape(REQ, HD, dtype=F32),
            shape(REQ, HD, dtype=F32),
        ],
        [VMEM] * 4 + [ANY] * 2,
        1 << 22,
        1 << 23,
        [pltpu.SemaphoreType.DMA((2,))],
    )(lengths, offload, host_instance, cache_slot, key_cache, value_cache)
    got = lax.all_to_all(message, ("pool", "inst"), 0, 0, tiled=True)
    message = call(
        functools.partial(attend_kernel, width=width), shape(POOLS * INSTS * CORES, REQ, HD), [VMEM] * 7, 1 << 26, 1 << 22
    )(got, keys, values, pick, cos, sin, span)
    got = lax.all_to_all(message, ("pool", "inst", "core"), 0, 0, tiled=True)
    message = call(output_kernel, shape(RING, REQ, HD), [VMEM] * 4, 1 << 25, 1 << 22)(
        got.reshape(POOLS * INSTS, CORES, REQ, HD), back, output_weight, buddy_weight
    )
    got = ring_exchange(message)
    return call(sum_kernel, shape(1, REQ, HD), [VMEM], 1 << 17, 1 << 18)(got)


def solution(mesh):
    finer = Mesh(mesh.devices.reshape(SIZES), AXES)
    in_specs = (
        P("inst", None, ("pool",) + TP),
        P(("pool",) + TP),
        P(None, TP),
        P(("pool",) + TP, None),
        P(("pool",) + TP, None),
        P(TP, None),
        P("pool", "inst", None, None, None),
        P("pool", "inst", None, None, None),
        P(),
        P(),
        P(),
        P(),
    )
    out_specs = P("inst", None, ("pool",) + TP)
    return jax.shard_map(shards, mesh=finer, in_specs=in_specs, out_specs=out_specs, check_vma=False)
```

time: 81.9 us -> 78.8 us (0.962)
  waiting for transfers between devices: 14.1 us -> 2.25 us
  blocking collectives: 43.2 us -> 53.5 us
  local copies, waits for them, and re-layouts: 2.91 us -> 11.5 us
  matrix products: 6.45 us -> 0 us
  Pallas kernels: 0 us -> 5.62 us
  other arithmetic: 4.74 us -> 0 us
  starting transfers between devices: 9.46 us -> 4.84 us
    unnamed x15 -> x28, local copies, waits for them, and re-layouts: 0.13 us -> 11.5 us
    all_to_all x2 -> x3, blocking collectives: 43.2 us -> 53.5 us  [the longest x2 43.6 us: ring_exchange(): return lax.all_to_all(x, AXES, 0, 0, axis_index_groups=RINGS, tiled=True)]
    dot_general x7 -> x0, matrix products: 6.45 us -> none  [the longest x1 1.85 us: shards(): jnp.einsum('rd,rpd->rp', q, keys, preferred_element_type=F32) * factor]
    pallas_call x0 -> x6, Pallas kernels: none -> 5.62 us  [the longest x1 2.12 us: shards(): call(output_kernel, shape(RING, REQ, HD), [VMEM] * 4, 1 << 25, 1 << 22)]
    all_to_all x1, waiting for transfers between devices: 5.94 us -> 0.44 us  [shards(): got = lax.all_to_all(message, ('pool', 'inst'), 0, 0, tiled=True)]
    all_to_all x1 -> x0, waiting for transfers between devices: 5.09 us -> none  [shards(): lax.all_to_all(jnp.broadcast_to(mixed[None], (8, rows, HD)), ('pool', 'in...]
    all_to_all x1 -> x0, starting transfers between devices: 4.42 us -> none  [shards(): lax.all_to_all(jnp.broadcast_to(mixed[None], (8, rows, HD)), ('pool', 'in...]
    reduce_sum x6 -> x0, other arithmetic: 2.26 us -> none  [the longest x1 0.95 us: shards(): squares = jnp.sum(x * x, axis=1)]
  transfers between devices with their start and end apart: 4 -> 3, of which waited for: 4 -> 2; matrix products, arithmetic and copies ran while one was open for 1% -> 0% of each run, Pallas kernels for 0% -> 4%
where the time goes in v2:
time: 78.8 us; the launch traced here: 77.8 us
  blocking collectives  53.5 us (68%)
  local copies, waits for them, and re-layouts  11.5 us (15%)
  Pallas kernels  5.62 us (7%)
  starting transfers between devices  4.84 us (6%)
  waiting for transfers between devices  2.25 us (3%)
    all_to_all x2, blocking collectives, ring_exchange(): return lax.all_to_all(x, AXES, 0, 0, axis_index_groups=RINGS, tiled=True)  43.6 us
    unnamed x28, local copies, waits for them, and re-layouts  11.5 us
    all_to_all x1, blocking collectives, shards(): got = lax.all_to_all(message, ('pool', 'inst', 'core'), 0, 0, tiled=True)  9.87 us
    all_to_all x1, starting transfers between devices, shards(): got = lax.all_to_all(message, ('pool', 'inst'), 0, 0, tiled=True)  4.83 us
    pallas_call x1, Pallas kernels, shards(): call(output_kernel, shape(RING, REQ, HD), [VMEM] * 4, 1 << 25, 1 << 22)  2.12 us
    ppermute x2, waiting for transfers between devices, swap_core(): return lax.ppermute(x, 'core', [(0, 1), (1, 0)])  1.82 us
  transfers between devices with their start and end apart: 3, of which 2 were waited for; matrix products, arithmetic and copies ran while one was open for 0% of the time, Pallas kernels for 4%

profile of v2, /device:TPU:2, one launch (start us, length us, event | category | flops | bytes accessed | tf_op | source)
XLA Modules:
  0.0 77.8 jit_solution(12374688203533637762)
XLA Ops:
  0.0 0.0 collective-permute-start.1
  0.0 0.0 copy-start.6
  0.0 0.9 %copy-done.6 = bf16[128,512]{1,0:T(8,128)(2,1)S(1)} copy-done((bf16[128,512]{1,0:T(8,128)(2,1)S(1)}, bf16[128,512]{1,0:T(8,128)(2,1)}, u32[]{:S(2)}) %copy-start.6) | copy-done | bytes 131096
  0.9 0.0 copy-start.7
  0.9 0.9 %copy-done.7 = bf16[128,512]{1,0:T(8,128)(2,1)S(1)} copy-done((bf16[128,512]{1,0:T(8,128)(2,1)S(1)}, bf16[128,512]{1,0:T(8,128)(2,1)}, u32[]{:S(2)}) %copy-start.7) | copy-done | bytes 131096
  1.8 0.0 copy-start.8
  1.8 0.7 copy-done.8
  2.5 0.0 copy-start.13
  2.5 0.7 copy-done.13
  3.2 0.2 shard_map.118
  3.3 0.0 copy-start.9
  3.4 0.0 copy-start.10
  3.4 0.0 copy-start.11
  3.4 0.0 copy-start.12
  3.4 29.3 %all_to_all.20.own_ref = bf16[16,112,128]{2,1,0:T(8,128)(2,1)S(1)} all-to-all(bf16[16,112,128]{2,1,0:T(8,128)(2,1)S(1)} %shard_map.118), channel_id=1, replica_groups={{0,130,4,134,8,138,12,142,16,146,20,150,24,154,28,158},{1,131,5,135,9,1..., dimensions={0} | all-to-all | bytes 917504 | tf_op jit(solution)/shard_map/all_to_all | solution.py:41
  32.7 0.0 collective-permute-start
  32.7 1.8 %collective-permute-done.other_ref = bf16[16,112,128]{2,1,0:T(8,128)(2,1)S(1)} collective-permute-done((bf16[16,112,128]{2,1,0:T(8,128)(2,1)S(1)}, bf16[16,112,128]{2,1,0:T(8,128)(2,1)S(1)}, u32[]{:S(2)}, u32[]{:S(2)}) %collective-permute-start) | collective-permute-done | bytes 458784 | tf_op jit(solution)/shard_map/ppermute | solution.py:45
  34.5 0.0 copy-start.2
  34.5 1.6 %copy-done.2 = bf16[8192,128]{1,0:T(8,128)(2,1)S(1)} copy-done((bf16[8192,128]{1,0:T(8,128)(2,1)S(1)}, bf16[8192,128]{1,0:T(8,128)(2,1)}, u32[]{:S(2)}) %copy-start.2) | copy-done | bytes 2097176
  36.1 1.0 %shard_map.119 = bf16[8,32,512]{2,1,0:T(8,128)(2,1)} custom-call(bf16[16,112,128]{2,1,0:T(8,128)(2,1)S(1)} %all_to_all.20.own_ref, bf16[16,112,128]{2,1,0:T(8,128)(2,1)S(1)} %collective-permute-done.other_ref, bf16[2,8,2,2,128,128]{5,4,3,2,1,0:T(8,128)(2,1)S(1)} %bitcast.3), custom_call_target="tpu_custom_call" | custom-call | flops 33554432 | bytes 4194304 | tf_op jit(solution)/shard_map/pallas_call | solution.py:252
  37.1 4.8 %all-to-all-start.1 = ((bf16[8,32,512]{2,1,0:T(8,128)(2,1)}), bf16[8,32,512]{2,1,0:T(8,128)(2,1)S(1)}, u32[]{:S(2)}, u32[]{:S(2)}) async-start(bf16[8,32,512]{2,1,0:T(8,128)(2,1)} %shard_map.119), calls=%async_computation.1 | async-start | bytes 524288 | tf_op jit(solution)/shard_map/all_to_all | solution.py:271
  41.9 0.0 copy-done.9
  41.9 0.0 copy-done.10
  42.0 0.0 copy-done.11
  42.0 0.0 copy-done.12
  42.0 0.0 copy-start
  42.0 2.2 %copy-done = bf16[1,1,32,128,512]{4,3,2,1,0:T(8,128)(2,1)S(1)} copy-done((bf16[1,1,32,128,512]{4,3,2,1,0:T(8,128)(2,1)S(1)}, bf16[1,1,32,128,512]{4,3,2,1,0:T(8,128)(2,1)}, u32[]{:S(2)}) %copy-start) | copy-done | bytes 4194328
  44.2 0.0 copy-start.1
  44.2 2.2 %copy-done.1 = bf16[1,1,32,128,512]{4,3,2,1,0:T(8,128)(2,1)S(1)} copy-done((bf16[1,1,32,128,512]{4,3,2,1,0:T(8,128)(2,1)S(1)}, bf16[1,1,32,128,512]{4,3,2,1,0:T(8,128)(2,1)}, u32[]{:S(2)}) %copy-start.1) | copy-done | bytes 4194328
  46.4 0.6 shard_map.120
  46.9 0.0 copy-start.4
  46.9 1.0 %copy-done.4 = bf16[32,128,128]{2,1,0:T(8,128)(2,1)} copy-done((bf16[32,128,128]{2,1,0:T(8,128)(2,1)}, bf16[32,128,128]{2,1,0:T(8,128)(2,1)S(1)}, u32[]{:S(2)}) %copy-start.4) | copy-done | bytes 1048600
  47.9 0.0 copy-start.3
  47.9 0.4 all-to-all-done.1.got_ref
  48.4 0.0 copy-start.5
  48.4 1.4 %copy-done.5 = bf16[32,128,128]{2,1,0:T(8,128)(2,1)S(1)} copy-done((bf16[32,128,128]{2,1,0:T(8,128)(2,1)S(1)}, bf16[32,128,128]{2,1,0:T(8,128)(2,1)}, u32[]{:S(2)}) %copy-start.5) | copy-done | bytes 1048600
  49.8 1.1 %shard_map.121 = bf16[16,32,128]{2,1,0:T(8,128)(2,1)S(1)} custom-call(bf16[8,32,512]{2,1,0:T(8,128)(2,1)S(1)} %all-to-all-done.1.got_ref, bf16[32,128,128]{2,1,0:T(8,128)(2,1)S(1)} %get-tuple-element.12.keys_ref, bf16[32,128,128]{2,1,0:T(8,128)(2,1)S(1)} %copy-done.5, bf16[32,256]{1,0:T(8,128)(2,1)S(1)} %get-tuple-element.14.pick_ref, ...), custom_call_target="tpu_custom_call" | custom-call | flops 67108864 | bytes 4194304 | tf_op jit(solution)/shard_map/pallas_call | solution.py:272
  50.9 9.9 %all_to_all.21 = bf16[16,32,128]{2,1,0:T(8,128)(2,1)S(1)} all-to-all(bf16[16,32,128]{2,1,0:T(8,128)(2,1)S(1)} %shard_map.121), channel_id=1, replica_groups=mesh['pool'=2,'inst'=4,'z'=8,'yh'=2,'core'=2] {'pool','inst','core'}, dimensions={0} | all-to-all | bytes 262144 | tf_op jit(solution)/shard_map/all_to_all | solution.py:275
  60.8 0.0 collective-permute-done.1.other_ref
  60.8 0.0 copy-done.3
  60.8 2.1 %shard_map.122 = bf16[16,32,128]{2,1,0:T(8,128)(2,1)S(1)} custom-call(bf16[8,2,32,128]{3,2,1,0:T(8,128)(2,1)S(1)} %bitcast.4, bf16[32,256]{1,0:T(8,128)(2,1)S(1)} %get-tuple-element.18.back_ref, bf16[128,8192]{1,0:T(8,128)(2,1)S(1)} %copy-done.3, bf16[128,8192]{1,0:T(8,128)(2,1)} %collective-permute-done.1.other_ref), custom_call_target="tpu_custom_call" | custom-call | flops 33554432 | bytes 4194304 | tf_op jit(solution)/shard_map/pallas_call | solution.py:276
  62.9 14.3 %all_to_all.22.got_ref = bf16[16,32,128]{2,1,0:T(8,128)(2,1)S(1)} all-to-all(bf16[16,32,128]{2,1,0:T(8,128)(2,1)S(1)} %shard_map.122), channel_id=1, replica_groups={{0,130,4,134,8,138,12,142,16,146,20,150,24,154,28,158},{1,131,5,135,9,1..., dimensions={0} | all-to-all | bytes 262144 | tf_op jit(solution)/shard_map/all_to_all | solution.py:41
  77.2 0.6 shard_map.123
Async XLA Ops:
  0.0 60.8 %collective-permute-start.1 = (bf16[128,8192]{1,0:T(8,128)(2,1)}, bf16[128,8192]{1,0:T(8,128)(2,1)}, u32[]{:S(2)}, u32[]{:S(2)}) collective-permute-start(bf16[128,8192]{1,0:T(8,128)(2,1)} %own_ref.1), channel_id=1, source_target_pairs={{0,1},{1,0},{2,3},{3,2},{4,5},{5,4},{6,7},{7,6},{8,9},{9,8},{10,11... | collective-permute-start | bytes 6291464 | tf_op jit(solution)/shard_map/ppermute | solution.py:45
  0.0 0.9 %copy-start.6 = (bf16[128,512]{1,0:T(8,128)(2,1)S(1)}, bf16[128,512]{1,0:T(8,128)(2,1)}, u32[]{:S(2)}) copy-start(bf16[128,512]{1,0:T(8,128)(2,1)} %wk_ref.1) | copy-start | bytes 393220
  0.9 0.9 %copy-start.7 = (bf16[128,512]{1,0:T(8,128)(2,1)S(1)}, bf16[128,512]{1,0:T(8,128)(2,1)}, u32[]{:S(2)}) copy-start(bf16[128,512]{1,0:T(8,128)(2,1)} %wv_ref.1) | copy-start | bytes 393220
  1.8 0.7 copy-start.8
  2.5 0.7 copy-start.13
  3.3 38.6 %copy-start.9 = (s32[4,32]{1,0:T(4,128)S(1)}, s32[4,32]{1,0:T(4,128)}, u32[]{:S(2)}) copy-start(s32[4,32]{1,0:T(4,128)} %lengths_ref.1) | copy-start | bytes 1540
  3.4 38.6 %copy-start.10 = (s32[4,32]{1,0:T(4,128)S(1)}, s32[4,32]{1,0:T(4,128)}, u32[]{:S(2)}) copy-start(s32[4,32]{1,0:T(4,128)} %offload_ref.1) | copy-start | bytes 1540
  3.4 38.6 %copy-start.11 = (s32[4,32]{1,0:T(4,128)S(1)}, s32[4,32]{1,0:T(4,128)}, u32[]{:S(2)}) copy-start(s32[4,32]{1,0:T(4,128)} %host_ref.1) | copy-start | bytes 1540
  3.4 38.6 %copy-start.12 = (s32[4,32]{1,0:T(4,128)S(1)}, s32[4,32]{1,0:T(4,128)}, u32[]{:S(2)}) copy-start(s32[4,32]{1,0:T(4,128)} %slot_ref.1) | copy-start | bytes 1540
  32.7 1.8 %collective-permute-start = (bf16[16,112,128]{2,1,0:T(8,128)(2,1)S(1)}, bf16[16,112,128]{2,1,0:T(8,128)(2,1)S(1)}, u32[]{:S(2)}, u32[]{:S(2)}) collective-permute-start(bf16[16,112,128]{2,1,0:T(8,128)(2,1)S(1)} %all_to_all.20.own_ref), channel_id=1, source_target_pairs={{0,1},{1,0},{2,3},{3,2},{4,5},{5,4},{6,7},{7,6},{8,9},{9,8},{10,11... | collective-permute-start | bytes 1376264 | tf_op jit(solution)/shard_map/ppermute | solution.py:45
  34.5 1.6 %copy-start.2 = (bf16[8192,128]{1,0:T(8,128)(2,1)S(1)}, bf16[8192,128]{1,0:T(8,128)(2,1)}, u32[]{:S(2)}) copy-start(bf16[8192,128]{1,0:T(8,128)(2,1)} %param.14) | copy-start | bytes 6291460
  37.1 11.2 %all-to-all-start.1 = ((bf16[8,32,512]{2,1,0:T(8,128)(2,1)}), bf16[8,32,512]{2,1,0:T(8,128)(2,1)S(1)}, u32[]{:S(2)}, u32[]{:S(2)}) async-start(bf16[8,32,512]{2,1,0:T(8,128)(2,1)} %shard_map.119), calls=%async_computation.1 | async-start | bytes 524288 | tf_op jit(solution)/shard_map/all_to_all | solution.py:271
  42.0 2.2 %copy-start = (bf16[1,1,32,128,512]{4,3,2,1,0:T(8,128)(2,1)S(1)}, bf16[1,1,32,128,512]{4,3,2,1,0:T(8,128)(2,1)}, u32[]{:S(2)}) copy-start(bf16[1,1,32,128,512]{4,3,2,1,0:T(8,128)(2,1)} %keys_ref.1) | copy-start | bytes 12582916
  44.2 2.2 %copy-start.1 = (bf16[1,1,32,128,512]{4,3,2,1,0:T(8,128)(2,1)S(1)}, bf16[1,1,32,128,512]{4,3,2,1,0:T(8,128)(2,1)}, u32[]{:S(2)}) copy-start(bf16[1,1,32,128,512]{4,3,2,1,0:T(8,128)(2,1)} %values_ref.1) | copy-start | bytes 12582916
  46.9 1.0 %copy-start.4 = (bf16[32,128,128]{2,1,0:T(8,128)(2,1)}, bf16[32,128,128]{2,1,0:T(8,128)(2,1)S(1)}, u32[]{:S(2)}) copy-start(bf16[32,128,128]{2,1,0:T(8,128)(2,1)S(1)} %get-tuple-element.13.values_ref) | copy-start | bytes 3145732
  47.9 12.9 %copy-start.3 = (bf16[128,8192]{1,0:T(8,128)(2,1)S(1)}, bf16[128,8192]{1,0:T(8,128)(2,1)}, u32[]{:S(2)}) copy-start(bf16[128,8192]{1,0:T(8,128)(2,1)} %own_ref.1) | copy-start | bytes 6291460
  48.4 1.4 %copy-start.5 = (bf16[32,128,128]{2,1,0:T(8,128)(2,1)S(1)}, bf16[32,128,128]{2,1,0:T(8,128)(2,1)}, u32[]{:S(2)}) copy-start(bf16[32,128,128]{2,1,0:T(8,128)(2,1)} %copy-done.4) | copy-start | bytes 3145732

commit v3 on v2

--- a/solution.py
+++ b/solution.py
@@ -22,7 +22,7 @@
 F32 = jnp.float32
 I32 = jnp.int32
 VMEM = pl.BlockSpec(memory_space=pltpu.VMEM)
-ANY = pl.BlockSpec(memory_space=pl.ANY)
+HBM = pl.BlockSpec(memory_space=pltpu.HBM)
 
 
 def device_number(p, i, z, y, c):
@@ -58,7 +58,21 @@
     return high, (x - high.astype(F32)).astype(BF)
 
 
-def features_kernel(x_ref, gain_ref, wk_ref, wv_ref, out_ref):
+def start_copies(pairs, sems):
+    copies = [pltpu.make_async_copy(a, b, sems.at[n]) for n, (a, b) in enumerate(pairs)]
+    for copy in copies:
+        copy.start()
+    return copies
+
+
+def head_lanes(z):
+    return pl.ds(pl.multiple_of((z // (ZS // HEADS)) * HD, HD), HD)
+
+
+def features_kernel(x_hbm, gain_hbm, wk_hbm, wv_hbm, out_ref, x_ref, gain_ref, wk_ref, wv_ref, sems):
+    pairs = ((x_hbm, x_ref), (gain_hbm, gain_ref), (wk_hbm, wk_ref), (wv_hbm, wv_ref))
+    for copy in start_copies(pairs, sems):
+        copy.wait()
     x = x_ref[0].astype(F32)
     scaled = (x * gain_ref[...].astype(F32)).astype(BF)
     squares = jnp.sum(x * x, axis=1, keepdims=True)
@@ -70,49 +84,31 @@
     k = dot(scaled, wk_ref[...]).astype(BF)
     v = dot(scaled, wv_ref[...]).astype(BF)
     for m in range(RING):
-        head = slice((m // POOLS) // (ZS // HEADS) * HD, ((m // POOLS) // (ZS // HEADS) + 1) * HD)
+        n = (m // POOLS) // (ZS // HEADS)
+        head = slice(n * HD, (n + 1) * HD)
         out_ref[m, 0:REQ, :] = scaled
         out_ref[m, REQ : 2 * REQ, :] = k[:, head]
         out_ref[m, 2 * REQ : 3 * REQ, :] = v[:, head]
         out_ref[m, 3 * REQ :, :] = extra
 
 
-def query_kernel(own_ref, other_ref, wq_ref, out_ref):
-    pool, yh, core = lax.axis_index("pool"), lax.axis_index("yh"), lax.axis_index("core")
-    side = pool ^ yh
-    q = jnp.zeros((REQ, HD), F32)
-    sums = jnp.zeros((2 * REQ, HD), F32)
-    extra = jnp.zeros((16, HD), F32)
-    for m in range(RING):
-        z, p = m // POOLS, m % POOLS
-        y = p ^ side
-        features = jnp.concatenate([own_ref[m, 0:REQ, :], other_ref[m, 0:REQ, :]], axis=1)
-        weight = jnp.concatenate([wq_ref[p, z, y, core], wq_ref[p, z, y, 1 - core]], axis=0)
-        q += dot(features, weight)
-        sums += own_ref[m, REQ : 3 * REQ, :].astype(F32) + other_ref[m, REQ : 3 * REQ, :].astype(F32)
-        extra += own_ref[m, 3 * REQ :, :].astype(F32) + other_ref[m, 3 * REQ :, :].astype(F32)
-    row = extra[0:1] + extra[1:2]
-    eye = iota((REQ, HD), 0) == iota((REQ, HD), 1)
-    squares = jnp.sum(jnp.where(eye, row, 0.0), axis=1, keepdims=True)
-    high = squares.astype(BF).astype(F32)
-    tail = jnp.where(iota((REQ, HD), 1) < HD // 2, high, squares - high)
-    message = jnp.concatenate([q, sums[:REQ], sums[REQ:], tail], axis=1).astype(BF)
-    for m in range(POOLS * INSTS):
-        out_ref[m] = message
-
-
-def tables_kernel(
-    lengths_ref, offload_ref, host_ref, slot_ref, keys_ref, values_ref,
-    keys_out, values_out, pick_ref, back_ref, cos_ref, sin_ref, span_ref, sems,
+def early_kernel(
+    lengths_hbm, offload_hbm, host_hbm, slot_hbm, keys_hbm, wq_hbm,
+    keys_out, wq_out, pick_ref, back_ref, cos_ref, sin_ref, span_ref,
+    lengths_ref, offload_ref, host_ref, slot_ref, sems,
 ):
     pool, inst, z = lax.axis_index("pool"), lax.axis_index("inst"), lax.axis_index("z")
-    lane = pl.ds(pl.multiple_of((z // (ZS // HEADS)) * HD, HD), HD)
-    copies = [
-        pltpu.make_async_copy(keys_ref.at[0, 0, :, :, lane], keys_out, sems.at[0]),
-        pltpu.make_async_copy(values_ref.at[0, 0, :, :, lane], values_out, sems.at[1]),
-    ]
-    for copy in copies:
-        copy.start()
+    core = lax.axis_index("core")
+    side = pool ^ lax.axis_index("yh")
+    pairs = [(lengths_hbm, lengths_ref), (offload_hbm, offload_ref), (host_hbm, host_ref), (slot_hbm, slot_ref)]
+    small = len(pairs)
+    for p in range(POOLS):
+        for n, c in enumerate((core, 1 - core)):
+            pairs.append((wq_hbm.at[p, :, p ^ side, c], wq_out.at[:, p, pl.ds(n * HD, HD), :]))
+    pairs.append((keys_hbm.at[0, 0, :, :, head_lanes(z)], keys_out))
+    copies = start_copies(pairs, sems)
+    for copy in copies[:small]:
+        copy.wait()
     home = iota((INSTS, REQ), 0) * REQ + iota((INSTS, REQ), 1)
     away = INSTS * REQ + host_ref[...] * REQ + slot_ref[...]
     seat = jnp.where(offload_ref[...] == 1, away, home)
@@ -140,8 +136,41 @@
     cos_ref[...] = jnp.cos(angles)
     sin_ref[...] = jnp.where(lanes < half, -jnp.sin(angles), jnp.sin(angles))
     span_ref[...] = jnp.broadcast_to(span, (REQ, HD))
-    for copy in copies:
+    for copy in copies[small:]:
         copy.wait()
+
+
+def late_kernel(values_hbm, own_hbm, other_hbm, values_out, own_out, other_out, sems):
+    core = lax.axis_index("core")
+    side = lax.axis_index("pool") ^ lax.axis_index("yh")
+    pairs = [(values_hbm.at[0, 0, :, :, head_lanes(lax.axis_index("z"))], values_out)]
+    for source, out in ((own_hbm, own_out), (other_hbm, other_out)):
+        for m in range(RING):
+            z, p = m // POOLS, m % POOLS
+            block = ((p * ZS + z) * YS + (p ^ side)) * CORES + core
+            lanes = pl.ds(pl.multiple_of(block * HD, HD), HD)
+            pairs.append((source.at[:, lanes], out.at[:, pl.ds(m * HD, HD)]))
+    for copy in start_copies(pairs, sems):
+        copy.wait()
+
+
+def query_kernel(own_ref, other_ref, wq_ref, out_ref):
+    q = jnp.zeros((REQ, HD), F32)
+    sums = jnp.zeros((2 * REQ, HD), F32)
+    extra = jnp.zeros((16, HD), F32)
+    for m in range(RING):
+        features = jnp.concatenate([own_ref[m, 0:REQ, :], other_ref[m, 0:REQ, :]], axis=1)
+        q += dot(features, wq_ref[m // POOLS, m % POOLS])
+        sums += own_ref[m, REQ : 3 * REQ, :].astype(F32) + other_ref[m, REQ : 3 * REQ, :].astype(F32)
+        extra += own_ref[m, 3 * REQ :, :].astype(F32) + other_ref[m, 3 * REQ :, :].astype(F32)
+    row = extra[0:1] + extra[1:2]
+    eye = iota((REQ, HD), 0) == iota((REQ, HD), 1)
+    squares = jnp.sum(jnp.where(eye, row, 0.0), axis=1, keepdims=True)
+    high = squares.astype(BF).astype(F32)
+    tail = jnp.where(iota((REQ, HD), 1) < HD // 2, high, squares - high)
+    message = jnp.concatenate([q, sums[:REQ], sums[REQ:], tail], axis=1).astype(BF)
+    for m in range(POOLS * INSTS):
+        out_ref[m] = message
 
 
 def attend_kernel(got_ref, keys_ref, values_ref, pick_ref, cos_ref, sin_ref, span_ref, out_ref, *, width):
@@ -187,19 +216,14 @@
 
 
 def output_kernel(got_ref, back_ref, own_ref, other_ref, out_ref):
-    pool, yh, core = lax.axis_index("pool"), lax.axis_index("yh"), lax.axis_index("core")
-    side = pool ^ yh
+    core = lax.axis_index("core")
     back = back_ref[...]
     seats = POOLS * INSTS * REQ
     mine = dot(back, got_ref[:, core].reshape(seats, HD)).astype(BF)
     buddy = dot(back, got_ref[:, 1 - core].reshape(seats, HD)).astype(BF)
-    rows = jnp.concatenate([mine, buddy], axis=1)
+    result = (dot(mine, own_ref[...]) + dot(buddy, other_ref[...])).astype(BF)
     for m in range(RING):
-        z, p = m // POOLS, m % POOLS
-        block = ((p * ZS + z) * YS + (p ^ side)) * CORES + core
-        lane = pl.ds(pl.multiple_of(block * HD, HD), HD)
-        weight = jnp.concatenate([own_ref[:, lane], other_ref[:, lane]], axis=0)
-        out_ref[m] = dot(rows, weight).astype(BF)
+        out_ref[m] = result[:, m * HD : (m + 1) * HD]
 
 
 def sum_kernel(got_ref, out_ref):
@@ -207,6 +231,10 @@
     for m in range(1, RING):
         total += got_ref[m].astype(F32)
     out_ref[0] = total.astype(BF)
+
+
+def in_hbm(*arrays):
+    return [pltpu.with_memory_space_constraint(a, pltpu.HBM) for a in arrays]
 
 
 def call(kernel, shapes, specs, flops, moved, scratch=(), limit=24):
@@ -243,38 +271,69 @@
     width = query_weight.shape[0]
     seats = POOLS * INSTS * REQ
 
-    message = call(features_kernel, shape(RING, 3 * REQ + 16, HD), [VMEM] * 4, 1 << 23, 1 << 20)(
-        hidden_states, norm_gain.reshape(1, HD), key_weight, value_weight
-    )
     buddy_weight = swap_core(output_weight)
+    message = call(
+        features_kernel,
+        shape(RING, 3 * REQ + 16, HD),
+        [HBM] * 4,
+        1 << 23,
+        1 << 20,
+        [
+            pltpu.VMEM((1, REQ, HD), BF),
+            pltpu.VMEM((1, HD), BF),
+            pltpu.VMEM(key_weight.shape, BF),
+            pltpu.VMEM(value_weight.shape, BF),
+            pltpu.SemaphoreType.DMA((4,)),
+        ],
+    )(*in_hbm(hidden_states, norm_gain.reshape(1, HD), key_weight, value_weight))
+    message, lengths = lax.optimization_barrier((message, lengths))
     got = ring_exchange(message)
-    other = swap_core(got)
-    message = call(query_kernel, shape(POOLS * INSTS, REQ, 4 * HD), [VMEM] * 3, 1 << 25, 1 << 22)(
-        got, other, query_weight.reshape(POOLS, ZS, YS, CORES, HD, HD)
-    )
-    keys, values, pick, back, cos, sin, span = call(
-        tables_kernel,
+    table = pltpu.VMEM(lengths.shape, I32)
+    early = call(
+        early_kernel,
         [
             shape(REQ, HD, HD),
-            shape(REQ, HD, HD),
+            shape(ZS, POOLS, CORES * HD, HD),
             shape(REQ, seats),
             shape(REQ, seats),
             shape(REQ, HD, dtype=F32),
             shape(REQ, HD, dtype=F32),
             shape(REQ, HD, dtype=F32),
         ],
-        [VMEM] * 4 + [ANY] * 2,
+        [HBM] * 6,
         1 << 22,
-        1 << 23,
-        [pltpu.SemaphoreType.DMA((2,))],
-    )(lengths, offload, host_instance, cache_slot, key_cache, value_cache)
+        1 << 22,
+        [table] * 4 + [pltpu.SemaphoreType.DMA((4 + 2 * POOLS + 1,))],
+    )(
+        *in_hbm(
+            lengths,
+            offload,
+            host_instance,
+            cache_slot,
+            key_cache,
+            query_weight.reshape(POOLS, ZS, YS, CORES, HD, HD),
+        )
+    )
+    got, early, value_cache = lax.optimization_barrier((got, early, value_cache))
+    keys, wq, pick, back, cos, sin, span = early
+    other = swap_core(got)
+    late = call(
+        late_kernel,
+        [shape(REQ, HD, HD), shape(HD, RING * HD), shape(HD, RING * HD)],
+        [HBM] * 3,
+        0,
+        1 << 22,
+        [pltpu.SemaphoreType.DMA((1 + 2 * RING,))],
+    )(*in_hbm(value_cache, output_weight, buddy_weight))
+    other, (values, keep, taken) = lax.optimization_barrier((other, late))
+    message = call(query_kernel, shape(POOLS * INSTS, REQ, 4 * HD), [VMEM] * 3, 1 << 25, 1 << 22)(got, other, wq)
     got = lax.all_to_all(message, ("pool", "inst"), 0, 0, tiled=True)
     message = call(
         functools.partial(attend_kernel, width=width), shape(POOLS * INSTS * CORES, REQ, HD), [VMEM] * 7, 1 << 26, 1 << 22
     )(got, keys, values, pick, cos, sin, span)
     got = lax.all_to_all(message, ("pool", "inst", "core"), 0, 0, tiled=True)
     message = call(output_kernel, shape(RING, REQ, HD), [VMEM] * 4, 1 << 25, 1 << 22)(
-        got.reshape(POOLS * INSTS, CORES, REQ, HD), back, output_weight, buddy_weight
+        got.reshape(POOLS * INSTS, CORES, REQ, HD), back, keep, taken
     )
     got = ring_exchange(message)
     return call(sum_kernel, shape(1, REQ, HD), [VMEM], 1 << 17, 1 << 18)(got)

time: 78.8 us -> 70.7 us (0.90)
  blocking collectives: 53.5 us -> 34.2 us
  waiting for transfers between devices: 2.25 us -> 16.7 us
  local copies, waits for them, and re-layouts: 11.5 us -> 0 us
  starting transfers between devices: 4.84 us -> 11 us
  Pallas kernels: 5.62 us -> 7.84 us
    all_to_all x2 -> x1, blocking collectives: 43.6 us -> 14.3 us  [ring_exchange(): return lax.all_to_all(x, AXES, 0, 0, axis_index_groups=RINGS, tiled=True)]
    all_to_all x1, waiting for transfers between devices: 0.44 us -> 16.6 us  [ring_exchange(): return lax.all_to_all(x, AXES, 0, 0, axis_index_groups=RINGS, tiled=True)]
    unnamed x28 -> x0, local copies, waits for them, and re-layouts: 11.5 us -> none
    all_to_all x0 -> x1, blocking collectives: none -> 11.4 us  [shards(): got = lax.all_to_all(message, ('pool', 'inst'), 0, 0, tiled=True)]
    all_to_all x1, starting transfers between devices: 4.83 us -> 11 us  [ring_exchange(): return lax.all_to_all(x, AXES, 0, 0, axis_index_groups=RINGS, tiled=True)]
    pallas_call x2 -> x3, Pallas kernels: 0.74 us -> 5.41 us  [the longest x1 1.97 us: shards(): call(features_kernel, shape(RING, 3 * REQ + 16, HD), [HBM] * 4, 1 << 23,...]
    ppermute x2, waiting for transfers between devices: 1.82 us -> 0.06 us  [swap_core(): return lax.ppermute(x, 'core', [(0, 1), (1, 0)])]
    pallas_call x1, Pallas kernels: 2.12 us -> 0.39 us  [shards(): call(output_kernel, shape(RING, REQ, HD), [VMEM] * 4, 1 << 25, 1 << 22)]
  transfers between devices with their start and end apart: 3 -> 3, of which waited for: 2 -> 2; matrix products, arithmetic and copies ran while one was open for 0% -> 0% of each run, Pallas kernels for 4% -> 8%
where the time goes in v3:
time: 70.7 us; the launch traced here: 69.8 us
  blocking collectives  34.2 us (48%)
  waiting for transfers between devices  16.7 us (24%)
  starting transfers between devices  11 us (16%)
  Pallas kernels  7.84 us (11%)
    all_to_all x1, waiting for transfers between devices, ring_exchange(): return lax.all_to_all(x, AXES, 0, 0, axis_index_groups=RINGS, tiled=True)  16.6 us
    all_to_all x1, blocking collectives, ring_exchange(): return lax.all_to_all(x, AXES, 0, 0, axis_index_groups=RINGS, tiled=True)  14.3 us
    all_to_all x1, blocking collectives, shards(): got = lax.all_to_all(message, ('pool', 'inst'), 0, 0, tiled=True)  11.4 us
    all_to_all x1, starting transfers between devices, ring_exchange(): return lax.all_to_all(x, AXES, 0, 0, axis_index_groups=RINGS, tiled=True)  11 us
    all_to_all x1, blocking collectives, shards(): got = lax.all_to_all(message, ('pool', 'inst', 'core'), 0, 0, tiled=True)  8.54 us
    pallas_call x1, Pallas kernels, shards(): call(features_kernel, shape(RING, 3 * REQ + 16, HD), [HBM] * 4, 1 << 23,...  1.97 us
    pallas_call x1, Pallas kernels, shards(): call(late_kernel, [shape(REQ, HD, HD), shape(HD, RING * HD), shape(HD, RI...  1.75 us
    pallas_call x1, Pallas kernels, shards(): call(early_kernel, [shape(REQ, HD, HD), shape(ZS, POOLS, CORES * HD, HD),...  1.69 us
  transfers between devices with their start and end apart: 3, of which 2 were waited for; matrix products, arithmetic and copies ran while one was open for 0% of the time, Pallas kernels for 8%

profile of v3, /device:TPU:2, one launch (start us, length us, event | category | flops | bytes accessed | tf_op | source)
XLA Modules:
  0.0 69.8 jit_solution(15371705586292469065)
XLA Ops:
  0.0 0.0 collective-permute-start.1
  0.0 2.0 %shard_map.118 = bf16[16,112,128]{2,1,0:T(8,128)(2,1)} custom-call(bf16[1,32,128]{2,1,0:T(8,128)(2,1)} %x_hbm.1, bf16[1,128]{1,0:T(2,128)(2,1)} %bitcast.5, bf16[128,512]{1,0:T(8,128)(2,1)} %wk_hbm.1, bf16[128,512]{1,0:T(8,128)(2,1)} %wv_hbm.1), custom_call_target="tpu_custom_call" | custom-call | flops 8388608 | bytes 1048576 | tf_op jit(solution)/shard_map/pallas_call | solution.py:275
  2.0 11.0 %all-to-all-start = ((bf16[16,112,128]{2,1,0:T(8,128)(2,1)}), bf16[16,112,128]{2,1,0:T(8,128)(2,1)S(1)}, u32[]{:S(2)}, u32[]{:S(2)}) async-start(bf16[16,112,128]{2,1,0:T(8,128)(2,1)} %shard_map.118), calls=%async_computation | async-start | bytes 917504 | tf_op jit(solution)/shard_map/all_to_all | solution.py:41
  13.0 1.7 %shard_map.119 = (bf16[32,128,128]{2,1,0:T(8,128)(2,1)S(1)}, bf16[8,2,256,128]{3,2,1,0:T(8,128)(2,1)S(1)}, bf16[32,256]{1,0:T(8,128)(2,1)S(1)}, bf16[32,256]{1,0...) custom-call(s32[4,32]{1,0:T(4,128)} %lengths_hbm, s32[4,32]{1,0:T(4,128)} %offload_hbm.1, ...), custom_call_target="tpu_custom_call" | custom-call | flops 4194304 | bytes 4194304 | tf_op jit(solution)/shard_map/pallas_call | solution.py:292
  14.7 16.6 %all-to-all-done.own_ref = bf16[16,112,128]{2,1,0:T(8,128)(2,1)S(1)} async-done(((bf16[16,112,128]{2,1,0:T(8,128)(2,1)}), bf16[16,112,128]{2,1,0:T(8,128)(2,1)S(1)}, u32[]{:S(2)}, u32[]{:S(2)}) %all-to-all-start) | async-done | bytes 458784 | tf_op jit(solution)/shard_map/all_to_all | solution.py:41
  31.4 0.0 collective-permute-start
  31.4 0.0 collective-permute-done.1.other_hbm
  31.4 1.7 %shard_map.120 = (bf16[32,128,128]{2,1,0:T(8,128)(2,1)S(1)}, bf16[128,2048]{1,0:T(8,128)(2,1)S(1)}, bf16[128,2048]{1,0:T(8,128)(2,1)S(1)}) custom-call(bf16[1,1,32,128,512]{4,3,2,1,0:T(8,128)(2,1)} %values_hbm, bf16[128,8192]{1,0:T(8,128)(2,1)} %own_hbm.1, bf16[128,8192]{1,0:T(8,128)(2,1)} %collective-permute-done.1.other_hbm), custom_call_target="tpu_custom_call" | custom-call | bytes 4194304 | tf_op jit(solution)/shard_map/pallas_call | solution.py:320
  33.1 0.1 collective-permute-done.other_ref
  33.2 0.3 shard_map.121
  33.5 11.4 %all_to_all.20.got_ref = bf16[8,32,512]{2,1,0:T(8,128)(2,1)S(1)} all-to-all(bf16[8,32,512]{2,1,0:T(8,128)(2,1)S(1)} %shard_map.121), channel_id=1, replica_groups=mesh['pool'=2,'inst'=4,'z'=8,'yh'=2,'core'=2] {'pool','inst'}, dimensions={0} | all-to-all | bytes 524288 | tf_op jit(solution)/shard_map/all_to_all | solution.py:330
  44.9 1.1 %shard_map.122 = bf16[16,32,128]{2,1,0:T(8,128)(2,1)S(1)} custom-call(bf16[8,32,512]{2,1,0:T(8,128)(2,1)S(1)} %all_to_all.20.got_ref, bf16[32,128,128]{2,1,0:T(8,128)(2,1)S(1)} %get-tuple-element.46.keys_ref, bf16[32,128,128]{2,1,0:T(8,128)(2,1)S(1)} %get-tuple-element.47.values_ref, bf16[32,256]{1,0:T(8,128)(2,1)S(1)} %get-tuple-element.48.pick_ref, ...), custom_call_target="tpu_custom_call" | custom-call | flops 67108864 | bytes 4194304 | tf_op jit(solution)/shard_map/pallas_call | solution.py:331
  46.0 8.5 %all_to_all.21 = bf16[16,32,128]{2,1,0:T(8,128)(2,1)S(1)} all-to-all(bf16[16,32,128]{2,1,0:T(8,128)(2,1)S(1)} %shard_map.122), channel_id=1, replica_groups=mesh['pool'=2,'inst'=4,'z'=8,'yh'=2,'core'=2] {'pool','inst','core'}, dimensions={0} | all-to-all | bytes 262144 | tf_op jit(solution)/shard_map/all_to_all | solution.py:334
  54.5 0.4 shard_map.123
  54.9 14.3 %all_to_all.22.got_ref = bf16[16,32,128]{2,1,0:T(8,128)(2,1)S(1)} all-to-all(bf16[16,32,128]{2,1,0:T(8,128)(2,1)S(1)} %shard_map.123), channel_id=1, replica_groups={{0,130,4,134,8,138,12,142,16,146,20,150,24,154,28,158},{1,131,5,135,9,1..., dimensions={0} | all-to-all | bytes 262144 | tf_op jit(solution)/shard_map/all_to_all | solution.py:41
  69.2 0.6 shard_map.124
Async XLA Ops:
  0.0 31.4 %collective-permute-start.1 = (bf16[128,8192]{1,0:T(8,128)(2,1)}, bf16[128,8192]{1,0:T(8,128)(2,1)}, u32[]{:S(2)}, u32[]{:S(2)}) collective-permute-start(bf16[128,8192]{1,0:T(8,128)(2,1)} %own_hbm.1), channel_id=1, source_target_pairs={{0,1},{1,0},{2,3},{3,2},{4,5},{5,4},{6,7},{7,6},{8,9},{9,8},{10,11... | collective-permute-start | bytes 6291464 | tf_op jit(solution)/shard_map/ppermute | solution.py:45
  2.0 29.4 %all-to-all-start = ((bf16[16,112,128]{2,1,0:T(8,128)(2,1)}), bf16[16,112,128]{2,1,0:T(8,128)(2,1)S(1)}, u32[]{:S(2)}, u32[]{:S(2)}) async-start(bf16[16,112,128]{2,1,0:T(8,128)(2,1)} %shard_map.118), calls=%async_computation | async-start | bytes 917504 | tf_op jit(solution)/shard_map/all_to_all | solution.py:41
  31.4 1.8 %collective-permute-start = (bf16[16,112,128]{2,1,0:T(8,128)(2,1)S(1)}, bf16[16,112,128]{2,1,0:T(8,128)(2,1)S(1)}, u32[]{:S(2)}, u32[]{:S(2)}) collective-permute-start(bf16[16,112,128]{2,1,0:T(8,128)(2,1)S(1)} %all-to-all-done.own_ref), channel_id=1, source_target_pairs={{0,1},{1,0},{2,3},{3,2},{4,5},{5,4},{6,7},{7,6},{8,9},{9,8},{10,11... | collective-permute-start | bytes 1376264 | tf_op jit(solution)/shard_map/ppermute | solution.py:45

commit v4 on v3

--- a/solution.py
+++ b/solution.py
@@ -13,6 +13,7 @@
 REQ = 32
 POOLS, INSTS, ZS, YS, CORES = 2, 4, 8, 2, 2
 RING = ZS * POOLS
+EXTRA = 8
 epsilon = 1e-05
 rope_base = 500000.0
 AXES = ("pool", "inst", "z", "yh", "core")
@@ -69,44 +70,65 @@
     return pl.ds(pl.multiple_of((z // (ZS // HEADS)) * HD, HD), HD)
 
 
-def features_kernel(x_hbm, gain_hbm, wk_hbm, wv_hbm, out_ref, x_ref, gain_ref, wk_ref, wv_ref, sems):
+def two_rows(row):
+    high = row.astype(BF).astype(F32)
+    at = iota((EXTRA, HD), 0)
+    return jnp.where(at == 0, high, jnp.where(at == 1, row - high, 0.0)).astype(BF)
+
+
+def features_kernel(
+    x_hbm, gain_hbm, wk_hbm, wv_hbm,
+    scaled_out, extra_out, keep_out, give_out,
+    x_ref, gain_ref, wk_ref, wv_ref, sems,
+):
     pairs = ((x_hbm, x_ref), (gain_hbm, gain_ref), (wk_hbm, wk_ref), (wv_hbm, wv_ref))
     for copy in start_copies(pairs, sems):
         copy.wait()
     x = x_ref[0].astype(F32)
     scaled = (x * gain_ref[...].astype(F32)).astype(BF)
     squares = jnp.sum(x * x, axis=1, keepdims=True)
-    eye = iota((REQ, HD), 0) == iota((REQ, HD), 1)
-    row = jnp.sum(jnp.where(eye, squares, 0.0), axis=0, keepdims=True)
-    high = row.astype(BF).astype(F32)
-    at = iota((16, HD), 0)
-    extra = jnp.where(at == 0, high, jnp.where(at == 1, row - high, 0.0)).astype(BF)
-    k = dot(scaled, wk_ref[...]).astype(BF)
-    v = dot(scaled, wv_ref[...]).astype(BF)
+    place = iota((REQ, HD), 0) + lax.axis_index("inst") * REQ == iota((REQ, HD), 1)
+    scaled_out[...] = scaled
+    extra_out[...] = two_rows(jnp.sum(jnp.where(place, squares, 0.0), axis=0, keepdims=True))
+    k = dot(scaled, wk_ref[...])
+    v = dot(scaled, wv_ref[...])
+    first = lax.axis_index("core") == 0
+    keep_out[...] = jnp.where(first, k, v).astype(BF)
+    give_out[...] = jnp.where(first, v, k).astype(BF)
+
+
+def message_kernel(scaled_ref, extra_ref, keep_ref, taken_ref, out_ref):
+    terms = (keep_ref[...].astype(F32) + taken_ref[...].astype(F32)).astype(BF)
     for m in range(RING):
         n = (m // POOLS) // (ZS // HEADS)
-        head = slice(n * HD, (n + 1) * HD)
-        out_ref[m, 0:REQ, :] = scaled
-        out_ref[m, REQ : 2 * REQ, :] = k[:, head]
-        out_ref[m, 2 * REQ : 3 * REQ, :] = v[:, head]
-        out_ref[m, 3 * REQ :, :] = extra
+        out_ref[m, 0:REQ, :] = scaled_ref[...]
+        out_ref[m, REQ : 2 * REQ, :] = terms[:, n * HD : (n + 1) * HD]
+        out_ref[m, 2 * REQ :, :] = extra_ref[...]
+
+
+def output_columns(source, out):
+    core = lax.axis_index("core")
+    side = lax.axis_index("pool") ^ lax.axis_index("yh")
+    pairs = []
+    for m in range(RING):
+        z, p = m // POOLS, m % POOLS
+        block = ((p * ZS + z) * YS + (p ^ side)) * CORES + core
+        lanes = pl.ds(pl.multiple_of(block * HD, HD), HD)
+        pairs.append((source.at[:, lanes], out.at[:, pl.ds(m * HD, HD)]))
+    return pairs
 
 
 def early_kernel(
-    lengths_hbm, offload_hbm, host_hbm, slot_hbm, keys_hbm, wq_hbm,
-    keys_out, wq_out, pick_ref, back_ref, cos_ref, sin_ref, span_ref,
+    lengths_hbm, offload_hbm, host_hbm, slot_hbm, keys_hbm, values_hbm, wo_hbm,
+    keys_out, values_out, wo_out, pick_ref, back_ref, cos_ref, sin_ref, span_ref,
     lengths_ref, offload_ref, host_ref, slot_ref, sems,
 ):
     pool, inst, z = lax.axis_index("pool"), lax.axis_index("inst"), lax.axis_index("z")
-    core = lax.axis_index("core")
-    side = pool ^ lax.axis_index("yh")
     pairs = [(lengths_hbm, lengths_ref), (offload_hbm, offload_ref), (host_hbm, host_ref), (slot_hbm, slot_ref)]
     small = len(pairs)
-    for p in range(POOLS):
-        for n, c in enumerate((core, 1 - core)):
-            pairs.append((wq_hbm.at[p, :, p ^ side, c], wq_out.at[:, p, pl.ds(n * HD, HD), :]))
     pairs.append((keys_hbm.at[0, 0, :, :, head_lanes(z)], keys_out))
-    copies = start_copies(pairs, sems)
+    pairs.append((values_hbm.at[0, 0, :, :, head_lanes(z)], values_out))
+    copies = start_copies(pairs + output_columns(wo_hbm, wo_out), sems)
     for copy in copies[:small]:
         copy.wait()
     home = iota((INSTS, REQ), 0) * REQ + iota((INSTS, REQ), 1)
@@ -140,44 +162,44 @@
         copy.wait()
 
 
-def late_kernel(values_hbm, own_hbm, other_hbm, values_out, own_out, other_out, sems):
+def late_kernel(wq_hbm, wo_hbm, wq_out, wo_out, sems):
     core = lax.axis_index("core")
     side = lax.axis_index("pool") ^ lax.axis_index("yh")
-    pairs = [(values_hbm.at[0, 0, :, :, head_lanes(lax.axis_index("z"))], values_out)]
-    for source, out in ((own_hbm, own_out), (other_hbm, other_out)):
-        for m in range(RING):
-            z, p = m // POOLS, m % POOLS
-            block = ((p * ZS + z) * YS + (p ^ side)) * CORES + core
-            lanes = pl.ds(pl.multiple_of(block * HD, HD), HD)
-            pairs.append((source.at[:, lanes], out.at[:, pl.ds(m * HD, HD)]))
-    for copy in start_copies(pairs, sems):
+    pairs = []
+    for p in range(POOLS):
+        for n, c in enumerate((core, 1 - core)):
+            pairs.append((wq_hbm.at[p, :, p ^ side, c], wq_out.at[:, p, pl.ds(n * HD, HD), :]))
+    for copy in start_copies(pairs + output_columns(wo_hbm, wo_out), sems):
         copy.wait()
 
 
 def query_kernel(own_ref, other_ref, wq_ref, out_ref):
     q = jnp.zeros((REQ, HD), F32)
-    sums = jnp.zeros((2 * REQ, HD), F32)
-    extra = jnp.zeros((16, HD), F32)
+    own = jnp.zeros((REQ, HD), F32)
+    other = jnp.zeros((REQ, HD), F32)
+    extra = jnp.zeros((EXTRA, HD), F32)
     for m in range(RING):
         features = jnp.concatenate([own_ref[m, 0:REQ, :], other_ref[m, 0:REQ, :]], axis=1)
         q += dot(features, wq_ref[m // POOLS, m % POOLS])
-        sums += own_ref[m, REQ : 3 * REQ, :].astype(F32) + other_ref[m, REQ : 3 * REQ, :].astype(F32)
-        extra += own_ref[m, 3 * REQ :, :].astype(F32) + other_ref[m, 3 * REQ :, :].astype(F32)
-    row = extra[0:1] + extra[1:2]
-    eye = iota((REQ, HD), 0) == iota((REQ, HD), 1)
-    squares = jnp.sum(jnp.where(eye, row, 0.0), axis=1, keepdims=True)
-    high = squares.astype(BF).astype(F32)
-    tail = jnp.where(iota((REQ, HD), 1) < HD // 2, high, squares - high)
-    message = jnp.concatenate([q, sums[:REQ], sums[REQ:], tail], axis=1).astype(BF)
+        own += own_ref[m, REQ : 2 * REQ, :].astype(F32)
+        other += other_ref[m, REQ : 2 * REQ, :].astype(F32)
+        extra += own_ref[m, 2 * REQ :, :].astype(F32) + other_ref[m, 2 * REQ :, :].astype(F32)
+    first = lax.axis_index("core") == 0
+    k, v = jnp.where(first, own, other), jnp.where(first, other, own)
+    rest = two_rows(extra[0:1] + extra[1:2])
     for m in range(POOLS * INSTS):
-        out_ref[m] = message
+        for n, part in enumerate((q, k, v)):
+            out_ref[m, n * REQ : (n + 1) * REQ, :] = part.astype(BF)
+        out_ref[m, 3 * REQ :, :] = rest
 
 
 def attend_kernel(got_ref, keys_ref, values_ref, pick_ref, cos_ref, sin_ref, span_ref, out_ref, *, width):
-    got = got_ref[...].reshape(POOLS * INSTS * REQ, 4 * HD)
-    mine = dot(pick_ref[...], got)
-    q, k, v, s = (mine[:, n * HD : (n + 1) * HD] for n in range(4))
-    squares = s[:, 0:1] + s[:, HD // 2 : HD // 2 + 1]
+    pick = pick_ref[...]
+    q, k, v = (dot(pick, got_ref[:, n * REQ : (n + 1) * REQ, :].reshape(pick.shape[1], HD)) for n in range(3))
+    rest = jnp.zeros((EXTRA, HD), F32)
+    for m in range(POOLS * INSTS):
+        rest += got_ref[m, 3 * REQ :, :].astype(F32)
+    squares = jnp.sum(pick[:, :HD].astype(F32) * (rest[0:1] + rest[1:2]), axis=1, keepdims=True)
     root = jnp.sqrt(squares / width + epsilon)
 
     def rotate(t):
@@ -271,10 +293,9 @@
     width = query_weight.shape[0]
     seats = POOLS * INSTS * REQ
 
-    buddy_weight = swap_core(output_weight)
-    message = call(
+    scaled, extra, keep, give = call(
         features_kernel,
-        shape(RING, 3 * REQ + 16, HD),
+        [shape(REQ, HD), shape(EXTRA, HD), shape(REQ, HEADS * HD), shape(REQ, HEADS * HD)],
         [HBM] * 4,
         1 << 23,
         1 << 20,
@@ -286,47 +307,43 @@
             pltpu.SemaphoreType.DMA((4,)),
         ],
     )(*in_hbm(hidden_states, norm_gain.reshape(1, HD), key_weight, value_weight))
-    message, lengths = lax.optimization_barrier((message, lengths))
+    message = call(message_kernel, shape(RING, 2 * REQ + EXTRA, HD), [VMEM] * 4, 1 << 14, 1 << 19)(
+        scaled, extra, keep, swap_core(give)
+    )
+    message, lengths, output_weight = lax.optimization_barrier((message, lengths, output_weight))
+    buddy_weight = swap_core(output_weight)
     got = ring_exchange(message)
     table = pltpu.VMEM(lengths.shape, I32)
     early = call(
         early_kernel,
         [
             shape(REQ, HD, HD),
-            shape(ZS, POOLS, CORES * HD, HD),
+            shape(REQ, HD, HD),
+            shape(HD, RING * HD),
             shape(REQ, seats),
             shape(REQ, seats),
             shape(REQ, HD, dtype=F32),
             shape(REQ, HD, dtype=F32),
             shape(REQ, HD, dtype=F32),
         ],
-        [HBM] * 6,
+        [HBM] * 7,
         1 << 22,
         1 << 22,
-        [table] * 4 + [pltpu.SemaphoreType.DMA((4 + 2 * POOLS + 1,))],
-    )(
-        *in_hbm(
-            lengths,
-            offload,
-            host_instance,
-            cache_slot,
-            key_cache,
-            query_weight.reshape(POOLS, ZS, YS, CORES, HD, HD),
-        )
-    )
-    got, early, value_cache = lax.optimization_barrier((got, early, value_cache))
-    keys, wq, pick, back, cos, sin, span = early
+        [table] * 4 + [pltpu.SemaphoreType.DMA((6 + RING,))],
+    )(*in_hbm(lengths, offload, host_instance, cache_slot, key_cache, value_cache, output_weight))
+    got, early, query_weight = lax.optimization_barrier((got, early, query_weight))
+    keys, values, keep, pick, back, cos, sin, span = early
     other = swap_core(got)
     late = call(
         late_kernel,
-        [shape(REQ, HD, HD), shape(HD, RING * HD), shape(HD, RING * HD)],
-        [HBM] * 3,
+        [shape(ZS, POOLS, CORES * HD, HD), shape(HD, RING * HD)],
+        [HBM] * 2,
         0,
         1 << 22,
-        [pltpu.SemaphoreType.DMA((1 + 2 * RING,))],
-    )(*in_hbm(value_cache, output_weight, buddy_weight))
-    other, (values, keep, taken) = lax.optimization_barrier((other, late))
-    message = call(query_kernel, shape(POOLS * INSTS, REQ, 4 * HD), [VMEM] * 3, 1 << 25, 1 << 22)(got, other, wq)
+        [pltpu.SemaphoreType.DMA((2 * POOLS + RING,))],
+    )(*in_hbm(query_weight.reshape(POOLS, ZS, YS, CORES, HD, HD), buddy_weight))
+    other, (wq, taken) = lax.optimization_barrier((other, late))
+    message = call(query_kernel, shape(POOLS * INSTS, 3 * REQ + EXTRA, HD), [VMEM] * 3, 1 << 25, 1 << 22)(got, other, wq)
     got = lax.all_to_all(message, ("pool", "inst"), 0, 0, tiled=True)
     message = call(
         functools.partial(attend_kernel, width=width), shape(POOLS * INSTS * CORES, REQ, HD), [VMEM] * 7, 1 << 26, 1 << 22

time: 70.7 us -> 67.1 us (0.949)
  waiting for transfers between devices: 16.7 us -> 13.9 us
    all_to_all x1, waiting for transfers between devices: 16.6 us -> 12.6 us  [ring_exchange(): return lax.all_to_all(x, AXES, 0, 0, axis_index_groups=RINGS, tiled=True)]
    ppermute x2 -> x3, waiting for transfers between devices: 0.06 us -> 1.33 us  [swap_core(): return lax.ppermute(x, 'core', [(0, 1), (1, 0)])]
    pallas_call x4 -> x5, Pallas kernels: 5.72 us -> 5.53 us  [the longest x1 1.87 us: shards(): call(early_kernel, [shape(REQ, HD, HD), shape(REQ, HD, HD), shape(HD, RIN...]
  transfers between devices with their start and end apart: 3 -> 4, of which waited for: 2 -> 3; matrix products, arithmetic and copies ran while one was open for 0% -> 0% of each run, Pallas kernels for 8% -> 5%
where the time goes in v4:
time: 67.1 us; the launch traced here: 66.3 us
  blocking collectives  33.6 us (50%)
  waiting for transfers between devices  13.9 us (21%)
  starting transfers between devices  11.3 us (17%)
  Pallas kernels  7.51 us (11%)
    all_to_all x1, blocking collectives, ring_exchange(): return lax.all_to_all(x, AXES, 0, 0, axis_index_groups=RINGS, tiled=True)  14.3 us
    all_to_all x1, waiting for transfers between devices, ring_exchange(): return lax.all_to_all(x, AXES, 0, 0, axis_index_groups=RINGS, tiled=True)  12.6 us
    all_to_all x1, starting transfers between devices, ring_exchange(): return lax.all_to_all(x, AXES, 0, 0, axis_index_groups=RINGS, tiled=True)  11 us
    all_to_all x1, blocking collectives, shards(): got = lax.all_to_all(message, ('pool', 'inst'), 0, 0, tiled=True)  10.8 us
    all_to_all x1, blocking collectives, shards(): got = lax.all_to_all(message, ('pool', 'inst', 'core'), 0, 0, tiled=True)  8.54 us
    pallas_call x1, Pallas kernels, shards(): call(early_kernel, [shape(REQ, HD, HD), shape(REQ, HD, HD), shape(HD, RIN...  1.87 us
    pallas_call x1, Pallas kernels, shards(): call(late_kernel, [shape(ZS, POOLS, CORES * HD, HD), shape(HD, RING * HD)...  1.43 us
  transfers between devices with their start and end apart: 4, of which 3 were waited for; matrix products, arithmetic and copies ran while one was open for 0% of the time, Pallas kernels for 5%

profile of v4, /device:TPU:2, one launch (start us, length us, event | category | flops | bytes accessed | tf_op | source)
XLA Modules:
  0.0 66.3 jit_solution(8167023262326606721)
XLA Ops:
  0.0 1.2 %shard_map.118 = (bf16[32,128]{1,0:T(8,128)(2,1)S(1)}, bf16[8,128]{1,0:T(8,128)(2,1)S(1)}, bf16[32,512]{1,0:T(8,128)(2,1)S(1)}, bf16[32,512]{1,0:T(8,128)(2,1)S(1)}) custom-call(bf16[1,32,128]{2,1,0:T(8,128)(2,1)} %x_hbm.1, bf16[1,128]{1,0:T(2,128)(2,1)} %bitcast.5, bf16[128,512]{1,0:T(8,128)(2,1)} %wk_hbm.1, bf16[128,512]{1,0:T(8,128)(2,1)} %wv_hbm.1), custom_call_target="tpu_custom_call" | custom-call | flops 8388608 | bytes 1048576 | tf_op jit(solution)/shard_map/pallas_call | solution.py:296
  1.2 0.1 collective-permute-start
  1.3 1.2 %collective-permute-done.taken_ref = bf16[32,512]{1,0:T(8,128)(2,1)S(1)} collective-permute-done((bf16[32,512]{1,0:T(8,128)(2,1)S(1)}, bf16[32,512]{1,0:T(8,128)(2,1)S(1)}, u32[]{:S(2)}, u32[]{:S(2)}) %collective-permute-start) | collective-permute-done | bytes 32800 | tf_op jit(solution)/shard_map/ppermute | solution.py:46
  2.5 0.7 %shard_map.119 = bf16[16,72,128]{2,1,0:T(8,128)(2,1)} custom-call(bf16[32,128]{1,0:T(8,128)(2,1)S(1)} %get-tuple-element.35.scaled_ref, bf16[8,128]{1,0:T(8,128)(2,1)S(1)} %get-tuple-element.36.extra_ref, bf16[32,512]{1,0:T(8,128)(2,1)S(1)} %get-tuple-element.37.keep_ref, bf16[32,512]{1,0:T(8,128)(2,1)S(1)} %collective-permute-done.taken_ref), custom_call_target="tpu_custom_call" | custom-call | flops 16384 | bytes 524288 | tf_op jit(solution)/shard_map/pallas_call | solution.py:310
  3.2 0.2 collective-permute-start.2
  3.4 11.0 %all-to-all-start = ((bf16[16,72,128]{2,1,0:T(8,128)(2,1)}), bf16[16,72,128]{2,1,0:T(8,128)(2,1)S(1)}, u32[]{:S(2)}, u32[]{:S(2)}) async-start(bf16[16,72,128]{2,1,0:T(8,128)(2,1)} %shard_map.119), calls=%async_computation | async-start | bytes 589824 | tf_op jit(solution)/shard_map/all_to_all | solution.py:42
  14.4 1.9 %shard_map.120 = (bf16[32,128,128]{2,1,0:T(8,128)(2,1)S(1)}, bf16[32,128,128]{2,1,0:T(8,128)(2,1)S(1)}, bf16[128,2048]{1,0:T(8,128)(2,1)S(1)}, bf16[32,256]{1,0:...) custom-call(s32[4,32]{1,0:T(4,128)} %lengths_hbm, ...), custom_call_target="tpu_custom_call" | custom-call | flops 4194304 | bytes 4194304 | tf_op jit(solution)/shard_map/pallas_call | solution.py:317
  16.3 12.6 %all-to-all-done.own_ref = bf16[16,72,128]{2,1,0:T(8,128)(2,1)S(1)} async-done(((bf16[16,72,128]{2,1,0:T(8,128)(2,1)}), bf16[16,72,128]{2,1,0:T(8,128)(2,1)S(1)}, u32[]{:S(2)}, u32[]{:S(2)}) %all-to-all-start) | async-done | bytes 294944 | tf_op jit(solution)/shard_map/all_to_all | solution.py:42
  28.9 0.0 collective-permute-start.1
  28.9 0.0 collective-permute-done.2.wo_hbm
  28.9 1.4 %shard_map.121 = (bf16[8,2,256,128]{3,2,1,0:T(8,128)(2,1)S(1)}, bf16[128,2048]{1,0:T(8,128)(2,1)S(1)}) custom-call(bf16[2,8,2,2,128,128]{5,4,3,2,1,0:T(8,128)(2,1)} %bitcast.4, bf16[128,8192]{1,0:T(8,128)(2,1)} %collective-permute-done.2.wo_hbm), custom_call_target="tpu_custom_call" | custom-call | bytes 4194304 | tf_op jit(solution)/shard_map/pallas_call | solution.py:337
  30.3 0.1 collective-permute-done.1.other_ref
  30.4 0.3 shard_map.122
  30.7 10.8 %all_to_all.20.got_ref = bf16[8,104,128]{2,1,0:T(8,128)(2,1)S(1)} all-to-all(bf16[8,104,128]{2,1,0:T(8,128)(2,1)S(1)} %shard_map.122), channel_id=1, replica_groups=mesh['pool'=2,'inst'=4,'z'=8,'yh'=2,'core'=2] {'pool','inst'}, dimensions={0} | all-to-all | bytes 425984 | tf_op jit(solution)/shard_map/all_to_all | solution.py:347
  41.5 1.0 %shard_map.123 = bf16[16,32,128]{2,1,0:T(8,128)(2,1)S(1)} custom-call(bf16[8,104,128]{2,1,0:T(8,128)(2,1)S(1)} %all_to_all.20.got_ref, bf16[32,128,128]{2,1,0:T(8,128)(2,1)S(1)} %get-tuple-element.56.keys_ref, bf16[32,128,128]{2,1,0:T(8,128)(2,1)S(1)} %get-tuple-element.57.values_ref, bf16[32,256]{1,0:T(8,128)(2,1)S(1)} %get-tuple-element.58.pick_ref, ...), custom_call_target="tpu_custom_call" | custom-call | flops 67108864 | bytes 4194304 | tf_op jit(solution)/shard_map/pallas_call | solution.py:348
  42.5 8.5 %all_to_all.21 = bf16[16,32,128]{2,1,0:T(8,128)(2,1)S(1)} all-to-all(bf16[16,32,128]{2,1,0:T(8,128)(2,1)S(1)} %shard_map.123), channel_id=1, replica_groups=mesh['pool'=2,'inst'=4,'z'=8,'yh'=2,'core'=2] {'pool','inst','core'}, dimensions={0} | all-to-all | bytes 262144 | tf_op jit(solution)/shard_map/all_to_all | solution.py:351
  51.0 0.4 shard_map.124
  51.4 14.3 %all_to_all.22.got_ref = bf16[16,32,128]{2,1,0:T(8,128)(2,1)S(1)} all-to-all(bf16[16,32,128]{2,1,0:T(8,128)(2,1)S(1)} %shard_map.124), channel_id=1, replica_groups={{0,130,4,134,8,138,12,142,16,146,20,150,24,154,28,158},{1,131,5,135,9,1..., dimensions={0} | all-to-all | bytes 262144 | tf_op jit(solution)/shard_map/all_to_all | solution.py:42
  65.7 0.6 shard_map.125
Async XLA Ops:
  1.2 1.3 %collective-permute-start = (bf16[32,512]{1,0:T(8,128)(2,1)S(1)}, bf16[32,512]{1,0:T(8,128)(2,1)S(1)}, u32[]{:S(2)}, u32[]{:S(2)}) collective-permute-start(bf16[32,512]{1,0:T(8,128)(2,1)S(1)} %get-tuple-element.38), channel_id=1, source_target_pairs={{0,1},{1,0},{2,3},{3,2},{4,5},{5,4},{6,7},{7,6},{8,9},{9,8},{10,11... | collective-permute-start | bytes 98312 | tf_op jit(solution)/shard_map/ppermute | solution.py:46
  3.2 25.6 %collective-permute-start.2 = (bf16[128,8192]{1,0:T(8,128)(2,1)}, bf16[128,8192]{1,0:T(8,128)(2,1)}, u32[]{:S(2)}, u32[]{:S(2)}) collective-permute-start(bf16[128,8192]{1,0:T(8,128)(2,1)} %wo_hbm), channel_id=1, source_target_pairs={{0,1},{1,0},{2,3},{3,2},{4,5},{5,4},{6,7},{7,6},{8,9},{9,8},{10,11... | collective-permute-start | bytes 6291464 | tf_op jit(solution)/shard_map/ppermute | solution.py:46
  3.4 25.5 %all-to-all-start = ((bf16[16,72,128]{2,1,0:T(8,128)(2,1)}), bf16[16,72,128]{2,1,0:T(8,128)(2,1)S(1)}, u32[]{:S(2)}, u32[]{:S(2)}) async-start(bf16[16,72,128]{2,1,0:T(8,128)(2,1)} %shard_map.119), calls=%async_computation | async-start | bytes 589824 | tf_op jit(solution)/shard_map/all_to_all | solution.py:42
  28.9 1.6 %collective-permute-start.1 = (bf16[16,72,128]{2,1,0:T(8,128)(2,1)S(1)}, bf16[16,72,128]{2,1,0:T(8,128)(2,1)S(1)}, u32[]{:S(2)}, u32[]{:S(2)}) collective-permute-start(bf16[16,72,128]{2,1,0:T(8,128)(2,1)S(1)} %all-to-all-done.own_ref), channel_id=1, source_target_pairs={{0,1},{1,0},{2,3},{3,2},{4,5},{5,4},{6,7},{7,6},{8,9},{9,8},{10,11... | collective-permute-start | bytes 884744 | tf_op jit(solution)/shard_map/ppermute | solution.py:46

commit v5 on v4

--- a/solution.py
+++ b/solution.py
@@ -30,16 +30,32 @@
     return (((p * INSTS + i) * ZS + z) * YS + y) * CORES + c
 
 
+PLACES = [((z + 5) % ZS, 1 - y) for z in range(ZS) for y in range(YS)]
 RINGS = [
-    [device_number(p, i, z, p ^ s, c) for z in range(ZS) for p in range(POOLS)]
+    [device_number(y ^ s, i, z, y, c) for z, y in PLACES]
     for s in range(2)
     for i in range(INSTS)
     for c in range(CORES)
 ]
 
 
-def ring_exchange(x):
-    return lax.all_to_all(x, AXES, 0, 0, axis_index_groups=RINGS, tiled=True)
+FIRST = 2
+HEADS_ALIKE = [(z, y, c) for z in range(ZS) for y in range(YS) for c in range(CORES)]
+TURNS = [(a, (i + FIRST) % INSTS) for a in range(POOLS) for i in range(INSTS)]
+HOSTS = [[device_number(a ^ y, i, z, y, c) for a, i in TURNS] for z, y, c in HEADS_ALIKE]
+CHIPS = [
+    [device_number(a ^ y, i, z, y, c) for a, i in TURNS for c in range(CORES)]
+    for z in range(ZS)
+    for y in range(YS)
+]
+
+
+def turn(inst):
+    return (inst + (INSTS - FIRST)) % INSTS
+
+
+def exchange(x, groups):
+    return lax.all_to_all(x, AXES, 0, 0, axis_index_groups=groups, tiled=True)
 
 
 def swap_core(x):
@@ -87,7 +103,7 @@
     x = x_ref[0].astype(F32)
     scaled = (x * gain_ref[...].astype(F32)).astype(BF)
     squares = jnp.sum(x * x, axis=1, keepdims=True)
-    place = iota((REQ, HD), 0) + lax.axis_index("inst") * REQ == iota((REQ, HD), 1)
+    place = iota((REQ, HD), 0) + turn(lax.axis_index("inst")) * REQ == iota((REQ, HD), 1)
     scaled_out[...] = scaled
     extra_out[...] = two_rows(jnp.sum(jnp.where(place, squares, 0.0), axis=0, keepdims=True))
     k = dot(scaled, wk_ref[...])
@@ -99,8 +115,8 @@
 
 def message_kernel(scaled_ref, extra_ref, keep_ref, taken_ref, out_ref):
     terms = (keep_ref[...].astype(F32) + taken_ref[...].astype(F32)).astype(BF)
-    for m in range(RING):
-        n = (m // POOLS) // (ZS // HEADS)
+    for m, (z, _) in enumerate(PLACES):
+        n = z // (ZS // HEADS)
         out_ref[m, 0:REQ, :] = scaled_ref[...]
         out_ref[m, REQ : 2 * REQ, :] = terms[:, n * HD : (n + 1) * HD]
         out_ref[m, 2 * REQ :, :] = extra_ref[...]
@@ -110,9 +126,8 @@
     core = lax.axis_index("core")
     side = lax.axis_index("pool") ^ lax.axis_index("yh")
     pairs = []
-    for m in range(RING):
-        z, p = m // POOLS, m % POOLS
-        block = ((p * ZS + z) * YS + (p ^ side)) * CORES + core
+    for m, (z, y) in enumerate(PLACES):
+        block = (((y ^ side) * ZS + z) * YS + y) * CORES + core
         lanes = pl.ds(pl.multiple_of(block * HD, HD), HD)
         pairs.append((source.at[:, lanes], out.at[:, pl.ds(m * HD, HD)]))
     return pairs
@@ -131,11 +146,12 @@
     copies = start_copies(pairs + output_columns(wo_hbm, wo_out), sems)
     for copy in copies[:small]:
         copy.wait()
-    home = iota((INSTS, REQ), 0) * REQ + iota((INSTS, REQ), 1)
-    away = INSTS * REQ + host_ref[...] * REQ + slot_ref[...]
+    yh = lax.axis_index("yh")
+    home = yh * (INSTS * REQ) + turn(iota((INSTS, REQ), 0)) * REQ + iota((INSTS, REQ), 1)
+    away = (1 - yh) * (INSTS * REQ) + turn(host_ref[...]) * REQ + slot_ref[...]
     seat = jnp.where(offload_ref[...] == 1, away, home)
     spans = lengths_ref[...].astype(F32)
-    here = iota((REQ, REQ), 0) + (pool * INSTS + inst) * REQ
+    here = iota((REQ, REQ), 0) + ((pool ^ yh) * INSTS + turn(inst)) * REQ
     square = iota((REQ, REQ), 0) == iota((REQ, REQ), 1)
     pick = jnp.zeros((REQ, POOLS * INSTS * REQ), F32)
     span = jnp.zeros((REQ, 1), F32)
@@ -143,7 +159,7 @@
     for i in range(INSTS):
         sits = seat[i : i + 1, :] == here
         wide = iota((REQ, POOLS * INSTS * REQ), 1) % (INSTS * REQ)
-        place = (wide == iota(wide.shape, 0) + i * REQ).astype(F32).astype(BF)
+        place = (wide == iota(wide.shape, 0) + turn(i) * REQ).astype(F32).astype(BF)
         pick += dot(sits.astype(F32).astype(BF), place)
         span += jnp.sum(jnp.where(sits, spans[i : i + 1, :], 0.0), axis=1, keepdims=True)
         turned = jnp.sum(jnp.where(square, seat[i : i + 1, :].astype(F32), 0.0), axis=1, keepdims=True)
@@ -166,9 +182,9 @@
     core = lax.axis_index("core")
     side = lax.axis_index("pool") ^ lax.axis_index("yh")
     pairs = []
-    for p in range(POOLS):
+    for y in range(YS):
         for n, c in enumerate((core, 1 - core)):
-            pairs.append((wq_hbm.at[p, :, p ^ side, c], wq_out.at[:, p, pl.ds(n * HD, HD), :]))
+            pairs.append((wq_hbm.at[y ^ side, :, y, c], wq_out.at[:, y, pl.ds(n * HD, HD), :]))
     for copy in start_copies(pairs + output_columns(wo_hbm, wo_out), sems):
         copy.wait()
 
@@ -178,9 +194,9 @@
     own = jnp.zeros((REQ, HD), F32)
     other = jnp.zeros((REQ, HD), F32)
     extra = jnp.zeros((EXTRA, HD), F32)
-    for m in range(RING):
+    for m, place in enumerate(PLACES):
         features = jnp.concatenate([own_ref[m, 0:REQ, :], other_ref[m, 0:REQ, :]], axis=1)
-        q += dot(features, wq_ref[m // POOLS, m % POOLS])
+        q += dot(features, wq_ref[place])
         own += own_ref[m, REQ : 2 * REQ, :].astype(F32)
         other += other_ref[m, REQ : 2 * REQ, :].astype(F32)
         extra += own_ref[m, 2 * REQ :, :].astype(F32) + other_ref[m, 2 * REQ :, :].astype(F32)
@@ -312,7 +328,7 @@
     )
     message, lengths, output_weight = lax.optimization_barrier((message, lengths, output_weight))
     buddy_weight = swap_core(output_weight)
-    got = ring_exchange(message)
+    got = exchange(message, RINGS)
     table = pltpu.VMEM(lengths.shape, I32)
     early = call(
         early_kernel,
@@ -336,23 +352,23 @@
     other = swap_core(got)
     late = call(
         late_kernel,
-        [shape(ZS, POOLS, CORES * HD, HD), shape(HD, RING * HD)],
+        [shape(ZS, YS, CORES * HD, HD), shape(HD, RING * HD)],
         [HBM] * 2,
         0,
         1 << 22,
-        [pltpu.SemaphoreType.DMA((2 * POOLS + RING,))],
+        [pltpu.SemaphoreType.DMA((2 * YS + RING,))],
     )(*in_hbm(query_weight.reshape(POOLS, ZS, YS, CORES, HD, HD), buddy_weight))
     other, (wq, taken) = lax.optimization_barrier((other, late))
     message = call(query_kernel, shape(POOLS * INSTS, 3 * REQ + EXTRA, HD), [VMEM] * 3, 1 << 25, 1 << 22)(got, other, wq)
-    got = lax.all_to_all(message, ("pool", "inst"), 0, 0, tiled=True)
+    got = exchange(message, HOSTS)
     message = call(
         functools.partial(attend_kernel, width=width), shape(POOLS * INSTS * CORES, REQ, HD), [VMEM] * 7, 1 << 26, 1 << 22
     )(got, keys, values, pick, cos, sin, span)
-    got = lax.all_to_all(message, ("pool", "inst", "core"), 0, 0, tiled=True)
+    got = exchange(message, CHIPS)
     message = call(output_kernel, shape(RING, REQ, HD), [VMEM] * 4, 1 << 25, 1 << 22)(
         got.reshape(POOLS * INSTS, CORES, REQ, HD), back, keep, taken
     )
-    got = ring_exchange(message)
+    got = exchange(message, RINGS)
     return call(sum_kernel, shape(1, REQ, HD), [VMEM], 1 << 17, 1 << 18)(got)
 
 

time: 67.1 us -> 61.5 us (0.917)
  waiting for transfers between devices: 13.9 us -> 8.37 us
  starting transfers between devices: 11.3 us -> 12.8 us
  blocking collectives: 33.6 us -> 32.2 us
    all_to_all x1, waiting for transfers between devices: 12.6 us -> 7.04 us  [exchange(): return lax.all_to_all(x, AXES, 0, 0, axis_index_groups=groups, tiled=True)]
    all_to_all x1, starting transfers between devices: 11 us -> 12.6 us  [exchange(): return lax.all_to_all(x, AXES, 0, 0, axis_index_groups=groups, tiled=True)]
    all_to_all x3, blocking collectives: 33.6 us -> 32.2 us  [exchange(): return lax.all_to_all(x, AXES, 0, 0, axis_index_groups=groups, tiled=True)]
where the time goes in v5:
time: 61.5 us; the launch traced here: 61 us
  blocking collectives  32.2 us (52%)
  starting transfers between devices  12.8 us (21%)
  waiting for transfers between devices  8.37 us (14%)
  Pallas kernels  7.5 us (12%)
    all_to_all x3, blocking collectives, exchange(): return lax.all_to_all(x, AXES, 0, 0, axis_index_groups=groups, tiled=True)  32.2 us
    all_to_all x1, starting transfers between devices, exchange(): return lax.all_to_all(x, AXES, 0, 0, axis_index_groups=groups, tiled=True)  12.6 us
    all_to_all x1, waiting for transfers between devices, exchange(): return lax.all_to_all(x, AXES, 0, 0, axis_index_groups=groups, tiled=True)  7.04 us
    pallas_call x1, Pallas kernels, shards(): call(early_kernel, [shape(REQ, HD, HD), shape(REQ, HD, HD), shape(HD, RIN...  1.86 us
    pallas_call x1, Pallas kernels, shards(): call(late_kernel, [shape(ZS, YS, CORES * HD, HD), shape(HD, RING * HD)],...  1.43 us
    ppermute x3, waiting for transfers between devices, swap_core(): return lax.ppermute(x, 'core', [(0, 1), (1, 0)])  1.33 us
  transfers between devices with their start and end apart: 4, of which 3 were waited for; matrix products, arithmetic and copies ran while one was open for 0% of the time, Pallas kernels for 5%

profile of v5, /device:TPU:2, one launch (start us, length us, event | category | flops | bytes accessed | tf_op | source)
XLA Modules:
  0.0 61.0 jit_solution(16263718950670346816)
XLA Ops:
  0.0 1.2 %shard_map.118 = (bf16[32,128]{1,0:T(8,128)(2,1)S(1)}, bf16[8,128]{1,0:T(8,128)(2,1)S(1)}, bf16[32,512]{1,0:T(8,128)(2,1)S(1)}, bf16[32,512]{1,0:T(8,128)(2,1)S(1)}) custom-call(bf16[1,32,128]{2,1,0:T(8,128)(2,1)} %x_hbm.1, bf16[1,128]{1,0:T(2,128)(2,1)} %bitcast.5, bf16[128,512]{1,0:T(8,128)(2,1)} %wk_hbm.1, bf16[128,512]{1,0:T(8,128)(2,1)} %wv_hbm.1), custom_call_target="tpu_custom_call" | custom-call | flops 8388608 | bytes 1048576 | tf_op jit(solution)/shard_map/pallas_call | solution.py:312
  1.2 0.1 collective-permute-start
  1.3 1.2 %collective-permute-done.taken_ref = bf16[32,512]{1,0:T(8,128)(2,1)S(1)} collective-permute-done((bf16[32,512]{1,0:T(8,128)(2,1)S(1)}, bf16[32,512]{1,0:T(8,128)(2,1)S(1)}, u32[]{:S(2)}, u32[]{:S(2)}) %collective-permute-start) | collective-permute-done | bytes 32800 | tf_op jit(solution)/shard_map/ppermute | solution.py:62
  2.5 0.7 %shard_map.119 = bf16[16,72,128]{2,1,0:T(8,128)(2,1)} custom-call(bf16[32,128]{1,0:T(8,128)(2,1)S(1)} %get-tuple-element.35.scaled_ref, bf16[8,128]{1,0:T(8,128)(2,1)S(1)} %get-tuple-element.36.extra_ref, bf16[32,512]{1,0:T(8,128)(2,1)S(1)} %get-tuple-element.37.keep_ref, bf16[32,512]{1,0:T(8,128)(2,1)S(1)} %collective-permute-done.taken_ref), custom_call_target="tpu_custom_call" | custom-call | flops 16384 | bytes 524288 | tf_op jit(solution)/shard_map/pallas_call | solution.py:326
  3.2 0.2 collective-permute-start.2
  3.4 12.6 %all-to-all-start = ((bf16[16,72,128]{2,1,0:T(8,128)(2,1)}), bf16[16,72,128]{2,1,0:T(8,128)(2,1)S(1)}, u32[]{:S(2)}, u32[]{:S(2)}) async-start(bf16[16,72,128]{2,1,0:T(8,128)(2,1)} %shard_map.119), calls=%async_computation | async-start | bytes 589824 | tf_op jit(solution)/shard_map/all_to_all | solution.py:58
  16.0 1.9 %shard_map.120 = (bf16[32,128,128]{2,1,0:T(8,128)(2,1)S(1)}, bf16[32,128,128]{2,1,0:T(8,128)(2,1)S(1)}, bf16[128,2048]{1,0:T(8,128)(2,1)S(1)}, bf16[32,256]{1,0:...) custom-call(s32[4,32]{1,0:T(4,128)} %lengths_hbm, ...), custom_call_target="tpu_custom_call" | custom-call | flops 4194304 | bytes 4194304 | tf_op jit(solution)/shard_map/pallas_call | solution.py:333
  17.8 7.0 %all-to-all-done.own_ref = bf16[16,72,128]{2,1,0:T(8,128)(2,1)S(1)} async-done(((bf16[16,72,128]{2,1,0:T(8,128)(2,1)}), bf16[16,72,128]{2,1,0:T(8,128)(2,1)S(1)}, u32[]{:S(2)}, u32[]{:S(2)}) %all-to-all-start) | async-done | bytes 294944 | tf_op jit(solution)/shard_map/all_to_all | solution.py:58
  24.9 0.0 collective-permute-start.1
  24.9 0.0 collective-permute-done.2.wo_hbm
  24.9 1.4 %shard_map.121 = (bf16[8,2,256,128]{3,2,1,0:T(8,128)(2,1)S(1)}, bf16[128,2048]{1,0:T(8,128)(2,1)S(1)}) custom-call(bf16[2,8,2,2,128,128]{5,4,3,2,1,0:T(8,128)(2,1)} %bitcast.4, bf16[128,8192]{1,0:T(8,128)(2,1)} %collective-permute-done.2.wo_hbm), custom_call_target="tpu_custom_call" | custom-call | bytes 4194304 | tf_op jit(solution)/shard_map/pallas_call | solution.py:353
  26.3 0.1 collective-permute-done.1.other_ref
  26.5 0.3 shard_map.122
  26.8 10.0 %all_to_all.20.got_ref = bf16[8,104,128]{2,1,0:T(8,128)(2,1)S(1)} all-to-all(bf16[8,104,128]{2,1,0:T(8,128)(2,1)S(1)} %shard_map.122), channel_id=1, replica_groups={{64,96,0,32,192,224,128,160},{65,97,1,33,193,225,129,161},{194,226,130,..., dimensions={0} | all-to-all | bytes 425984 | tf_op jit(solution)/shard_map/all_to_all | solution.py:58
  36.8 1.0 %shard_map.123 = bf16[16,32,128]{2,1,0:T(8,128)(2,1)S(1)} custom-call(bf16[8,104,128]{2,1,0:T(8,128)(2,1)S(1)} %all_to_all.20.got_ref, bf16[32,128,128]{2,1,0:T(8,128)(2,1)S(1)} %get-tuple-element.56.keys_ref, bf16[32,128,128]{2,1,0:T(8,128)(2,1)S(1)} %get-tuple-element.57.values_ref, bf16[32,256]{1,0:T(8,128)(2,1)S(1)} %get-tuple-element.58.pick_ref, ...), custom_call_target="tpu_custom_call" | custom-call | flops 67108864 | bytes 4194304 | tf_op jit(solution)/shard_map/pallas_call | solution.py:364
  37.7 9.0 %all_to_all.21 = bf16[16,32,128]{2,1,0:T(8,128)(2,1)S(1)} all-to-all(bf16[16,32,128]{2,1,0:T(8,128)(2,1)S(1)} %shard_map.123), channel_id=1, replica_groups={{64,65,96,97,0,1,32,33,192,193,224,225,128,129,160,161},{194,195,226,22..., dimensions={0} | all-to-all | bytes 262144 | tf_op jit(solution)/shard_map/all_to_all | solution.py:58
  46.7 0.4 shard_map.124
  47.1 13.2 %all_to_all.22.got_ref = bf16[16,32,128]{2,1,0:T(8,128)(2,1)S(1)} all-to-all(bf16[16,32,128]{2,1,0:T(8,128)(2,1)S(1)} %shard_map.124), channel_id=1, replica_groups={{150,20,154,24,158,28,130,0,134,4,138,8,142,12,146,16},{151,21,155,25,1..., dimensions={0} | all-to-all | bytes 262144 | tf_op jit(solution)/shard_map/all_to_all | solution.py:58
  60.3 0.6 %shard_map.125 = bf16[1,32,128]{2,1,0:T(8,128)(2,1)} custom-call(bf16[16,32,128]{2,1,0:T(8,128)(2,1)S(1)} %all_to_all.22.got_ref), custom_call_target="tpu_custom_call" | custom-call | flops 131072 | bytes 262144 | tf_op jit(solution)/shard_map/pallas_call | solution.py:372
Async XLA Ops:
  1.2 1.3 %collective-permute-start = (bf16[32,512]{1,0:T(8,128)(2,1)S(1)}, bf16[32,512]{1,0:T(8,128)(2,1)S(1)}, u32[]{:S(2)}, u32[]{:S(2)}) collective-permute-start(bf16[32,512]{1,0:T(8,128)(2,1)S(1)} %get-tuple-element.38), channel_id=1, source_target_pairs={{0,1},{1,0},{2,3},{3,2},{4,5},{5,4},{6,7},{7,6},{8,9},{9,8},{10,11... | collective-permute-start | bytes 98312 | tf_op jit(solution)/shard_map/ppermute | solution.py:62
  3.2 21.6 %collective-permute-start.2 = (bf16[128,8192]{1,0:T(8,128)(2,1)}, bf16[128,8192]{1,0:T(8,128)(2,1)}, u32[]{:S(2)}, u32[]{:S(2)}) collective-permute-start(bf16[128,8192]{1,0:T(8,128)(2,1)} %wo_hbm), channel_id=1, source_target_pairs={{0,1},{1,0},{2,3},{3,2},{4,5},{5,4},{6,7},{7,6},{8,9},{9,8},{10,11... | collective-permute-start | bytes 6291464 | tf_op jit(solution)/shard_map/ppermute | solution.py:62
  3.4 21.5 %all-to-all-start = ((bf16[16,72,128]{2,1,0:T(8,128)(2,1)}), bf16[16,72,128]{2,1,0:T(8,128)(2,1)S(1)}, u32[]{:S(2)}, u32[]{:S(2)}) async-start(bf16[16,72,128]{2,1,0:T(8,128)(2,1)} %shard_map.119), calls=%async_computation | async-start | bytes 589824 | tf_op jit(solution)/shard_map/all_to_all | solution.py:58
  24.9 1.6 %collective-permute-start.1 = (bf16[16,72,128]{2,1,0:T(8,128)(2,1)S(1)}, bf16[16,72,128]{2,1,0:T(8,128)(2,1)S(1)}, u32[]{:S(2)}, u32[]{:S(2)}) collective-permute-start(bf16[16,72,128]{2,1,0:T(8,128)(2,1)S(1)} %all-to-all-done.own_ref), channel_id=1, source_target_pairs={{0,1},{1,0},{2,3},{3,2},{4,5},{5,4},{6,7},{7,6},{8,9},{9,8},{10,11... | collective-permute-start | bytes 884744 | tf_op jit(solution)/shard_map/ppermute | solution.py:62

commit v6 on v5

--- a/solution.py
+++ b/solution.py
@@ -42,9 +42,9 @@
 FIRST = 2
 HEADS_ALIKE = [(z, y, c) for z in range(ZS) for y in range(YS) for c in range(CORES)]
 TURNS = [(a, (i + FIRST) % INSTS) for a in range(POOLS) for i in range(INSTS)]
-HOSTS = [[device_number(a ^ y, i, z, y, c) for a, i in TURNS] for z, y, c in HEADS_ALIKE]
+HOSTS = [[device_number(1 ^ a ^ y, i, z, y, c) for a, i in TURNS] for z, y, c in HEADS_ALIKE]
 CHIPS = [
-    [device_number(a ^ y, i, z, y, c) for a, i in TURNS for c in range(CORES)]
+    [device_number(1 ^ a ^ y, i, z, y, c) for a, i in TURNS for c in range(CORES)]
     for z in range(ZS)
     for y in range(YS)
 ]
@@ -122,36 +122,24 @@
         out_ref[m, 2 * REQ :, :] = extra_ref[...]
 
 
-def output_columns(source, out):
-    core = lax.axis_index("core")
-    side = lax.axis_index("pool") ^ lax.axis_index("yh")
-    pairs = []
-    for m, (z, y) in enumerate(PLACES):
-        block = (((y ^ side) * ZS + z) * YS + y) * CORES + core
-        lanes = pl.ds(pl.multiple_of(block * HD, HD), HD)
-        pairs.append((source.at[:, lanes], out.at[:, pl.ds(m * HD, HD)]))
-    return pairs
-
-
-def early_kernel(
-    lengths_hbm, offload_hbm, host_hbm, slot_hbm, keys_hbm, values_hbm, wo_hbm,
-    keys_out, values_out, wo_out, pick_ref, back_ref, cos_ref, sin_ref, span_ref,
+def tables_kernel(
+    lengths_hbm, offload_hbm, host_hbm, slot_hbm, values_hbm,
+    values_out, pick_ref, back_ref, cos_ref, sin_ref, span_ref,
     lengths_ref, offload_ref, host_ref, slot_ref, sems,
 ):
-    pool, inst, z = lax.axis_index("pool"), lax.axis_index("inst"), lax.axis_index("z")
+    pool, inst = lax.axis_index("pool"), lax.axis_index("inst")
     pairs = [(lengths_hbm, lengths_ref), (offload_hbm, offload_ref), (host_hbm, host_ref), (slot_hbm, slot_ref)]
     small = len(pairs)
-    pairs.append((keys_hbm.at[0, 0, :, :, head_lanes(z)], keys_out))
-    pairs.append((values_hbm.at[0, 0, :, :, head_lanes(z)], values_out))
-    copies = start_copies(pairs + output_columns(wo_hbm, wo_out), sems)
+    pairs.append((values_hbm.at[0, 0, :, :, head_lanes(lax.axis_index("z"))], values_out))
+    copies = start_copies(pairs, sems)
     for copy in copies[:small]:
         copy.wait()
     yh = lax.axis_index("yh")
-    home = yh * (INSTS * REQ) + turn(iota((INSTS, REQ), 0)) * REQ + iota((INSTS, REQ), 1)
-    away = (1 - yh) * (INSTS * REQ) + turn(host_ref[...]) * REQ + slot_ref[...]
+    home = (1 - yh) * (INSTS * REQ) + turn(iota((INSTS, REQ), 0)) * REQ + iota((INSTS, REQ), 1)
+    away = yh * (INSTS * REQ) + turn(host_ref[...]) * REQ + slot_ref[...]
     seat = jnp.where(offload_ref[...] == 1, away, home)
     spans = lengths_ref[...].astype(F32)
-    here = iota((REQ, REQ), 0) + ((pool ^ yh) * INSTS + turn(inst)) * REQ
+    here = iota((REQ, REQ), 0) + ((1 ^ pool ^ yh) * INSTS + turn(inst)) * REQ
     square = iota((REQ, REQ), 0) == iota((REQ, REQ), 1)
     pick = jnp.zeros((REQ, POOLS * INSTS * REQ), F32)
     span = jnp.zeros((REQ, 1), F32)
@@ -178,29 +166,21 @@
         copy.wait()
 
 
-def late_kernel(wq_hbm, wo_hbm, wq_out, wo_out, sems):
+def query_kernel(own_ref, other_ref, wq_ref, out_ref):
     core = lax.axis_index("core")
     side = lax.axis_index("pool") ^ lax.axis_index("yh")
-    pairs = []
-    for y in range(YS):
-        for n, c in enumerate((core, 1 - core)):
-            pairs.append((wq_hbm.at[y ^ side, :, y, c], wq_out.at[:, y, pl.ds(n * HD, HD), :]))
-    for copy in start_copies(pairs + output_columns(wo_hbm, wo_out), sems):
-        copy.wait()
-
-
-def query_kernel(own_ref, other_ref, wq_ref, out_ref):
     q = jnp.zeros((REQ, HD), F32)
     own = jnp.zeros((REQ, HD), F32)
     other = jnp.zeros((REQ, HD), F32)
     extra = jnp.zeros((EXTRA, HD), F32)
-    for m, place in enumerate(PLACES):
+    for m, (z, y) in enumerate(PLACES):
+        weight = jnp.concatenate([wq_ref[y ^ side, z, y, c] for c in (core, 1 - core)], axis=0)
         features = jnp.concatenate([own_ref[m, 0:REQ, :], other_ref[m, 0:REQ, :]], axis=1)
-        q += dot(features, wq_ref[place])
+        q += dot(features, weight)
         own += own_ref[m, REQ : 2 * REQ, :].astype(F32)
         other += other_ref[m, REQ : 2 * REQ, :].astype(F32)
         extra += own_ref[m, 2 * REQ :, :].astype(F32) + other_ref[m, 2 * REQ :, :].astype(F32)
-    first = lax.axis_index("core") == 0
+    first = core == 0
     k, v = jnp.where(first, own, other), jnp.where(first, other, own)
     rest = two_rows(extra[0:1] + extra[1:2])
     for m in range(POOLS * INSTS):
@@ -224,7 +204,8 @@
     q = rotate(q / root).astype(BF)
     k = rotate(k / root).astype(BF)
     v = (v / root).astype(BF)
-    keys = keys_ref[...].reshape(REQ * HD, HD)
+    lanes = head_lanes(lax.axis_index("z"))
+    keys = keys_ref[0, 0, :, :, lanes].reshape(REQ * HD, HD)
     values = values_ref[...].reshape(REQ * HD, HD)
     every = lax.dot_general(q, keys, (((1,), (1,)), ((), ())), preferred_element_type=F32)
     request = iota((8, HD), 0)
@@ -259,9 +240,14 @@
     seats = POOLS * INSTS * REQ
     mine = dot(back, got_ref[:, core].reshape(seats, HD)).astype(BF)
     buddy = dot(back, got_ref[:, 1 - core].reshape(seats, HD)).astype(BF)
-    result = (dot(mine, own_ref[...]) + dot(buddy, other_ref[...])).astype(BF)
-    for m in range(RING):
-        out_ref[m] = result[:, m * HD : (m + 1) * HD]
+    side = lax.axis_index("pool") ^ lax.axis_index("yh")
+    parts = []
+    for z, y in PLACES:
+        block = (((y ^ side) * ZS + z) * YS + y) * CORES + core
+        lanes = pl.ds(pl.multiple_of(block * HD, HD), HD)
+        parts.append((dot(mine, own_ref[:, lanes]) + dot(buddy, other_ref[:, lanes])).astype(BF))
+    for m, part in enumerate(parts):
+        out_ref[m] = part
 
 
 def sum_kernel(got_ref, out_ref):
@@ -326,47 +312,45 @@
     message = call(message_kernel, shape(RING, 2 * REQ + EXTRA, HD), [VMEM] * 4, 1 << 14, 1 << 19)(
         scaled, extra, keep, swap_core(give)
     )
-    message, lengths, output_weight = lax.optimization_barrier((message, lengths, output_weight))
+    message, output_weight = lax.optimization_barrier((message, output_weight))
     buddy_weight = swap_core(output_weight)
     got = exchange(message, RINGS)
+    got, lengths, key_cache = lax.optimization_barrier((got, lengths, key_cache))
+    other = swap_core(got)
     table = pltpu.VMEM(lengths.shape, I32)
-    early = call(
-        early_kernel,
+    tables = call(
+        tables_kernel,
         [
             shape(REQ, HD, HD),
-            shape(REQ, HD, HD),
-            shape(HD, RING * HD),
             shape(REQ, seats),
             shape(REQ, seats),
             shape(REQ, HD, dtype=F32),
             shape(REQ, HD, dtype=F32),
             shape(REQ, HD, dtype=F32),
         ],
-        [HBM] * 7,
+        [HBM] * 5,
         1 << 22,
         1 << 22,
-        [table] * 4 + [pltpu.SemaphoreType.DMA((6 + RING,))],
-    )(*in_hbm(lengths, offload, host_instance, cache_slot, key_cache, value_cache, output_weight))
-    got, early, query_weight = lax.optimization_barrier((got, early, query_weight))
-    keys, values, keep, pick, back, cos, sin, span = early
-    other = swap_core(got)
-    late = call(
-        late_kernel,
-        [shape(ZS, YS, CORES * HD, HD), shape(HD, RING * HD)],
-        [HBM] * 2,
-        0,
-        1 << 22,
-        [pltpu.SemaphoreType.DMA((2 * YS + RING,))],
-    )(*in_hbm(query_weight.reshape(POOLS, ZS, YS, CORES, HD, HD), buddy_weight))
-    other, (wq, taken) = lax.optimization_barrier((other, late))
-    message = call(query_kernel, shape(POOLS * INSTS, 3 * REQ + EXTRA, HD), [VMEM] * 3, 1 << 25, 1 << 22)(got, other, wq)
+        [table] * 4 + [pltpu.SemaphoreType.DMA((5,))],
+    )(
+        *in_hbm(
+            lengths,
+            offload,
+            host_instance,
+            cache_slot,
+            value_cache,
+        )
+    )
+    other, tables, buddy_weight = lax.optimization_barrier((other, tables, buddy_weight))
+    values, pick, back, cos, sin, span = tables
+    message = call(query_kernel, shape(POOLS * INSTS, 3 * REQ + EXTRA, HD), [VMEM] * 3, 1 << 25, 1 << 22)(got, other, query_weight.reshape(POOLS, ZS, YS, CORES, HD, HD))
     got = exchange(message, HOSTS)
     message = call(
         functools.partial(attend_kernel, width=width), shape(POOLS * INSTS * CORES, REQ, HD), [VMEM] * 7, 1 << 26, 1 << 22
-    )(got, keys, values, pick, cos, sin, span)
+    )(got, key_cache, values, pick, cos, sin, span)
     got = exchange(message, CHIPS)
     message = call(output_kernel, shape(RING, REQ, HD), [VMEM] * 4, 1 << 25, 1 << 22)(
-        got.reshape(POOLS * INSTS, CORES, REQ, HD), back, keep, taken
+        got.reshape(POOLS * INSTS, CORES, REQ, HD), back, output_weight, buddy_weight
     )
     got = exchange(message, RINGS)
     return call(sum_kernel, shape(1, REQ, HD), [VMEM], 1 << 17, 1 << 18)(got)

time: 61.5 us -> 59.7 us (0.971)
  blocking collectives: 32.2 us -> 52.3 us
  starting transfers between devices: 12.8 us -> 0.34 us
  waiting for transfers between devices: 8.37 us -> 1.28 us
  Pallas kernels: 7.5 us -> 5.09 us
    all_to_all x3 -> x4, blocking collectives: 32.2 us -> 52.3 us  [exchange(): return lax.all_to_all(x, AXES, 0, 0, axis_index_groups=groups, tiled=True)]
    all_to_all x1 -> x0, starting transfers between devices: 12.6 us -> none  [exchange(): return lax.all_to_all(x, AXES, 0, 0, axis_index_groups=groups, tiled=True)]
    all_to_all x1 -> x0, waiting for transfers between devices: 7.04 us -> none  [exchange(): return lax.all_to_all(x, AXES, 0, 0, axis_index_groups=groups, tiled=True)]
    pallas_call x2 -> x1, Pallas kernels: 3.29 us -> 1.48 us  [shards(): call(tables_kernel, [shape(REQ, HD, HD), shape(REQ, seats), shape(REQ, se...]
    pallas_call x1, Pallas kernels: 0.74 us -> 0.03 us  [shards(): call(message_kernel, shape(RING, 2 * REQ + EXTRA, HD), [VMEM] * 4, 1 << 1...]
  transfers between devices with their start and end apart: 4 -> 3, of which waited for: 3 -> 2; matrix products, arithmetic and copies ran while one was open for 0% -> 0% of each run, Pallas kernels for 5% -> 2%
where the time goes in v6:
time: 59.7 us; the launch traced here: 59.5 us
  blocking collectives  52.3 us (88%)
  Pallas kernels  5.09 us (9%)
  waiting for transfers between devices  1.28 us (2%)
    all_to_all x4, blocking collectives, exchange(): return lax.all_to_all(x, AXES, 0, 0, axis_index_groups=groups, tiled=True)  52.3 us
    pallas_call x1, Pallas kernels, shards(): call(tables_kernel, [shape(REQ, HD, HD), shape(REQ, seats), shape(REQ, se...  1.48 us
    ppermute x3, waiting for transfers between devices, swap_core(): return lax.ppermute(x, 'core', [(0, 1), (1, 0)])  1.28 us
    pallas_call x1, Pallas kernels, shards(): call(features_kernel, [shape(REQ, HD), shape(EXTRA, HD), shape(REQ, HEADS...  1.2 us
  transfers between devices with their start and end apart: 3, of which 2 were waited for; matrix products, arithmetic and copies ran while one was open for 0% of the time, Pallas kernels for 2%

profile of v6, /device:TPU:2, one launch (start us, length us, event | category | flops | bytes accessed | tf_op | source)
XLA Modules:
  0.0 59.5 jit_solution(3362489736118483794)
XLA Ops:
  0.0 1.2 %shard_map.118 = (bf16[32,128]{1,0:T(8,128)(2,1)S(1)}, bf16[8,128]{1,0:T(8,128)(2,1)S(1)}, bf16[32,512]{1,0:T(8,128)(2,1)S(1)}, bf16[32,512]{1,0:T(8,128)(2,1)S(1)}) custom-call(bf16[1,32,128]{2,1,0:T(8,128)(2,1)} %x_hbm.1, bf16[1,128]{1,0:T(2,128)(2,1)} %bitcast.5, bf16[128,512]{1,0:T(8,128)(2,1)} %wk_hbm.1, bf16[128,512]{1,0:T(8,128)(2,1)} %wv_hbm.1), custom_call_target="tpu_custom_call" | custom-call | flops 8388608 | bytes 1048576 | tf_op jit(solution)/shard_map/pallas_call | solution.py:298
  1.2 0.1 collective-permute-start
  1.3 1.2 %collective-permute-done.taken_ref = bf16[32,512]{1,0:T(8,128)(2,1)S(1)} collective-permute-done((bf16[32,512]{1,0:T(8,128)(2,1)S(1)}, bf16[32,512]{1,0:T(8,128)(2,1)S(1)}, u32[]{:S(2)}, u32[]{:S(2)}) %collective-permute-start) | collective-permute-done | bytes 32800 | tf_op jit(solution)/shard_map/ppermute | solution.py:62
  2.5 0.2 collective-permute-start.2
  2.8 20.5 %all_to_all.20.own_ref = bf16[16,72,128]{2,1,0:T(8,128)(2,1)S(1)} all-to-all(bf16[16,72,128]{2,1,0:T(8,128)(2,1)S(1)} %shard_map.119), channel_id=1, replica_groups={{150,20,154,24,158,28,130,0,134,4,138,8,142,12,146,16},{151,21,155,25,1..., dimensions={0} | all-to-all | bytes 589824 | tf_op jit(solution)/shard_map/all_to_all | solution.py:58
  23.3 0.0 copy-start.1
  23.3 0.0 collective-permute-start.1
  23.3 0.0 copy-start
  23.3 1.5 %shard_map.120 = (bf16[32,128,128]{2,1,0:T(8,128)(2,1)S(1)}, bf16[32,256]{1,0:T(8,128)(2,1)S(1)}, bf16[32,256]{1,0:T(8,128)(2,1)S(1)}, f32[32,128]{1,0:T(8,128)S...) custom-call(s32[4,32]{1,0:T(4,128)} %lengths_hbm, s32[4,32]{1,0:T(4,128)} %offload_hbm.1, s32[4,32]{1,0:T(4,128)} %host_hbm.1, ...), custom_call_target="tpu_custom_call" | custom-call | flops 4194304 | bytes 4194304 | tf_op jit(solution)/shard_map/pallas_call | solution.py:321
  24.8 0.1 collective-permute-done.1.other_ref
  24.9 0.0 collective-permute-done.2.other_ref
  24.9 0.4 copy-done.1
  25.3 0.3 shard_map.121
  25.6 9.6 %all_to_all.21.got_ref = bf16[8,104,128]{2,1,0:T(8,128)(2,1)S(1)} all-to-all(bf16[8,104,128]{2,1,0:T(8,128)(2,1)S(1)} %shard_map.121), channel_id=1, replica_groups={{192,224,128,160,64,96,0,32},{193,225,129,161,65,97,1,33},{66,98,2,34,1..., dimensions={0} | all-to-all | bytes 425984 | tf_op jit(solution)/shard_map/all_to_all | solution.py:58
  35.2 0.0 copy-done
  35.2 0.0 copy-start.2
  35.2 1.0 %shard_map.122 = bf16[16,32,128]{2,1,0:T(8,128)(2,1)S(1)} custom-call(bf16[8,104,128]{2,1,0:T(8,128)(2,1)S(1)} %all_to_all.21.got_ref, bf16[1,1,32,128,512]{4,3,2,1,0:T(8,128)(2,1)S(1)} %copy-done, bf16[32,128,128]{2,1,0:T(8,128)(2,1)S(1)} %get-tuple-element.44.values_ref, bf16[32,256]{1,0:T(8,128)(2,1)S(1)} %get-tuple-element.45.pick_ref, ...), custom_call_target="tpu_custom_call" | custom-call | flops 67108864 | bytes 4194304 | tf_op jit(solution)/shard_map/pallas_call | solution.py:348
  36.2 9.2 %all_to_all.22 = bf16[16,32,128]{2,1,0:T(8,128)(2,1)S(1)} all-to-all(bf16[16,32,128]{2,1,0:T(8,128)(2,1)S(1)} %shard_map.122), channel_id=1, replica_groups={{192,193,224,225,128,129,160,161,64,65,96,97,0,1,32,33},{66,67,98,99,2,..., dimensions={0} | all-to-all | bytes 262144 | tf_op jit(solution)/shard_map/all_to_all | solution.py:58
  45.5 0.0 copy-done.2
  45.5 0.5 shard_map.123
  46.0 12.9 %all_to_all.23.got_ref = bf16[16,32,128]{2,1,0:T(8,128)(2,1)S(1)} all-to-all(bf16[16,32,128]{2,1,0:T(8,128)(2,1)S(1)} %shard_map.123), channel_id=1, replica_groups={{150,20,154,24,158,28,130,0,134,4,138,8,142,12,146,16},{151,21,155,25,1..., dimensions={0} | all-to-all | bytes 262144 | tf_op jit(solution)/shard_map/all_to_all | solution.py:58
  58.8 0.6 %shard_map.124 = bf16[1,32,128]{2,1,0:T(8,128)(2,1)} custom-call(bf16[16,32,128]{2,1,0:T(8,128)(2,1)S(1)} %all_to_all.23.got_ref), custom_call_target="tpu_custom_call" | custom-call | flops 131072 | bytes 262144 | tf_op jit(solution)/shard_map/pallas_call | solution.py:356
  (1 shorter events, 0.0 us)
Async XLA Ops:
  1.2 1.3 %collective-permute-start = (bf16[32,512]{1,0:T(8,128)(2,1)S(1)}, bf16[32,512]{1,0:T(8,128)(2,1)S(1)}, u32[]{:S(2)}, u32[]{:S(2)}) collective-permute-start(bf16[32,512]{1,0:T(8,128)(2,1)S(1)} %get-tuple-element.31), channel_id=1, source_target_pairs={{0,1},{1,0},{2,3},{3,2},{4,5},{5,4},{6,7},{7,6},{8,9},{9,8},{10,11... | collective-permute-start | bytes 98312 | tf_op jit(solution)/shard_map/ppermute | solution.py:62
  2.5 22.4 %collective-permute-start.2 = (bf16[128,8192]{1,0:T(8,128)(2,1)}, bf16[128,8192]{1,0:T(8,128)(2,1)S(1)}, u32[]{:S(2)}, u32[]{:S(2)}) collective-permute-start(bf16[128,8192]{1,0:T(8,128)(2,1)} %own_ref), channel_id=1, source_target_pairs={{0,1},{1,0},{2,3},{3,2},{4,5},{5,4},{6,7},{7,6},{8,9},{9,8},{10,11... | collective-permute-start | bytes 6291464 | tf_op jit(solution)/shard_map/ppermute | solution.py:62
  23.3 2.0 %copy-start.1 = (bf16[8192,128]{1,0:T(8,128)(2,1)S(1)}, bf16[8192,128]{1,0:T(8,128)(2,1)}, u32[]{:S(2)}) copy-start(bf16[8192,128]{1,0:T(8,128)(2,1)} %param.14) | copy-start | bytes 6291460
  23.3 1.6 %collective-permute-start.1 = (bf16[16,72,128]{2,1,0:T(8,128)(2,1)S(1)}, bf16[16,72,128]{2,1,0:T(8,128)(2,1)S(1)}, u32[]{:S(2)}, u32[]{:S(2)}) collective-permute-start(bf16[16,72,128]{2,1,0:T(8,128)(2,1)S(1)} %all_to_all.20.own_ref), channel_id=1, source_target_pairs={{0,1},{1,0},{2,3},{3,2},{4,5},{5,4},{6,7},{7,6},{8,9},{9,8},{10,11... | collective-permute-start | bytes 884744 | tf_op jit(solution)/shard_map/ppermute | solution.py:62
  23.3 11.9 %copy-start = (bf16[1,1,32,128,512]{4,3,2,1,0:T(8,128)(2,1)S(1)}, bf16[1,1,32,128,512]{4,3,2,1,0:T(8,128)(2,1)}, u32[]{:S(2)}) copy-start(bf16[1,1,32,128,512]{4,3,2,1,0:T(8,128)(2,1)} %keys_ref) | copy-start | bytes 12582916
  35.2 10.2 %copy-start.2 = (bf16[128,8192]{1,0:T(8,128)(2,1)S(1)}, bf16[128,8192]{1,0:T(8,128)(2,1)}, u32[]{:S(2)}) copy-start(bf16[128,8192]{1,0:T(8,128)(2,1)} %own_ref) | copy-start | bytes 6291460

commit v7 on v6

--- a/solution.py
+++ b/solution.py
@@ -201,8 +201,8 @@
     def rotate(t):
         return t * cos_ref[...] + pltpu.roll(t, HD // 2, 1) * sin_ref[...]
 
-    q = rotate(q / root).astype(BF)
-    k = rotate(k / root).astype(BF)
+    q = rotate(q).astype(BF)
+    k = rotate(k).astype(BF)
     v = (v / root).astype(BF)
     lanes = head_lanes(lax.axis_index("z"))
     keys = keys_ref[0, 0, :, :, lanes].reshape(REQ * HD, HD)
@@ -216,20 +216,20 @@
             r = group * 8 + n
             block = jnp.where(request == n, every[group * 8 : group * 8 + 8, r * HD : (r + 1) * HD], block)
         rows.append(block)
-    factor = HD ** (-0.5)
-    scores = jnp.concatenate(rows, axis=0) * factor
-    own_score = jnp.sum(q.astype(F32) * k.astype(F32), axis=1, keepdims=True) * factor
+    scale = HD ** (-0.5) / root
+    scores = jnp.concatenate(rows, axis=0) * scale
+    own_score = jnp.sum(q.astype(F32) * k.astype(F32), axis=1, keepdims=True) * (scale / root)
     visible = iota((REQ, HD), 1).astype(F32) < span_ref[...]
     scores = jnp.where(visible, scores, -jnp.inf)
-    peak = jnp.maximum(jnp.max(scores, axis=1, keepdims=True), own_score)
+    peak = jnp.maximum(jnp.max(scores, axis=1, keepdims=True), -1e30)
     exps = jnp.exp(scores - peak)
-    own_exp = jnp.exp(own_score - peak)
-    total = jnp.sum(exps, axis=1, keepdims=True) + own_exp
-    weights = exps / total
-    own_weight = (own_exp / total).astype(BF).astype(F32)
     request = iota((REQ, HD), 0)
-    spread = jnp.concatenate([jnp.where(request == r, weights, 0.0).astype(BF) for r in range(REQ)], axis=1)
-    mixed = (dot(spread, values) + own_weight * v.astype(F32)).astype(BF)
+    spread = jnp.concatenate([jnp.where(request == r, exps, 0.0).astype(BF) for r in range(REQ)], axis=1)
+    mixed = dot(spread, values)
+    top = jnp.maximum(peak, own_score)
+    cached, own = jnp.exp(peak - top), jnp.exp(own_score - top)
+    total = jnp.sum(exps, axis=1, keepdims=True) * cached + own
+    mixed = (mixed * (cached / total) + (own / total) * v.astype(F32)).astype(BF)
     for m in range(POOLS * INSTS * CORES):
         out_ref[m] = mixed
 
@@ -241,11 +241,16 @@
     mine = dot(back, got_ref[:, core].reshape(seats, HD)).astype(BF)
     buddy = dot(back, got_ref[:, 1 - core].reshape(seats, HD)).astype(BF)
     side = lax.axis_index("pool") ^ lax.axis_index("yh")
+    rows = jnp.concatenate([mine, buddy], axis=1)
     parts = []
-    for z, y in PLACES:
-        block = (((y ^ side) * ZS + z) * YS + y) * CORES + core
-        lanes = pl.ds(pl.multiple_of(block * HD, HD), HD)
-        parts.append((dot(mine, own_ref[:, lanes]) + dot(buddy, other_ref[:, lanes])).astype(BF))
+    for m in range(0, RING, 2):
+        weights = []
+        for z, y in PLACES[m : m + 2]:
+            block = (((y ^ side) * ZS + z) * YS + y) * CORES + core
+            lanes = pl.ds(pl.multiple_of(block * HD, HD), HD)
+            weights.append(jnp.concatenate([own_ref[:, lanes], other_ref[:, lanes]], axis=0))
+        two = dot(rows, jnp.concatenate(weights, axis=1)).astype(BF)
+        parts += [two[:, :HD], two[:, HD:]]
     for m, part in enumerate(parts):
         out_ref[m] = part
 

time: 59.7 us -> 59.6 us (level)
  no operation moved by 1% of the time
where the time goes in v7:
time: 59.6 us; the launch traced here: 59.4 us
  blocking collectives  52.3 us (88%)
  Pallas kernels  4.97 us (8%)
  waiting for transfers between devices  1.28 us (2%)
    all_to_all x4, blocking collectives, exchange(): return lax.all_to_all(x, AXES, 0, 0, axis_index_groups=groups, tiled=True)  52.3 us
    pallas_call x1, Pallas kernels, shards(): call(tables_kernel, [shape(REQ, HD, HD), shape(REQ, seats), shape(REQ, se...  1.48 us
    ppermute x3, waiting for transfers between devices, swap_core(): return lax.ppermute(x, 'core', [(0, 1), (1, 0)])  1.28 us
    pallas_call x1, Pallas kernels, shards(): call(features_kernel, [shape(REQ, HD), shape(EXTRA, HD), shape(REQ, HEADS...  1.2 us
  transfers between devices with their start and end apart: 3, of which 2 were waited for; matrix products, arithmetic and copies ran while one was open for 0% of the time, Pallas kernels for 2%

profile of v7, /device:TPU:2, one launch (start us, length us, event | category | flops | bytes accessed | tf_op | source)
XLA Modules:
  0.0 59.4 jit_solution(4247189270058088859)
XLA Ops:
  0.0 1.2 %shard_map.118 = (bf16[32,128]{1,0:T(8,128)(2,1)S(1)}, bf16[8,128]{1,0:T(8,128)(2,1)S(1)}, bf16[32,512]{1,0:T(8,128)(2,1)S(1)}, bf16[32,512]{1,0:T(8,128)(2,1)S(1)}) custom-call(bf16[1,32,128]{2,1,0:T(8,128)(2,1)} %x_hbm.1, bf16[1,128]{1,0:T(2,128)(2,1)} %bitcast.5, bf16[128,512]{1,0:T(8,128)(2,1)} %wk_hbm.1, bf16[128,512]{1,0:T(8,128)(2,1)} %wv_hbm.1), custom_call_target="tpu_custom_call" | custom-call | flops 8388608 | bytes 1048576 | tf_op jit(solution)/shard_map/pallas_call | solution.py:303
  1.2 0.1 collective-permute-start
  1.3 1.2 %collective-permute-done.taken_ref = bf16[32,512]{1,0:T(8,128)(2,1)S(1)} collective-permute-done((bf16[32,512]{1,0:T(8,128)(2,1)S(1)}, bf16[32,512]{1,0:T(8,128)(2,1)S(1)}, u32[]{:S(2)}, u32[]{:S(2)}) %collective-permute-start) | collective-permute-done | bytes 32800 | tf_op jit(solution)/shard_map/ppermute | solution.py:62
  2.5 0.2 collective-permute-start.2
  2.8 20.5 %all_to_all.20.own_ref = bf16[16,72,128]{2,1,0:T(8,128)(2,1)S(1)} all-to-all(bf16[16,72,128]{2,1,0:T(8,128)(2,1)S(1)} %shard_map.119), channel_id=1, replica_groups={{150,20,154,24,158,28,130,0,134,4,138,8,142,12,146,16},{151,21,155,25,1..., dimensions={0} | all-to-all | bytes 589824 | tf_op jit(solution)/shard_map/all_to_all | solution.py:58
  23.3 0.0 copy-start.1
  23.3 0.0 collective-permute-start.1
  23.3 0.0 copy-start
  23.3 1.5 %shard_map.120 = (bf16[32,128,128]{2,1,0:T(8,128)(2,1)S(1)}, bf16[32,256]{1,0:T(8,128)(2,1)S(1)}, bf16[32,256]{1,0:T(8,128)(2,1)S(1)}, f32[32,128]{1,0:T(8,128)S...) custom-call(s32[4,32]{1,0:T(4,128)} %lengths_hbm, s32[4,32]{1,0:T(4,128)} %offload_hbm.1, s32[4,32]{1,0:T(4,128)} %host_hbm.1, ...), custom_call_target="tpu_custom_call" | custom-call | flops 4194304 | bytes 4194304 | tf_op jit(solution)/shard_map/pallas_call | solution.py:326
  24.8 0.1 collective-permute-done.1.other_ref
  24.9 0.0 collective-permute-done.2.other_ref
  24.9 0.4 copy-done.1
  25.3 0.3 shard_map.121
  25.6 9.6 %all_to_all.21.got_ref = bf16[8,104,128]{2,1,0:T(8,128)(2,1)S(1)} all-to-all(bf16[8,104,128]{2,1,0:T(8,128)(2,1)S(1)} %shard_map.121), channel_id=1, replica_groups={{192,224,128,160,64,96,0,32},{193,225,129,161,65,97,1,33},{66,98,2,34,1..., dimensions={0} | all-to-all | bytes 425984 | tf_op jit(solution)/shard_map/all_to_all | solution.py:58
  35.2 0.0 copy-done
  35.2 0.0 copy-start.2
  35.2 0.9 %shard_map.122 = bf16[16,32,128]{2,1,0:T(8,128)(2,1)S(1)} custom-call(bf16[8,104,128]{2,1,0:T(8,128)(2,1)S(1)} %all_to_all.21.got_ref, bf16[1,1,32,128,512]{4,3,2,1,0:T(8,128)(2,1)S(1)} %copy-done, bf16[32,128,128]{2,1,0:T(8,128)(2,1)S(1)} %get-tuple-element.44.values_ref, bf16[32,256]{1,0:T(8,128)(2,1)S(1)} %get-tuple-element.45.pick_ref, ...), custom_call_target="tpu_custom_call" | custom-call | flops 67108864 | bytes 4194304 | tf_op jit(solution)/shard_map/pallas_call | solution.py:353
  36.1 9.3 %all_to_all.22 = bf16[16,32,128]{2,1,0:T(8,128)(2,1)S(1)} all-to-all(bf16[16,32,128]{2,1,0:T(8,128)(2,1)S(1)} %shard_map.122), channel_id=1, replica_groups={{192,193,224,225,128,129,160,161,64,65,96,97,0,1,32,33},{66,67,98,99,2,..., dimensions={0} | all-to-all | bytes 262144 | tf_op jit(solution)/shard_map/all_to_all | solution.py:58
  45.4 0.0 copy-done.2
  45.4 0.4 shard_map.123
  45.8 12.9 %all_to_all.23.got_ref = bf16[16,32,128]{2,1,0:T(8,128)(2,1)S(1)} all-to-all(bf16[16,32,128]{2,1,0:T(8,128)(2,1)S(1)} %shard_map.123), channel_id=1, replica_groups={{150,20,154,24,158,28,130,0,134,4,138,8,142,12,146,16},{151,21,155,25,1..., dimensions={0} | all-to-all | bytes 262144 | tf_op jit(solution)/shard_map/all_to_all | solution.py:58
  58.7 0.6 %shard_map.124 = bf16[1,32,128]{2,1,0:T(8,128)(2,1)} custom-call(bf16[16,32,128]{2,1,0:T(8,128)(2,1)S(1)} %all_to_all.23.got_ref), custom_call_target="tpu_custom_call" | custom-call | flops 131072 | bytes 262144 | tf_op jit(solution)/shard_map/pallas_call | solution.py:361
  (1 shorter events, 0.0 us)
Async XLA Ops:
  1.2 1.3 %collective-permute-start = (bf16[32,512]{1,0:T(8,128)(2,1)S(1)}, bf16[32,512]{1,0:T(8,128)(2,1)S(1)}, u32[]{:S(2)}, u32[]{:S(2)}) collective-permute-start(bf16[32,512]{1,0:T(8,128)(2,1)S(1)} %get-tuple-element.31), channel_id=1, source_target_pairs={{0,1},{1,0},{2,3},{3,2},{4,5},{5,4},{6,7},{7,6},{8,9},{9,8},{10,11... | collective-permute-start | bytes 98312 | tf_op jit(solution)/shard_map/ppermute | solution.py:62
  2.5 22.4 %collective-permute-start.2 = (bf16[128,8192]{1,0:T(8,128)(2,1)}, bf16[128,8192]{1,0:T(8,128)(2,1)S(1)}, u32[]{:S(2)}, u32[]{:S(2)}) collective-permute-start(bf16[128,8192]{1,0:T(8,128)(2,1)} %own_ref), channel_id=1, source_target_pairs={{0,1},{1,0},{2,3},{3,2},{4,5},{5,4},{6,7},{7,6},{8,9},{9,8},{10,11... | collective-permute-start | bytes 6291464 | tf_op jit(solution)/shard_map/ppermute | solution.py:62
  23.3 2.0 %copy-start.1 = (bf16[8192,128]{1,0:T(8,128)(2,1)S(1)}, bf16[8192,128]{1,0:T(8,128)(2,1)}, u32[]{:S(2)}) copy-start(bf16[8192,128]{1,0:T(8,128)(2,1)} %param.14) | copy-start | bytes 6291460
  23.3 1.6 %collective-permute-start.1 = (bf16[16,72,128]{2,1,0:T(8,128)(2,1)S(1)}, bf16[16,72,128]{2,1,0:T(8,128)(2,1)S(1)}, u32[]{:S(2)}, u32[]{:S(2)}) collective-permute-start(bf16[16,72,128]{2,1,0:T(8,128)(2,1)S(1)} %all_to_all.20.own_ref), channel_id=1, source_target_pairs={{0,1},{1,0},{2,3},{3,2},{4,5},{5,4},{6,7},{7,6},{8,9},{9,8},{10,11... | collective-permute-start | bytes 884744 | tf_op jit(solution)/shard_map/ppermute | solution.py:62
  23.3 11.9 %copy-start = (bf16[1,1,32,128,512]{4,3,2,1,0:T(8,128)(2,1)S(1)}, bf16[1,1,32,128,512]{4,3,2,1,0:T(8,128)(2,1)}, u32[]{:S(2)}) copy-start(bf16[1,1,32,128,512]{4,3,2,1,0:T(8,128)(2,1)} %keys_ref) | copy-start | bytes 12582916
  35.2 10.2 %copy-start.2 = (bf16[128,8192]{1,0:T(8,128)(2,1)S(1)}, bf16[128,8192]{1,0:T(8,128)(2,1)}, u32[]{:S(2)}) copy-start(bf16[128,8192]{1,0:T(8,128)(2,1)} %own_ref) | copy-start | bytes 6291460

commit v8 on v7

--- a/solution.py
+++ b/solution.py
@@ -13,7 +13,7 @@
 REQ = 32
 POOLS, INSTS, ZS, YS, CORES = 2, 4, 8, 2, 2
 RING = ZS * POOLS
-EXTRA = 8
+EXTRA = 16
 epsilon = 1e-05
 rope_base = 500000.0
 AXES = ("pool", "inst", "z", "yh", "core")

time: 59.6 us -> 60.5 us (1.015)
  blocking collectives: 52.3 us -> 53.2 us
    all_to_all x4, blocking collectives: 52.3 us -> 53.2 us  [exchange(): return lax.all_to_all(x, AXES, 0, 0, axis_index_groups=groups, tiled=True)]
where the time goes in v8:
time: 60.5 us; the launch traced here: 60.2 us
  blocking collectives  53.2 us (88%)
  Pallas kernels  4.98 us (8%)
  waiting for transfers between devices  1.33 us (2%)
    all_to_all x4, blocking collectives, exchange(): return lax.all_to_all(x, AXES, 0, 0, axis_index_groups=groups, tiled=True)  53.2 us
    pallas_call x1, Pallas kernels, shards(): call(tables_kernel, [shape(REQ, HD, HD), shape(REQ, seats), shape(REQ, se...  1.48 us
    ppermute x3, waiting for transfers between devices, swap_core(): return lax.ppermute(x, 'core', [(0, 1), (1, 0)])  1.33 us
  transfers between devices with their start and end apart: 3, of which 2 were waited for; matrix products, arithmetic and copies ran while one was open for 0% of the time, Pallas kernels for 2%

profile of v8, /device:TPU:2, one launch (start us, length us, event | category | flops | bytes accessed | tf_op | source)
XLA Modules:
  0.0 60.2 jit_solution(10284355501164537857)
XLA Ops:
  0.0 1.2 %shard_map.118 = (bf16[32,128]{1,0:T(8,128)(2,1)S(1)}, bf16[16,128]{1,0:T(8,128)(2,1)S(1)}, bf16[32,512]{1,0:T(8,128)(2,1)S(1)}, bf16[32,512]{1,0:T(8,128)(2,1)S(1)}) custom-call(bf16[1,32,128]{2,1,0:T(8,128)(2,1)} %x_hbm.1, bf16[1,128]{1,0:T(2,128)(2,1)} %bitcast.5, bf16[128,512]{1,0:T(8,128)(2,1)} %wk_hbm.1, bf16[128,512]{1,0:T(8,128)(2,1)} %wv_hbm.1), custom_call_target="tpu_custom_call" | custom-call | flops 8388608 | bytes 1048576 | tf_op jit(solution)/shard_map/pallas_call | solution.py:303
  1.2 0.1 collective-permute-start
  1.3 1.2 %collective-permute-done.taken_ref = bf16[32,512]{1,0:T(8,128)(2,1)S(1)} collective-permute-done((bf16[32,512]{1,0:T(8,128)(2,1)S(1)}, bf16[32,512]{1,0:T(8,128)(2,1)S(1)}, u32[]{:S(2)}, u32[]{:S(2)}) %collective-permute-start) | collective-permute-done | bytes 32800 | tf_op jit(solution)/shard_map/ppermute | solution.py:62
  2.5 0.2 collective-permute-start.2
  2.8 21.3 %all_to_all.20.own_ref = bf16[16,80,128]{2,1,0:T(8,128)(2,1)S(1)} all-to-all(bf16[16,80,128]{2,1,0:T(8,128)(2,1)S(1)} %shard_map.119), channel_id=1, replica_groups={{150,20,154,24,158,28,130,0,134,4,138,8,142,12,146,16},{151,21,155,25,1..., dimensions={0} | all-to-all | bytes 655360 | tf_op jit(solution)/shard_map/all_to_all | solution.py:58
  24.0 0.0 copy-start.1
  24.1 0.0 collective-permute-start.1
  24.1 0.0 copy-start
  24.1 1.5 %shard_map.120 = (bf16[32,128,128]{2,1,0:T(8,128)(2,1)S(1)}, bf16[32,256]{1,0:T(8,128)(2,1)S(1)}, bf16[32,256]{1,0:T(8,128)(2,1)S(1)}, f32[32,128]{1,0:T(8,128)S...) custom-call(s32[4,32]{1,0:T(4,128)} %lengths_hbm, s32[4,32]{1,0:T(4,128)} %offload_hbm.1, s32[4,32]{1,0:T(4,128)} %host_hbm.1, ...), custom_call_target="tpu_custom_call" | custom-call | flops 4194304 | bytes 4194304 | tf_op jit(solution)/shard_map/pallas_call | solution.py:326
  25.5 0.1 collective-permute-done.1.other_ref
  25.7 0.0 collective-permute-done.2.other_ref
  25.7 0.4 copy-done.1
  26.0 0.3 shard_map.121
  26.3 9.7 %all_to_all.21.got_ref = bf16[8,112,128]{2,1,0:T(8,128)(2,1)S(1)} all-to-all(bf16[8,112,128]{2,1,0:T(8,128)(2,1)S(1)} %shard_map.121), channel_id=1, replica_groups={{192,224,128,160,64,96,0,32},{193,225,129,161,65,97,1,33},{66,98,2,34,1..., dimensions={0} | all-to-all | bytes 458752 | tf_op jit(solution)/shard_map/all_to_all | solution.py:58
  36.1 0.0 copy-done
  36.1 0.0 copy-start.2
  36.1 0.9 %shard_map.122 = bf16[16,32,128]{2,1,0:T(8,128)(2,1)S(1)} custom-call(bf16[8,112,128]{2,1,0:T(8,128)(2,1)S(1)} %all_to_all.21.got_ref, bf16[1,1,32,128,512]{4,3,2,1,0:T(8,128)(2,1)S(1)} %copy-done, bf16[32,128,128]{2,1,0:T(8,128)(2,1)S(1)} %get-tuple-element.44.values_ref, bf16[32,256]{1,0:T(8,128)(2,1)S(1)} %get-tuple-element.45.pick_ref, ...), custom_call_target="tpu_custom_call" | custom-call | flops 67108864 | bytes 4194304 | tf_op jit(solution)/shard_map/pallas_call | solution.py:353
  37.0 9.3 %all_to_all.22 = bf16[16,32,128]{2,1,0:T(8,128)(2,1)S(1)} all-to-all(bf16[16,32,128]{2,1,0:T(8,128)(2,1)S(1)} %shard_map.122), channel_id=1, replica_groups={{192,193,224,225,128,129,160,161,64,65,96,97,0,1,32,33},{66,67,98,99,2,..., dimensions={0} | all-to-all | bytes 262144 | tf_op jit(solution)/shard_map/all_to_all | solution.py:58
  46.3 0.0 copy-done.2
  46.3 0.4 shard_map.123
  46.7 12.9 %all_to_all.23.got_ref = bf16[16,32,128]{2,1,0:T(8,128)(2,1)S(1)} all-to-all(bf16[16,32,128]{2,1,0:T(8,128)(2,1)S(1)} %shard_map.123), channel_id=1, replica_groups={{150,20,154,24,158,28,130,0,134,4,138,8,142,12,146,16},{151,21,155,25,1..., dimensions={0} | all-to-all | bytes 262144 | tf_op jit(solution)/shard_map/all_to_all | solution.py:58
  59.6 0.6 %shard_map.124 = bf16[1,32,128]{2,1,0:T(8,128)(2,1)} custom-call(bf16[16,32,128]{2,1,0:T(8,128)(2,1)S(1)} %all_to_all.23.got_ref), custom_call_target="tpu_custom_call" | custom-call | flops 131072 | bytes 262144 | tf_op jit(solution)/shard_map/pallas_call | solution.py:361
  (1 shorter events, 0.0 us)
Async XLA Ops:
  1.2 1.3 %collective-permute-start = (bf16[32,512]{1,0:T(8,128)(2,1)S(1)}, bf16[32,512]{1,0:T(8,128)(2,1)S(1)}, u32[]{:S(2)}, u32[]{:S(2)}) collective-permute-start(bf16[32,512]{1,0:T(8,128)(2,1)S(1)} %get-tuple-element.31), channel_id=1, source_target_pairs={{0,1},{1,0},{2,3},{3,2},{4,5},{5,4},{6,7},{7,6},{8,9},{9,8},{10,11... | collective-permute-start | bytes 98312 | tf_op jit(solution)/shard_map/ppermute | solution.py:62
  2.5 23.1 %collective-permute-start.2 = (bf16[128,8192]{1,0:T(8,128)(2,1)}, bf16[128,8192]{1,0:T(8,128)(2,1)S(1)}, u32[]{:S(2)}, u32[]{:S(2)}) collective-permute-start(bf16[128,8192]{1,0:T(8,128)(2,1)} %own_ref), channel_id=1, source_target_pairs={{0,1},{1,0},{2,3},{3,2},{4,5},{5,4},{6,7},{7,6},{8,9},{9,8},{10,11... | collective-permute-start | bytes 6291464 | tf_op jit(solution)/shard_map/ppermute | solution.py:62
  24.0 2.0 %copy-start.1 = (bf16[8192,128]{1,0:T(8,128)(2,1)S(1)}, bf16[8192,128]{1,0:T(8,128)(2,1)}, u32[]{:S(2)}) copy-start(bf16[8192,128]{1,0:T(8,128)(2,1)} %param.14) | copy-start | bytes 6291460
  24.1 1.6 %collective-permute-start.1 = (bf16[16,80,128]{2,1,0:T(8,128)(2,1)S(1)}, bf16[16,80,128]{2,1,0:T(8,128)(2,1)S(1)}, u32[]{:S(2)}, u32[]{:S(2)}) collective-permute-start(bf16[16,80,128]{2,1,0:T(8,128)(2,1)S(1)} %all_to_all.20.own_ref), channel_id=1, source_target_pairs={{0,1},{1,0},{2,3},{3,2},{4,5},{5,4},{6,7},{7,6},{8,9},{9,8},{10,11... | collective-permute-start | bytes 983048 | tf_op jit(solution)/shard_map/ppermute | solution.py:62
  24.1 12.0 %copy-start = (bf16[1,1,32,128,512]{4,3,2,1,0:T(8,128)(2,1)S(1)}, bf16[1,1,32,128,512]{4,3,2,1,0:T(8,128)(2,1)}, u32[]{:S(2)}) copy-start(bf16[1,1,32,128,512]{4,3,2,1,0:T(8,128)(2,1)} %keys_ref) | copy-start | bytes 12582916
  36.1 10.2 %copy-start.2 = (bf16[128,8192]{1,0:T(8,128)(2,1)S(1)}, bf16[128,8192]{1,0:T(8,128)(2,1)}, u32[]{:S(2)}) copy-start(bf16[128,8192]{1,0:T(8,128)(2,1)} %own_ref) | copy-start | bytes 6291460

commit v9 on v7

--- a/solution.py
+++ b/solution.py
@@ -42,7 +42,7 @@
 FIRST = 2
 HEADS_ALIKE = [(z, y, c) for z in range(ZS) for y in range(YS) for c in range(CORES)]
 TURNS = [(a, (i + FIRST) % INSTS) for a in range(POOLS) for i in range(INSTS)]
-HOSTS = [[device_number(1 ^ a ^ y, i, z, y, c) for a, i in TURNS] for z, y, c in HEADS_ALIKE]
+HOSTS = [[device_number(a ^ y, i, z, y, c) for a, i in TURNS] for z, y, c in HEADS_ALIKE]
 CHIPS = [
     [device_number(1 ^ a ^ y, i, z, y, c) for a, i in TURNS for c in range(CORES)]
     for z in range(ZS)

time: 59.6 us -> 60 us (level)
  no operation moved by 1% of the time
where the time goes in v9:
time: 60 us; the launch traced here: 59.7 us
  blocking collectives  52.7 us (88%)
  Pallas kernels  4.97 us (8%)
  waiting for transfers between devices  1.28 us (2%)
    all_to_all x4, blocking collectives, exchange(): return lax.all_to_all(x, AXES, 0, 0, axis_index_groups=groups, tiled=True)  52.7 us
    pallas_call x1, Pallas kernels, shards(): call(tables_kernel, [shape(REQ, HD, HD), shape(REQ, seats), shape(REQ, se...  1.48 us
    ppermute x3, waiting for transfers between devices, swap_core(): return lax.ppermute(x, 'core', [(0, 1), (1, 0)])  1.28 us
    pallas_call x1, Pallas kernels, shards(): call(features_kernel, [shape(REQ, HD), shape(EXTRA, HD), shape(REQ, HEADS...  1.2 us
  transfers between devices with their start and end apart: 3, of which 2 were waited for; matrix products, arithmetic and copies ran while one was open for 0% of the time, Pallas kernels for 2%

profile of v9, /device:TPU:2, one launch (start us, length us, event | category | flops | bytes accessed | tf_op | source)
XLA Modules:
  0.0 59.7 jit_solution(17742579275004311817)
XLA Ops:
  0.0 1.2 %shard_map.118 = (bf16[32,128]{1,0:T(8,128)(2,1)S(1)}, bf16[8,128]{1,0:T(8,128)(2,1)S(1)}, bf16[32,512]{1,0:T(8,128)(2,1)S(1)}, bf16[32,512]{1,0:T(8,128)(2,1)S(1)}) custom-call(bf16[1,32,128]{2,1,0:T(8,128)(2,1)} %x_hbm.1, bf16[1,128]{1,0:T(2,128)(2,1)} %bitcast.5, bf16[128,512]{1,0:T(8,128)(2,1)} %wk_hbm.1, bf16[128,512]{1,0:T(8,128)(2,1)} %wv_hbm.1), custom_call_target="tpu_custom_call" | custom-call | flops 8388608 | bytes 1048576 | tf_op jit(solution)/shard_map/pallas_call | solution.py:303
  1.2 0.1 collective-permute-start
  1.3 1.2 %collective-permute-done.taken_ref = bf16[32,512]{1,0:T(8,128)(2,1)S(1)} collective-permute-done((bf16[32,512]{1,0:T(8,128)(2,1)S(1)}, bf16[32,512]{1,0:T(8,128)(2,1)S(1)}, u32[]{:S(2)}, u32[]{:S(2)}) %collective-permute-start) | collective-permute-done | bytes 32800 | tf_op jit(solution)/shard_map/ppermute | solution.py:62
  2.5 0.2 collective-permute-start.2
  2.8 20.5 %all_to_all.20.own_ref = bf16[16,72,128]{2,1,0:T(8,128)(2,1)S(1)} all-to-all(bf16[16,72,128]{2,1,0:T(8,128)(2,1)S(1)} %shard_map.119), channel_id=1, replica_groups={{150,20,154,24,158,28,130,0,134,4,138,8,142,12,146,16},{151,21,155,25,1..., dimensions={0} | all-to-all | bytes 589824 | tf_op jit(solution)/shard_map/all_to_all | solution.py:58
  23.3 0.0 copy-start.1
  23.3 0.0 collective-permute-start.1
  23.3 0.0 copy-start
  23.3 1.5 %shard_map.120 = (bf16[32,128,128]{2,1,0:T(8,128)(2,1)S(1)}, bf16[32,256]{1,0:T(8,128)(2,1)S(1)}, bf16[32,256]{1,0:T(8,128)(2,1)S(1)}, f32[32,128]{1,0:T(8,128)S...) custom-call(s32[4,32]{1,0:T(4,128)} %lengths_hbm, s32[4,32]{1,0:T(4,128)} %offload_hbm.1, s32[4,32]{1,0:T(4,128)} %host_hbm.1, ...), custom_call_target="tpu_custom_call" | custom-call | flops 4194304 | bytes 4194304 | tf_op jit(solution)/shard_map/pallas_call | solution.py:326
  24.8 0.1 collective-permute-done.1.other_ref
  24.9 0.0 collective-permute-done.2.other_ref
  24.9 0.4 copy-done.1
  25.3 0.3 shard_map.121
  25.6 9.7 %all_to_all.21.got_ref = bf16[8,104,128]{2,1,0:T(8,128)(2,1)S(1)} all-to-all(bf16[8,104,128]{2,1,0:T(8,128)(2,1)S(1)} %shard_map.121), channel_id=1, replica_groups={{64,96,0,32,192,224,128,160},{65,97,1,33,193,225,129,161},{194,226,130,..., dimensions={0} | all-to-all | bytes 425984 | tf_op jit(solution)/shard_map/all_to_all | solution.py:58
  35.3 0.0 copy-done
  35.3 0.0 copy-start.2
  35.3 0.9 %shard_map.122 = bf16[16,32,128]{2,1,0:T(8,128)(2,1)S(1)} custom-call(bf16[8,104,128]{2,1,0:T(8,128)(2,1)S(1)} %all_to_all.21.got_ref, bf16[1,1,32,128,512]{4,3,2,1,0:T(8,128)(2,1)S(1)} %copy-done, bf16[32,128,128]{2,1,0:T(8,128)(2,1)S(1)} %get-tuple-element.44.values_ref, bf16[32,256]{1,0:T(8,128)(2,1)S(1)} %get-tuple-element.45.pick_ref, ...), custom_call_target="tpu_custom_call" | custom-call | flops 67108864 | bytes 4194304 | tf_op jit(solution)/shard_map/pallas_call | solution.py:353
  36.2 9.5 %all_to_all.22 = bf16[16,32,128]{2,1,0:T(8,128)(2,1)S(1)} all-to-all(bf16[16,32,128]{2,1,0:T(8,128)(2,1)S(1)} %shard_map.122), channel_id=1, replica_groups={{192,193,224,225,128,129,160,161,64,65,96,97,0,1,32,33},{66,67,98,99,2,..., dimensions={0} | all-to-all | bytes 262144 | tf_op jit(solution)/shard_map/all_to_all | solution.py:58
  45.8 0.0 copy-done.2
  45.8 0.4 shard_map.123
  46.2 12.9 %all_to_all.23.got_ref = bf16[16,32,128]{2,1,0:T(8,128)(2,1)S(1)} all-to-all(bf16[16,32,128]{2,1,0:T(8,128)(2,1)S(1)} %shard_map.123), channel_id=1, replica_groups={{150,20,154,24,158,28,130,0,134,4,138,8,142,12,146,16},{151,21,155,25,1..., dimensions={0} | all-to-all | bytes 262144 | tf_op jit(solution)/shard_map/all_to_all | solution.py:58
  59.1 0.6 %shard_map.124 = bf16[1,32,128]{2,1,0:T(8,128)(2,1)} custom-call(bf16[16,32,128]{2,1,0:T(8,128)(2,1)S(1)} %all_to_all.23.got_ref), custom_call_target="tpu_custom_call" | custom-call | flops 131072 | bytes 262144 | tf_op jit(solution)/shard_map/pallas_call | solution.py:361
  (1 shorter events, 0.0 us)
Async XLA Ops:
  1.2 1.3 %collective-permute-start = (bf16[32,512]{1,0:T(8,128)(2,1)S(1)}, bf16[32,512]{1,0:T(8,128)(2,1)S(1)}, u32[]{:S(2)}, u32[]{:S(2)}) collective-permute-start(bf16[32,512]{1,0:T(8,128)(2,1)S(1)} %get-tuple-element.31), channel_id=1, source_target_pairs={{0,1},{1,0},{2,3},{3,2},{4,5},{5,4},{6,7},{7,6},{8,9},{9,8},{10,11... | collective-permute-start | bytes 98312 | tf_op jit(solution)/shard_map/ppermute | solution.py:62
  2.5 22.4 %collective-permute-start.2 = (bf16[128,8192]{1,0:T(8,128)(2,1)}, bf16[128,8192]{1,0:T(8,128)(2,1)S(1)}, u32[]{:S(2)}, u32[]{:S(2)}) collective-permute-start(bf16[128,8192]{1,0:T(8,128)(2,1)} %own_ref), channel_id=1, source_target_pairs={{0,1},{1,0},{2,3},{3,2},{4,5},{5,4},{6,7},{7,6},{8,9},{9,8},{10,11... | collective-permute-start | bytes 6291464 | tf_op jit(solution)/shard_map/ppermute | solution.py:62
  23.3 2.0 %copy-start.1 = (bf16[8192,128]{1,0:T(8,128)(2,1)S(1)}, bf16[8192,128]{1,0:T(8,128)(2,1)}, u32[]{:S(2)}) copy-start(bf16[8192,128]{1,0:T(8,128)(2,1)} %param.14) | copy-start | bytes 6291460
  23.3 1.6 %collective-permute-start.1 = (bf16[16,72,128]{2,1,0:T(8,128)(2,1)S(1)}, bf16[16,72,128]{2,1,0:T(8,128)(2,1)S(1)}, u32[]{:S(2)}, u32[]{:S(2)}) collective-permute-start(bf16[16,72,128]{2,1,0:T(8,128)(2,1)S(1)} %all_to_all.20.own_ref), channel_id=1, source_target_pairs={{0,1},{1,0},{2,3},{3,2},{4,5},{5,4},{6,7},{7,6},{8,9},{9,8},{10,11... | collective-permute-start | bytes 884744 | tf_op jit(solution)/shard_map/ppermute | solution.py:62
  23.3 12.0 %copy-start = (bf16[1,1,32,128,512]{4,3,2,1,0:T(8,128)(2,1)S(1)}, bf16[1,1,32,128,512]{4,3,2,1,0:T(8,128)(2,1)}, u32[]{:S(2)}) copy-start(bf16[1,1,32,128,512]{4,3,2,1,0:T(8,128)(2,1)} %keys_ref) | copy-start | bytes 12582916
  35.3 10.4 %copy-start.2 = (bf16[128,8192]{1,0:T(8,128)(2,1)S(1)}, bf16[128,8192]{1,0:T(8,128)(2,1)}, u32[]{:S(2)}) copy-start(bf16[128,8192]{1,0:T(8,128)(2,1)} %own_ref) | copy-start | bytes 6291460
